TPU v7x, 256 devices: a whole 4x4x8 slice. The times are simulated.
256 devices in a mesh: row: 8 (over y, x_lo), col: 32 (over z, x_hi, core).
Axes of the slice: x: 4 (x_hi: 2, x_lo: 2; x = x_hi * 2 + x_lo), y: 4, z: 8, core: 2. Of those that a mesh axis runs over, the one named last changes fastest.
Arguments:
- q_load: bfloat16 [8, 4096, 4096], P('row', 'col'), may hold values from -160 to 160
- k_load: bfloat16 [8, 4096, 512], P('row', 'col'), may hold values from -160 to 160
- v_load: bfloat16 [8, 4096, 512], P('row', 'col'), may hold values from -6 to 6
- q_bias: float32 [4096], replicated, may hold values from -3 to 3
- k_bias: float32 [512], replicated, may hold values from -3 to 3
- v_bias: float32 [512], replicated, may hold values from -3 to 3
- place: int32 [8, 4096], P('row', 'col'), may hold values from 0 to 4095, as said below
- segment: int32 [8, 4096], P('row', 'col'), may hold values from 0 to 7, never falling along the last dimension, each value on 1 to 1024 neighbouring positions
- d_context: bfloat16 [8, 4096, 4096], P('row', 'col'), may hold values from -6 to 6
Outputs:
- context: bfloat16 [8, 4096, 4096], P('row', 'col')
- grad_q: bfloat16 [8, 4096, 4096], P('row', 'col')
- grad_k: bfloat16 [8, 4096, 512], P('row', 'col')
- grad_v: bfloat16 [8, 4096, 512], P('row', 'col')
- bias_grad_q: float32 [4096], P(('row', 'col'))
- bias_grad_kv: float32 [2, 512], P(None, ('row', 'col'))
Inputs may be any that keep to these rules, and one draw needn't show every extreme that they name: `place`: in each group every position appears once, and each device holds the same number of rows for each device of its col group. `segment`: in each group the numbers never fall, every sample covers 1 to 1024 positions and one covers exactly 1024; every number appears.
All inputs are finite; a program needn't handle non-finite values.
Results may differ from a plain program's by a relative error of at most 0.034.
Values may be sent and summed in bfloat16 or wider, within the bound.
No kernel may reach another device: no remote copies, remote signals or barrier semaphores. Data moves between devices by JAX's collectives and lax.ppermute only.
A program may use at most 64 MiB of HBM per device.

v0:
```python
import jax
import jax.numpy as jnp
from jax import lax
from jax.sharding import PartitionSpec as P

HEADS = 32
KV_HEADS = 4
HEAD_DIM = 128
LEN_CAP = 1024
BLOCK = 512


ROPE_BASE = 1000000.0
MASKED = -1e30


def rotation(segment, width):
    length = segment.shape[0]
    index = jnp.arange(length, dtype=jnp.int32)
    change = jnp.concatenate([jnp.ones((1,), dtype=jnp.bool_), segment[1:] != segment[:-1]])
    begins = lax.cummax(jnp.where(change, index, jnp.zeros_like(index)), axis=0)
    offset = (index - begins).astype(jnp.float32)
    powers = jnp.arange(width // 2, dtype=jnp.float32) * (2.0 / width)
    rates = ROPE_BASE ** (-powers)
    angle = offset[:, None] * rates[None, :]
    return (jnp.cos(angle), jnp.sin(angle))


def rotate(values, cosine, sine, sign):
    half = values.shape[-1] // 2
    front = values[..., :half]
    back = values[..., half:]
    turn_cos = cosine[:, None, :]
    turn_sin = sign * sine[:, None, :]
    return jnp.concatenate(
        [front * turn_cos - back * turn_sin, back * turn_cos + front * turn_sin], axis=-1
    )


def head_pass(query, keys, values, upstream, segment, scale, reach):
    length, width = query.shape
    window = BLOCK + reach
    pad_keys = jnp.concatenate([jnp.zeros((reach, width), keys.dtype), keys])
    pad_values = jnp.concatenate([jnp.zeros((reach, width), values.dtype), values])
    pad_segment = jnp.concatenate([jnp.full((reach,), -1, jnp.int32), segment])

    def visit(carry, block):
        grad_keys, grad_values = carry
        start = block * BLOCK
        q_part = lax.dynamic_slice_in_dim(query, start, BLOCK, 0)
        up_part = lax.dynamic_slice_in_dim(upstream, start, BLOCK, 0)
        seg_rows = lax.dynamic_slice_in_dim(segment, start, BLOCK, 0)
        k_part = lax.dynamic_slice_in_dim(pad_keys, start, window, 0)
        v_part = lax.dynamic_slice_in_dim(pad_values, start, window, 0)
        seg_cols = lax.dynamic_slice_in_dim(pad_segment, start, window, 0)
        row_pos = start + jnp.arange(BLOCK, dtype=jnp.int32)
        col_pos = start - reach + jnp.arange(window, dtype=jnp.int32)
        allowed = (seg_rows[:, None] == seg_cols[None, :]) & (col_pos[None, :] <= row_pos[:, None])
        scores = (
            lax.dot_general(
                q_part, k_part, (((1,), (1,)), ((), ())), preferred_element_type=jnp.float32
            )
            * scale
        )
        scores = jnp.where(allowed, scores, MASKED)
        top = jnp.max(scores, axis=1, keepdims=True)
        weights = jnp.where(allowed, jnp.exp(scores - top), 0.0)
        prob = weights / jnp.sum(weights, axis=1, keepdims=True)
        prob_low = prob.astype(jnp.bfloat16)
        output = jnp.dot(prob_low, v_part, preferred_element_type=jnp.float32).astype(jnp.bfloat16)
        delta = jnp.sum(
            up_part.astype(jnp.float32) * output.astype(jnp.float32), axis=1, keepdims=True
        )
        grad_prob = lax.dot_general(
            up_part, v_part, (((1,), (1,)), ((), ())), preferred_element_type=jnp.float32
        )
        grad_score = (prob * (grad_prob - delta)).astype(jnp.bfloat16)
        grad_query = jnp.dot(grad_score, k_part, preferred_element_type=jnp.float32) * scale
        key_term = (
            lax.dot_general(
                grad_score, q_part, (((0,), (0,)), ((), ())), preferred_element_type=jnp.float32
            )
            * scale
        )
        value_term = lax.dot_general(
            prob_low, up_part, (((0,), (0,)), ((), ())), preferred_element_type=jnp.float32
        )
        grad_keys = lax.dynamic_update_slice_in_dim(
            grad_keys, lax.dynamic_slice_in_dim(grad_keys, start, window, 0) + key_term, start, 0
        )
        grad_values = lax.dynamic_update_slice_in_dim(
            grad_values,
            lax.dynamic_slice_in_dim(grad_values, start, window, 0) + value_term,
            start,
            0,
        )
        return ((grad_keys, grad_values), (output, grad_query))

    init = (
        jnp.zeros((length + reach, width), jnp.float32),
        jnp.zeros((length + reach, width), jnp.float32),
    )
    carry, stacked = lax.scan(visit, init, jnp.arange(length // BLOCK, dtype=jnp.int32))
    outputs = stacked[0].reshape(length, width)
    grad_queries = stacked[1].reshape(length, width)
    return (outputs, grad_queries, carry[0][reach:], carry[1][reach:])


def per_device(q_load, k_load, v_load, q_bias, k_bias, v_bias, place, segment, d_context):
    col_count = lax.axis_size("col")
    tok_count = q_load.shape[1]
    group_size = HEADS // KV_HEADS
    local_heads = HEADS // col_count
    scale = HEAD_DIM ** (-0.5)
    first_head = lax.axis_index("col") * local_heads
    q_width = HEADS * HEAD_DIM
    kv_width = KV_HEADS * HEAD_DIM
    reach = min(LEN_CAP, tok_count * col_count // 2)
    upstream = d_context[0].reshape(tok_count, HEADS, HEAD_DIM)
    bucket = tok_count // col_count
    order = jnp.argsort(place[0] // tok_count, stable=True)
    sent = (
        lax.all_to_all(
            q_load[0][order].reshape(col_count, bucket, q_width),
            "col",
            split_axis=0,
            concat_axis=0,
            tiled=True,
        ),
        lax.all_to_all(
            k_load[0][order].reshape(col_count, bucket, kv_width),
            "col",
            split_axis=0,
            concat_axis=0,
            tiled=True,
        ),
        lax.all_to_all(
            v_load[0][order].reshape(col_count, bucket, kv_width),
            "col",
            split_axis=0,
            concat_axis=0,
            tiled=True,
        ),
        lax.all_to_all(
            place[0][order].reshape(col_count, bucket),
            "col",
            split_axis=0,
            concat_axis=0,
            tiled=True,
        ),
    )
    slots = sent[3].reshape(tok_count) % tok_count
    arrange = jnp.argsort(slots)
    plan_q = sent[0].reshape(tok_count, HEADS, HEAD_DIM)[arrange]
    plan_k = jnp.repeat(sent[1].reshape(tok_count, KV_HEADS, HEAD_DIM)[arrange], group_size, axis=1)
    plan_v = jnp.repeat(sent[2].reshape(tok_count, KV_HEADS, HEAD_DIM)[arrange], group_size, axis=1)
    segment_all = lax.all_gather(segment, "col", axis=1, tiled=True)[0]
    head_q, head_k, head_v, head_up = (
        lax.all_to_all(plan_q, "col", split_axis=1, concat_axis=0, tiled=True),
        lax.all_to_all(plan_k, "col", split_axis=1, concat_axis=0, tiled=True),
        lax.all_to_all(plan_v, "col", split_axis=1, concat_axis=0, tiled=True),
        lax.all_to_all(upstream, "col", split_axis=1, concat_axis=0, tiled=True),
    )
    q_gain = lax.dynamic_slice_in_dim(q_bias.reshape(HEADS, HEAD_DIM), first_head, local_heads, 0)
    k_gain = lax.dynamic_slice_in_dim(
        jnp.repeat(k_bias.reshape(KV_HEADS, HEAD_DIM), group_size, axis=0),
        first_head,
        local_heads,
        0,
    )
    v_gain = lax.dynamic_slice_in_dim(
        jnp.repeat(v_bias.reshape(KV_HEADS, HEAD_DIM), group_size, axis=0),
        first_head,
        local_heads,
        0,
    )
    cosine, sine = rotation(segment_all, HEAD_DIM)
    query = rotate(head_q.astype(jnp.float32) + q_gain, cosine, sine, 1.0).astype(jnp.bfloat16)
    keys = rotate(head_k.astype(jnp.float32) + k_gain, cosine, sine, 1.0).astype(jnp.bfloat16)
    values = (head_v.astype(jnp.float32) + v_gain).astype(jnp.bfloat16)

    def attend(query_head, key_head, value_head, up_head):
        return head_pass(query_head, key_head, value_head, up_head, segment_all, scale, reach)

    outputs, grad_query, grad_key, grad_value = jax.vmap(attend, in_axes=1, out_axes=1)(
        query, keys, values, head_up
    )
    back_q = rotate(grad_query, cosine, sine, -1.0)
    back_k = rotate(grad_key, cosine, sine, -1.0)
    empty = jnp.zeros((HEADS, HEAD_DIM), jnp.float32)
    term_q = lax.dynamic_update_slice_in_dim(empty, jnp.sum(back_q, axis=0), first_head, 0).reshape(
        q_width
    )
    slot_k = lax.dynamic_update_slice_in_dim(empty, jnp.sum(back_k, axis=0), first_head, 0)
    slot_k = slot_k.reshape(KV_HEADS, group_size, HEAD_DIM).sum(axis=1).reshape(kv_width)
    slot_v = lax.dynamic_update_slice_in_dim(empty, jnp.sum(grad_value, axis=0), first_head, 0)
    slot_v = slot_v.reshape(KV_HEADS, group_size, HEAD_DIM).sum(axis=1).reshape(kv_width)
    bias_q, bias_kv = (
        lax.psum_scatter(term_q, ("row", "col"), scatter_dimension=0, tiled=True),
        lax.psum_scatter(
            jnp.stack([slot_k, slot_v]), ("row", "col"), scatter_dimension=1, tiled=True
        ),
    )
    low_q = back_q.astype(jnp.bfloat16)
    low_k = back_k.astype(jnp.bfloat16)
    low_v = grad_value.astype(jnp.bfloat16)
    context, plan_dq, plan_dk, plan_dv = (
        lax.all_to_all(outputs, "col", split_axis=0, concat_axis=1, tiled=True),
        lax.all_to_all(low_q, "col", split_axis=0, concat_axis=1, tiled=True),
        lax.all_to_all(low_k, "col", split_axis=0, concat_axis=1, tiled=True),
        lax.all_to_all(low_v, "col", split_axis=0, concat_axis=1, tiled=True),
    )
    fold_k = (
        plan_dk.astype(jnp.float32).reshape(tok_count, KV_HEADS, group_size, HEAD_DIM).sum(axis=2)
    )
    fold_k = fold_k.astype(jnp.bfloat16).reshape(tok_count, kv_width)
    fold_v = (
        plan_dv.astype(jnp.float32).reshape(tok_count, KV_HEADS, group_size, HEAD_DIM).sum(axis=2)
    )
    fold_v = fold_v.astype(jnp.bfloat16).reshape(tok_count, kv_width)
    returned = (
        lax.all_to_all(
            plan_dq.reshape(tok_count, q_width)[slots].reshape(col_count, bucket, q_width),
            "col",
            split_axis=0,
            concat_axis=0,
            tiled=True,
        ),
        lax.all_to_all(
            fold_k[slots].reshape(col_count, bucket, kv_width),
            "col",
            split_axis=0,
            concat_axis=0,
            tiled=True,
        ),
        lax.all_to_all(
            fold_v[slots].reshape(col_count, bucket, kv_width),
            "col",
            split_axis=0,
            concat_axis=0,
            tiled=True,
        ),
    )
    undo = jnp.argsort(order)
    out_q = returned[0].reshape(tok_count, q_width)[undo]
    out_k = returned[1].reshape(tok_count, kv_width)[undo]
    out_v = returned[2].reshape(tok_count, kv_width)[undo]
    return (
        context.reshape(1, tok_count, q_width),
        out_q[None],
        out_k[None],
        out_v[None],
        bias_q,
        bias_kv,
    )


def solution(mesh):
    return jax.shard_map(
        per_device,
        mesh=mesh,
        in_specs=(
            P("row", "col", None),
            P("row", "col", None),
            P("row", "col", None),
            P(),
            P(),
            P(),
            P("row", "col"),
            P("row", "col"),
            P("row", "col", None),
        ),
        out_specs=(
            P("row", "col", None),
            P("row", "col", None),
            P("row", "col", None),
            P("row", "col", None),
            P(("row", "col")),
            P(None, ("row", "col")),
        ),
        check_vma=False,
    )
```

profile of v0, /device:TPU:16, one launch (start us, length us, event | category | flops | bytes accessed | tf_op | source)
XLA Modules:
  0.0 817.6 jit_solution(13587331595590342310)
XLA Ops:
  6.3 11.3 %all-to-all-start.1 = ((s32[32,1,4]{2,1,0:T(1,128)}), s32[32,1,4]{2,1,0:T(1,128)S(1)}, u32[]{:S(2)}, u32[]{:S(2)}) async-start(s32[32,1,4]{2,1,0:T(1,128)} %bitcast.21), calls=%async_computation.1 | async-start | bytes 32768 | tf_op jit(solution)/shard_map/all_to_all | solution.py:144
  20.1 7.2 all-to-all-done.1
  32.7 9.1 %all-to-all-done.3 = bf16[32,4,512]{2,1,0:T(4,128)(2,1)S(1)} async-done(((bf16[32,4,512]{2,1,0:T(4,128)(2,1)}), bf16[32,4,512]{2,1,0:T(4,128)(2,1)S(1)}, u32[]{:S(2)}, u32[]{:S(2)}) %all-to-all-start.3) | async-done | bytes 131104 | tf_op jit(solution)/shard_map/all_to_all | solution.py:130
  48.1 8.3 %all-to-all-done.6 = bf16[32,4,512]{2,1,0:T(4,128)(2,1)S(1)} async-done(((bf16[32,4,512]{2,1,0:T(4,128)(2,1)}), bf16[32,4,512]{2,1,0:T(4,128)(2,1)S(1)}, u32[]{:S(2)}, u32[]{:S(2)}) %all-to-all-start.6) | async-done | bytes 131104 | tf_op jit(solution)/shard_map/all_to_all | solution.py:137
  56.4 3.9 all-to-all-start
  61.7 27.9 %all-to-all-done = bf16[32,4,4096]{2,1,0:T(4,128)(2,1)S(1)} async-done(((bf16[32,4,4096]{2,1,0:T(4,128)(2,1)}), bf16[32,4,4096]{2,1,0:T(4,128)(2,1)S(1)}, u32[]{:S(2)}, u32[]{:S(2)}) %all-to-all-start) | async-done | bytes 1048608 | tf_op jit(solution)/shard_map/all_to_all | solution.py:123
  89.6 4.7 all-to-all-start.5
  99.0 24.4 %all-to-all-done.5 = bf16[128,32,128]{0,2,1:T(8,128)(2,1)S(1)} async-done(((bf16[128,32,128]{0,2,1:T(8,128)(2,1)}), bf16[128,32,128]{0,2,1:T(8,128)(2,1)S(1)}, u32[]{:S(2)}, u32[]{:S(2)}) %all-to-all-start.5) | async-done | bytes 1048608 | tf_op jit(solution)/shard_map/all_to_all | solution.py:162
  124.7 4.8 all-to-all-start.7
  130.4 28.2 %all-to-all-done.7 = bf16[128,32,128]{2,0,1:T(8,128)(2,1)S(1)} async-done(((bf16[128,32,128]{2,0,1:T(8,128)(2,1)}), bf16[128,32,128]{2,0,1:T(8,128)(2,1)S(1)}, u32[]{:S(2)}, u32[]{:S(2)}) %all-to-all-start.7) | async-done | bytes 1048608 | tf_op jit(solution)/shard_map/all_to_all | solution.py:161
  159.9 4.9 all-to-all-start.4
  164.8 56.5 %all_gather.3 = s32[1,4096]{1,0:T(1,128)S(1)} all-gather(s32[1,128]{1,0:T(1,128)S(1)} %copy-done.31), channel_id=1, replica_groups=mesh['row'=8,'col'=32] {'col'}, dimensions={1}, use_global_device_ids=true | all-gather | bytes 16896 | tf_op jit(solution)/shard_map/all_gather | solution.py:157
  227.9 9.0 %all-to-all-start.2 = ((bf16[128,32,128]{2,0,1:T(8,128)(2,1)}), bf16[128,32,128]{2,0,1:T(8,128)(2,1)S(1)}, u32[]{:S(2)}, u32[]{:S(2)}) async-start(bf16[128,32,128]{2,0,1:T(8,128)(2,1)} %copy.47), calls=%async_computation.2 | async-start | bytes 2097152 | tf_op jit(solution)/shard_map/all_to_all | solution.py:159
  239.9 26.1 %all-to-all-done.2 = bf16[128,32,128]{2,0,1:T(8,128)(2,1)S(1)} async-done(((bf16[128,32,128]{2,0,1:T(8,128)(2,1)}), bf16[128,32,128]{2,0,1:T(8,128)(2,1)S(1)}, u32[]{:S(2)}, u32[]{:S(2)}) %all-to-all-start.2) | async-done | bytes 1048608 | tf_op jit(solution)/shard_map/all_to_all | solution.py:159
  266.5 9.3 %fusion.70 = (bf16[1,4096,64]{2,1,0:T(8,128)(2,1)S(1)}, bf16[1,4096,64]{2,1,0:T(8,128)(2,1)S(1)}, bf16[1,4096,64]{2,1,0:T(8,128)(2,1)S(1)}, bf16[1,4096,64]{2,1,0:T(8,128)(2,1)S(1)}) fusion(f32[4096,1,128]{2,0,1:T(8,128)S(1)} %bitcast_add_fusion.1, f32[64]{0:T(128)S(1)} %negate_power_fusion, f32[4096]{0:T(1024)S(1)} %fusion.77, ...), kind=kLoop, calls=%fused_computation.116 | loop fusion | flops 4456448 | bytes 6308096 | tf_op jit(solution)/shard_map/concatenate | solution.py:35
  282.4 242.9 %while.26 = (s32[]{:T(128)}, f32[1,5120,128]{2,1,0:T(8,128)}, f32[1,5120,128]{2,1,0:T(8,128)}, bf16[8,1,512,128]{3,2,0,1:T(8,128)(2,1)}, f32[8,1,512,128]{3,2,1,...) while((s32[]{:T(128)}, f32[1,5120,128]{2,1,0:T(8,128)}, ...), condition=%wide.region_9.10_spmd, body=%wide.region_4.9_spmd.sunk | while | flops 1227424256 | bytes 49144176 | solution.py:103
  527.6 9.8 %fusion.56 = (f32[4096,1,64]{2,0,1:T(8,128)S(1)}, f32[4096,1,64]{2,0,1:T(8,128)S(1)}, f32[4096,1,64]{2,0,1:T(8,128)S(1)}, f32[4096,1,64]{2,0,1:T(8,128)}) fusion(f32[4096,1,128]{2,0,1:T(8,128)S(1)} %slice_bitcast_fusion, f32[64]{0:T(128)S(1)} %copy-done.28, f32[4096]{0:T(1024)S(1)} %copy-done.24, f32[4096,1,128]{2,0,1:T(8,128)S(1)} %bitcast.245), kind=kLoop, calls=%fused_computation.89 | loop fusion | flops 3670016 | bytes 8405248 | tf_op jit(solution)/shard_map/sub | solution.py:36
  544.8 5.0 all-to-all-start.11
  554.3 24.5 %all-to-all-done.11 = bf16[32,2,8192]{2,1,0:T(2,128)(2,1)} async-done(((bf16[32,2,8192]{2,1,0:T(2,128)(2,1)}), bf16[32,2,8192]{2,1,0:T(2,128)(2,1)}, u32[]{:S(2)}, u32[]{:S(2)}) %all-to-all-start.11) | async-done | bytes 1048608 | tf_op jit(solution)/shard_map/all_to_all | solution.py:210
  578.8 4.8 all-to-all-start.9
  587.9 24.8 %all-to-all-done.9 = bf16[32,2,8192]{2,1,0:T(2,128)(2,1)S(1)} async-done(((bf16[32,2,8192]{2,1,0:T(2,128)(2,1)}), bf16[32,2,8192]{2,1,0:T(2,128)(2,1)S(1)}, u32[]{:S(2)}, u32[]{:S(2)}) %all-to-all-start.9) | async-done | bytes 1048608 | tf_op jit(solution)/shard_map/all_to_all | solution.py:209
  612.7 4.8 all-to-all-start.13
  621.4 25.3 %all-to-all-done.13 = bf16[32,2,8192]{2,1,0:T(2,128)(2,1)S(1)} async-done(((bf16[32,2,8192]{2,1,0:T(2,128)(2,1)}), bf16[32,2,8192]{2,1,0:T(2,128)(2,1)S(1)}, u32[]{:S(2)}, u32[]{:S(2)}) %all-to-all-start.13) | async-done | bytes 1048608 | tf_op jit(solution)/shard_map/all_to_all | solution.py:211
  646.7 4.8 all-to-all-start.8
  651.7 4.3 reshape.1141
  660.0 20.6 %all-to-all-done.8 = bf16[32,2,8192]{2,1,0:T(2,128)(2,1)S(1)} async-done(((bf16[32,2,8192]{2,1,0:T(2,128)(2,1)}), bf16[32,2,8192]{2,1,0:T(2,128)(2,1)S(1)}, u32[]{:S(2)}, u32[]{:S(2)}) %all-to-all-start.8) | async-done | bytes 1048608 | tf_op jit(solution)/shard_map/all_to_all | solution.py:208
  680.6 4.8 all-to-all-start.12
  685.4 4.3 reshape.1143
  696.2 7.5 all-to-all-start.14
  708.5 5.9 all-to-all-done.14
  714.5 4.7 all-to-all-start.10
  728.6 77.7 %all-reduce.5 = (f32[4096]{0:T(1024)S(1)}, f32[2,512]{1,0:T(2,128)S(1)}) all-reduce(f32[4096]{0:T(1024)S(1)} %bitcast.275, f32[2,512]{1,0:T(2,128)S(1)} %pad_maximum_fusion.3), channel_id=2, replica_groups=mesh['row'=8,'col'=32] {'row','col'}, use_global_device_ids=true, to_apply=%region_14.15.clone | all-reduce | flops 5120 | bytes 40960
  (472 shorter events, 340.7 us)
Async XLA Ops:
  0.6 45.1 %copy-start = (bf16[1,128,4096]{2,1,0:T(8,128)(2,1)S(1)}, bf16[1,128,4096]{2,1,0:T(8,128)(2,1)}, u32[]{:S(2)}) copy-start(bf16[1,128,4096]{2,1,0:T(8,128)(2,1)} %param.15) | copy-start | bytes 3145732
  0.6 30.5 %copy-start.7 = (bf16[1,128,512]{2,1,0:T(8,128)(2,1)S(1)}, bf16[1,128,512]{2,1,0:T(8,128)(2,1)}, u32[]{:S(2)}) copy-start(bf16[1,128,512]{2,1,0:T(8,128)(2,1)} %param.17) | copy-start | bytes 393220
  4.0 13.6 %copy-start.34 = (s32[128]{0:T(128)}, s32[128]{0:T(128)S(1)}, u32[]{:S(2)}) copy-start(s32[128]{0:T(128)S(1)} %get-tuple-element.185) | copy-start | bytes 1540
  6.3 21.0 %all-to-all-start.1 = ((s32[32,1,4]{2,1,0:T(1,128)}), s32[32,1,4]{2,1,0:T(1,128)S(1)}, u32[]{:S(2)}, u32[]{:S(2)}) async-start(s32[32,1,4]{2,1,0:T(1,128)} %bitcast.21), calls=%async_computation.1 | async-start | bytes 32768 | tf_op jit(solution)/shard_map/all_to_all | solution.py:144
  27.3 67.5 %copy-start.21 = (s32[32,1,4]{2,1,0:T(1,128)}, s32[32,1,4]{2,1,0:T(1,128)S(1)}, u32[]{:S(2)}) copy-start(s32[32,1,4]{2,1,0:T(1,128)S(1)} %all-to-all-done.1) | copy-start | bytes 1540
  27.3 14.6 %all-to-all-start.3 = ((bf16[32,4,512]{2,1,0:T(4,128)(2,1)}), bf16[32,4,512]{2,1,0:T(4,128)(2,1)S(1)}, u32[]{:S(2)}, u32[]{:S(2)}) async-start(bf16[32,4,512]{2,1,0:T(4,128)(2,1)} %reshape.828), calls=%async_computation.3 | async-start | bytes 262144 | tf_op jit(solution)/shard_map/all_to_all | solution.py:130
  41.8 14.6 %all-to-all-start.6 = ((bf16[32,4,512]{2,1,0:T(4,128)(2,1)}), bf16[32,4,512]{2,1,0:T(4,128)(2,1)S(1)}, u32[]{:S(2)}, u32[]{:S(2)}) async-start(bf16[32,4,512]{2,1,0:T(4,128)(2,1)} %reshape.833), calls=%async_computation.6 | async-start | bytes 262144 | tf_op jit(solution)/shard_map/all_to_all | solution.py:137
  46.9 13.4 %copy-start.16 = (bf16[1,128,4096]{2,1,0:T(8,128)(2,1)S(1)}, bf16[1,128,4096]{2,1,0:T(8,128)(2,1)}, u32[]{:S(2)}) copy-start(bf16[1,128,4096]{2,1,0:T(8,128)(2,1)} %param.23) | copy-start | bytes 3145732
  56.4 33.2 %all-to-all-start = ((bf16[32,4,4096]{2,1,0:T(4,128)(2,1)}), bf16[32,4,4096]{2,1,0:T(4,128)(2,1)S(1)}, u32[]{:S(2)}, u32[]{:S(2)}) async-start(bf16[32,4,4096]{2,1,0:T(4,128)(2,1)} %reshape.823), calls=%async_computation | async-start | bytes 2097152 | tf_op jit(solution)/shard_map/all_to_all | solution.py:123
  89.6 33.8 %all-to-all-start.5 = ((bf16[128,32,128]{0,2,1:T(8,128)(2,1)}), bf16[128,32,128]{0,2,1:T(8,128)(2,1)S(1)}, u32[]{:S(2)}, u32[]{:S(2)}) async-start(bf16[128,32,128]{0,2,1:T(8,128)(2,1)} %bitcast.41), calls=%async_computation.5 | async-start | bytes 2097152 | tf_op jit(solution)/shard_map/all_to_all | solution.py:162
  123.4 36.5 %copy-start.14 = (bf16[128,32,128]{0,2,1:T(8,128)(2,1)}, bf16[128,32,128]{0,2,1:T(8,128)(2,1)S(1)}, u32[]{:S(2)}) copy-start(bf16[128,32,128]{0,2,1:T(8,128)(2,1)S(1)} %all-to-all-done.5) | copy-start | bytes 3145732
  124.7 33.9 %all-to-all-start.7 = ((bf16[128,32,128]{2,0,1:T(8,128)(2,1)}), bf16[128,32,128]{2,0,1:T(8,128)(2,1)S(1)}, u32[]{:S(2)}, u32[]{:S(2)}) async-start(bf16[128,32,128]{2,0,1:T(8,128)(2,1)} %bitcast.251), calls=%async_computation.7 | async-start | bytes 2097152 | tf_op jit(solution)/shard_map/all_to_all | solution.py:161
  129.5 35.3 %copy-start.31 = (s32[1,128]{1,0:T(1,128)S(1)}, s32[1,128]{1,0:T(1,128)}, u32[]{:S(2)}) copy-start(s32[1,128]{1,0:T(1,128)} %param.22) | copy-start | bytes 1540
  129.5 92.5 %copy-start.29 = (f32[512]{0:T(512)S(1)}, f32[512]{0:T(512)}, u32[]{:S(2)}) copy-start(f32[512]{0:T(512)} %param.20) | copy-start | bytes 6148
  129.6 92.4 %copy-start.30 = (f32[512]{0:T(512)S(1)}, f32[512]{0:T(512)}, u32[]{:S(2)}) copy-start(f32[512]{0:T(512)} %param.19) | copy-start | bytes 6148
  159.9 68.0 %all-to-all-start.4 = ((bf16[128,32,128]{2,0,1:T(8,128)(2,1)}), bf16[128,32,128]{2,0,1:T(8,128)(2,1)}, u32[]{:S(2)}, u32[]{:S(2)}) async-start(bf16[128,32,128]{2,0,1:T(8,128)(2,1)} %bitcast.250), calls=%async_computation.4 | async-start | bytes 2097152 | tf_op jit(solution)/shard_map/all_to_all | solution.py:160
  222.0 44.4 %copy-start.27 = (f32[64]{0:T(128)}, f32[64]{0:T(128)S(1)}, u32[]{:S(2)}) copy-start(f32[64]{0:T(128)S(1)} %negate_power_fusion) | copy-start | bytes 772
  223.0 43.5 %copy-start.23 = (f32[4096]{0:T(1024)}, f32[4096]{0:T(1024)S(1)}, u32[]{:S(2)}) copy-start(f32[4096]{0:T(1024)S(1)} %fusion.77) | copy-start | bytes 49156
  227.9 38.1 %all-to-all-start.2 = ((bf16[128,32,128]{2,0,1:T(8,128)(2,1)}), bf16[128,32,128]{2,0,1:T(8,128)(2,1)S(1)}, u32[]{:S(2)}, u32[]{:S(2)}) async-start(bf16[128,32,128]{2,0,1:T(8,128)(2,1)} %copy.47), calls=%async_computation.2 | async-start | bytes 2097152 | tf_op jit(solution)/shard_map/all_to_all | solution.py:159
  537.4 12.4 %copy-start.4 = (f32[4096,1,64]{2,0,1:T(8,128)}, f32[4096,1,64]{2,0,1:T(8,128)S(1)}, u32[]{:S(2)}) copy-start(f32[4096,1,64]{2,0,1:T(8,128)S(1)} %get-tuple-element.328) | copy-start | bytes 3145732
  544.8 34.0 %all-to-all-start.11 = ((bf16[32,2,8192]{2,1,0:T(2,128)(2,1)}), bf16[32,2,8192]{2,1,0:T(2,128)(2,1)}, u32[]{:S(2)}, u32[]{:S(2)}) async-start(bf16[32,2,8192]{2,1,0:T(2,128)(2,1)} %reshape.1140), calls=%async_computation.11 | async-start | bytes 2097152 | tf_op jit(solution)/shard_map/all_to_all | solution.py:210
  578.8 33.9 %all-to-all-start.9 = ((bf16[32,2,8192]{2,1,0:T(2,128)(2,1)}), bf16[32,2,8192]{2,1,0:T(2,128)(2,1)S(1)}, u32[]{:S(2)}, u32[]{:S(2)}) async-start(bf16[32,2,8192]{2,1,0:T(2,128)(2,1)} %reshape.1138), calls=%async_computation.9 | async-start | bytes 2097152 | tf_op jit(solution)/shard_map/all_to_all | solution.py:209
  612.7 33.9 %all-to-all-start.13 = ((bf16[32,2,8192]{2,1,0:T(2,128)(2,1)}), bf16[32,2,8192]{2,1,0:T(2,128)(2,1)S(1)}, u32[]{:S(2)}, u32[]{:S(2)}) async-start(bf16[32,2,8192]{2,1,0:T(2,128)(2,1)} %reshape.1142), calls=%async_computation.13 | async-start | bytes 2097152 | tf_op jit(solution)/shard_map/all_to_all | solution.py:211
  620.2 31.3 %copy-start.22 = (s32[32,1,4]{2,1,0:T(1,128)S(1)}, s32[32,1,4]{2,1,0:T(1,128)}, u32[]{:S(2)}) copy-start(s32[32,1,4]{2,1,0:T(1,128)} %copy-done.21) | copy-start | bytes 1540
  646.7 33.9 %all-to-all-start.8 = ((bf16[32,2,8192]{2,1,0:T(2,128)(2,1)}), bf16[32,2,8192]{2,1,0:T(2,128)(2,1)S(1)}, u32[]{:S(2)}, u32[]{:S(2)}) async-start(bf16[32,2,8192]{2,1,0:T(2,128)(2,1)} %reshape.1136), calls=%async_computation.8 | async-start | bytes 2097152 | tf_op jit(solution)/shard_map/all_to_all | solution.py:208
  680.6 10.3 %copy-start.9 = (bf16[32,2,8192]{2,1,0:T(2,128)(2,1)}, bf16[32,2,8192]{2,1,0:T(2,128)(2,1)S(1)}, u32[]{:S(2)}) copy-start(bf16[32,2,8192]{2,1,0:T(2,128)(2,1)S(1)} %all-to-all-done.8) | copy-start | bytes 3145732
  680.6 15.6 %all-to-all-start.12 = ((bf16[32,4,512]{2,1,0:T(4,128)(2,1)}), bf16[32,4,512]{2,1,0:T(4,128)(2,1)S(1)}, u32[]{:S(2)}, u32[]{:S(2)}) async-start(bf16[32,4,512]{2,1,0:T(4,128)(2,1)} %reshape.843), calls=%async_computation.12 | async-start | bytes 262144 | tf_op jit(solution)/shard_map/all_to_all | solution.py:229
  690.9 12.8 %copy-start.12 = (bf16[32,2,8192]{2,1,0:T(2,128)(2,1)S(1)}, bf16[32,2,8192]{2,1,0:T(2,128)(2,1)}, u32[]{:S(2)}) copy-start(bf16[32,2,8192]{2,1,0:T(2,128)(2,1)} %copy-done.11) | copy-start | bytes 3145732
  696.2 18.3 %all-to-all-start.14 = ((bf16[32,4,512]{2,1,0:T(4,128)(2,1)}), bf16[32,4,512]{2,1,0:T(4,128)(2,1)S(1)}, u32[]{:S(2)}, u32[]{:S(2)}) async-start(bf16[32,4,512]{2,1,0:T(4,128)(2,1)} %reshape.845), calls=%async_computation.14 | async-start | bytes 262144 | tf_op jit(solution)/shard_map/all_to_all | solution.py:236
  707.3 11.9 %copy-start.35 = (s32[128]{0:T(128)S(1)}, s32[128]{0:T(128)}, u32[]{:S(2)}) copy-start(s32[128]{0:T(128)} %copy-done.34) | copy-start | bytes 1540
  714.5 99.4 %all-to-all-start.10 = ((bf16[32,4,4096]{2,1,0:T(4,128)(2,1)}), bf16[32,4,4096]{2,1,0:T(4,128)(2,1)}, u32[]{:S(2)}, u32[]{:S(2)}) async-start(bf16[32,4,4096]{2,1,0:T(4,128)(2,1)} %reshape.841), calls=%async_computation.10 | async-start | bytes 2097152 | tf_op jit(solution)/shard_map/all_to_all | solution.py:222
  725.6 82.0 %copy-start.10 = (bf16[32,2,8192]{2,1,0:T(2,128)(2,1)S(1)}, bf16[32,2,8192]{2,1,0:T(2,128)(2,1)}, u32[]{:S(2)}) copy-start(bf16[32,2,8192]{2,1,0:T(2,128)(2,1)} %copy-done.9) | copy-start | bytes 3145732
  (68 other events, 242.3 us)
where the time goes:
time: 832 us; the launch traced here: 818 us
  waiting for transfers between devices  235 us (28%)
  local copies, waits for them, and re-layouts  146 us (18%)
  blocking collectives  134 us (16%)
  matrix products  134 us (16%)
  starting transfers between devices  82.9 us (10%)
  other arithmetic  78 us (9%)
    unnamed x1, blocking collectives  77.7 us
    all_gather x1, blocking collectives, per_device(): segment_all = lax.all_gather(segment, 'col', axis=1, tiled=True)[0]  56.5 us
    dot_general x8, matrix products, visit(): lax.dot_general(grad_score, q_part, (((0,), (0,)), ((), ())), preferred_e...  29 us
    scatter x8, local copies, waits for them, and re-layouts, visit(): lax.dynamic_update_slice_in_dim(grad_keys, lax.dynamic_slice_in_dim(grad_...  28.9 us
    scatter x8, local copies, waits for them, and re-layouts, visit(): lax.dynamic_update_slice_in_dim(grad_values, lax.dynamic_slice_in_dim(gra...  28.8 us
    dot_general x8, matrix products, visit(): lax.dot_general(prob_low, up_part, (((0,), (0,)), ((), ())), preferred_el...  28.4 us
    all_to_all x1, waiting for transfers between devices, per_device(): lax.all_to_all(plan_v, 'col', split_axis=1, concat_axis=0, tiled=True)  28.2 us
    all_to_all x1, waiting for transfers between devices, per_device(): lax.all_to_all(q_load[0][order].reshape(col_count, bucket, q_width), 'col...  27.9 us
  transfers between devices with their start and end apart: 15, of which 13 were waited for; matrix products, arithmetic and copies ran while one was open for 9% of the time, Pallas kernels for 0%

commit v1 on v0

v1 whole, which is shorter than its diff:
```python
import functools

import jax
import jax.numpy as jnp
from jax import lax
from jax.experimental import pallas as pl
from jax.experimental.pallas import tpu as pltpu
from jax.sharding import PartitionSpec as P

HEADS = 32
KV_HEADS = 4
GROUP = 8
HEAD_DIM = 128
SEGS = 8
TOK = 128
SLAB = 512
QBLK = 256
KTILE = 256
WINDOW = 1280
Q_WIDTH = HEADS * HEAD_DIM
KV_WIDTH = KV_HEADS * HEAD_DIM
PART = GROUP * HEAD_DIM
SENT = PART + 6 * HEAD_DIM + 128
BACK = PART + 6 * HEAD_DIM
MIB = 1024 * 1024

ROPE_BASE = 1000000.0
MASKED = -1e30
LOG2E = 1.4426950408889634
F32 = jnp.float32
BF16 = jnp.bfloat16

NN = (((1,), (0,)), ((), ()))
NT = (((1,), (1,)), ((), ()))


def dot(a, b, dims=NN):
    return lax.dot_general(a, b, dims, preferred_element_type=F32)


def iota(shape, axis):
    return lax.broadcasted_iota(jnp.int32, shape, axis)


def row_to_column(row, size):
    same = iota((size, size), 0) == iota((size, size), 1)
    return jnp.sum(jnp.where(same, row, 0.0), axis=1, keepdims=True)


def pack_kernel(q_ref, k_ref, v_ref, place_ref, seg_ref, out_ref):
    place_row = place_ref[...].astype(F32)
    place_col = row_to_column(place_row, TOK)
    rank = jnp.sum(jnp.where(place_col < place_row, 1.0, 0.0), axis=0, keepdims=True)
    pick = iota((TOK, TOK), 0).astype(F32) == rank
    pick_low = jnp.where(pick, 1.0, 0.0).astype(BF16)
    ranked = jnp.sum(jnp.where(pick, place_row, 0.0), axis=1, keepdims=True)
    inside = ranked - ((iota((TOK, 1), 0) // 16) * SLAB).astype(F32)
    high = jnp.floor(inside * (1.0 / 128.0))
    low = inside - 128.0 * high
    seg_col = row_to_column(seg_ref[...].astype(F32), TOK)
    lane = iota((TOK, 128), 1)
    below = jnp.sum(
        jnp.where(seg_col < (lane - 8).astype(F32), 1.0, 0.0), axis=0, keepdims=True
    )
    lane16 = iota((16, 128), 1)
    counts = jnp.where(iota((16, 128), 0) == 0, below, 0.0)
    for j in range(KV_HEADS):
        part = dot(pick_low, q_ref[:, PART * j : PART * (j + 1)]).astype(BF16)
        for z in range(8):
            out_ref[4 * z + j, :, 0:PART] = part[16 * z : 16 * z + 16]
    keys = dot(pick_low, k_ref[...]).astype(BF16)
    vals = dot(pick_low, v_ref[...]).astype(BF16)
    for z in range(8):
        meta = counts
        for t in range(3):
            s = (z - 2 + t) % 8
            rows = slice(16 * s, 16 * s + 16)
            meta = jnp.where(lane16 == 2 * t, high[rows], meta)
            meta = jnp.where(lane16 == 2 * t + 1, low[rows], meta)
            base = PART + 256 * t
            for j in range(KV_HEADS):
                head = slice(HEAD_DIM * j, HEAD_DIM * (j + 1))
                out_ref[4 * z + j, :, base : base + 128] = keys[rows, head]
                out_ref[4 * z + j, :, base + 128 : base + 256] = vals[rows, head]
        for j in range(KV_HEADS):
            out_ref[4 * z + j, :, BACK:SENT] = meta.astype(BF16)


def turn(values, cosine, sine):
    return values * cosine + pltpu.roll(values, HEAD_DIM // 2, 1) * sine


def unturn(values, cosine, sine):
    return values * cosine - pltpu.roll(values, HEAD_DIM // 2, 1) * sine


def attend_kernel(
    col_ref, recv_ref, up0, up1, up2, up3, qb_ref, kb_ref, vb_ref, cos_ref, sin_ref,
    ctx0, ctx1, ctx2, ctx3, back_ref, bias_ref,
    up_s, q_s, k_s, v_s, kt_s, vt_s, cos_s, sin_s, mask_s, s_s, p_s, dk_s, dv_s, ctx_s, dq_s,
):
    col = col_ref[0]
    z = col // 4
    j = col % 4
    first = SLAB * (z - 2)
    scale = HEAD_DIM ** (-0.5)

    for s, ref in enumerate((up0, up1, up2, up3)):
        up_s[pl.ds(pl.multiple_of(TOK * (j ^ s), TOK), TOK), :] = ref[...]

    meta = recv_ref[:, BACK:SENT].astype(F32)
    meta_rows = jnp.transpose(meta)
    starts = [jnp.sum(meta[:, 8 + v : 9 + v]).astype(jnp.int32) for v in range(SEGS)]

    for b in range(12):
        at = first + TOK * b
        rows = slice(TOK * b, TOK * (b + 1))
        for v in range(SEGS):
            begin = starts[v]
            end = starts[v + 1] if v + 1 < SEGS else jnp.int32(8 * SLAB)
            if v == 0:
                cos_s[rows, :] = jnp.zeros((TOK, HEAD_DIM), F32)
                sin_s[rows, :] = jnp.zeros((TOK, HEAD_DIM), F32)

            @pl.when((begin < at + TOK) & (end > at))
            def _():
                src = pl.ds(at - begin + TOK, TOK)
                inside = at + iota((TOK, HEAD_DIM), 0) >= begin
                cos_s[rows, :] = jnp.where(inside, cos_ref[src, :], cos_s[rows, :])
                sin_s[rows, :] = jnp.where(inside, sin_ref[src, :], sin_s[rows, :])

    k_bias = kb_ref[:, pl.ds(pl.multiple_of(HEAD_DIM * j, HEAD_DIM), HEAD_DIM)]
    v_bias = vb_ref[:, pl.ds(pl.multiple_of(HEAD_DIM * j, HEAD_DIM), HEAD_DIM)]
    q_bias = qb_ref[:, pl.ds(pl.multiple_of(PART * j, PART), PART)]
    spot = iota((SLAB, SLAB), 0).astype(F32)
    for t in range(3):
        pos = meta_rows[2 * t : 2 * t + 1] * 128.0 + meta_rows[2 * t + 1 : 2 * t + 2]
        pick = jnp.where(spot == pos, 1.0, 0.0).astype(BF16)
        rows = slice(SLAB * t, SLAB * (t + 1))
        base = PART + 256 * t
        both = dot(pick, recv_ref[:, base : base + 256])
        keys = turn(both[:, :128] + k_bias, cos_s[rows, :], sin_s[rows, :])
        vals = both[:, 128:] + v_bias
        k_s[rows, :] = keys.astype(BF16)
        v_s[rows, :] = vals.astype(BF16)
        kt_s[:, rows] = jnp.transpose(keys).astype(BF16)
        vt_s[:, rows] = jnp.transpose(vals).astype(BF16)
        if t == 2:
            for pair in range(4):
                lanes = slice(256 * pair, 256 * (pair + 1))
                both = dot(pick, recv_ref[:, lanes]) + q_bias[:, lanes]
                for u in range(2):
                    one = both[:, 128 * u : 128 * (u + 1)]
                    q_s[2 * pair + u] = turn(one, cos_s[rows, :], sin_s[rows, :]).astype(BF16)

    for i in range(2):
        here = SLAB * z + QBLK * i + iota((1, QBLK), 1)
        begin = jnp.zeros((1, QBLK), jnp.int32)
        for v in range(1, SEGS):
            begin = jnp.where(here >= starts[v], jnp.maximum(begin, starts[v]), begin)
        there = first + QBLK * i + iota((WINDOW, 1), 0)
        mask_s[i] = jnp.where((there >= begin) & (there <= here), 0.0, MASKED)

    dk_s[...] = jnp.zeros_like(dk_s)
    dv_s[...] = jnp.zeros_like(dv_s)
    tiles = WINDOW // KTILE

    def one_head(h, _):
        lanes = pl.ds(pl.multiple_of(h * HEAD_DIM, HEAD_DIM), HEAD_DIM)
        for i in range(2):
            q_rows = slice(QBLK * i, QBLK * (i + 1))
            query = q_s[h, q_rows, :]
            up = up_s[q_rows, lanes]
            up_t = jnp.transpose(up.astype(F32))
            top = None
            for t in range(tiles):
                k_rows = slice(QBLK * i + KTILE * t, QBLK * i + KTILE * (t + 1))
                tile = slice(KTILE * t, KTILE * (t + 1))
                score = dot(k_s[k_rows, :], query, NT) * (scale * LOG2E) + mask_s[i, tile, :]
                s_s[tile, :] = score
                peak = jnp.max(score, axis=0, keepdims=True)
                top = peak if top is None else jnp.maximum(top, peak)
            total = None
            for t in range(tiles):
                tile = slice(KTILE * t, KTILE * (t + 1))
                weight = jnp.exp2(s_s[tile, :] - top)
                s_s[tile, :] = weight
                share = jnp.sum(weight, axis=0, keepdims=True)
                total = share if total is None else total + share
            invert = 1.0 / total
            out_t = None
            for t in range(tiles):
                k_rows = slice(QBLK * i + KTILE * t, QBLK * i + KTILE * (t + 1))
                tile = slice(KTILE * t, KTILE * (t + 1))
                prob = s_s[tile, :] * invert
                s_s[tile, :] = prob
                prob_low = prob.astype(BF16)
                term = dot(vt_s[:, k_rows], prob_low)
                out_t = term if out_t is None else out_t + term
                dv_s[k_rows, :] += dot(prob_low, up)
                p_s[tile, :] = dot(v_s[k_rows, :], up, NT)
            out_low = out_t.astype(BF16).astype(F32)
            ctx_s[q_rows, lanes] = jnp.transpose(out_low).astype(BF16)
            delta = jnp.sum(up_t * out_low, axis=0, keepdims=True)
            dq_t = None
            for t in range(tiles):
                k_rows = slice(QBLK * i + KTILE * t, QBLK * i + KTILE * (t + 1))
                tile = slice(KTILE * t, KTILE * (t + 1))
                dscore = (s_s[tile, :] * (p_s[tile, :] - delta)).astype(BF16)
                term = dot(kt_s[:, k_rows], dscore)
                dq_t = term if dq_t is None else dq_t + term
                dk_s[k_rows, :] += dot(dscore, query)
            dq = jnp.transpose(dq_t) * scale
            w_rows = slice(2 * SLAB + QBLK * i, 2 * SLAB + QBLK * (i + 1))
            dq = unturn(dq, cos_s[w_rows, :], sin_s[w_rows, :])
            dq_s[q_rows, lanes] = dq.astype(BF16)
            mine = jnp.sum(dq, axis=0, keepdims=True)
            if i == 0:
                bias_ref[pl.ds(h, 1), :] = mine
            else:
                bias_ref[pl.ds(h, 1), :] += mine
        return 0

    lax.fori_loop(0, GROUP, one_head, 0)

    for s, ref in enumerate((ctx0, ctx1, ctx2, ctx3)):
        ref[...] = ctx_s[pl.ds(pl.multiple_of(TOK * (j ^ s), TOK), TOK), :]

    sum_k = jnp.zeros((1, HEAD_DIM), F32)
    sum_v = jnp.zeros((1, HEAD_DIM), F32)
    across = iota((SLAB, SLAB), 1).astype(F32)
    for t in range(3):
        rows = slice(SLAB * t, SLAB * (t + 1))
        pos = meta[:, 2 * t : 2 * t + 1] * 128.0 + meta[:, 2 * t + 1 : 2 * t + 2]
        drop = jnp.where(across == pos, 1.0, 0.0).astype(BF16)
        dk = unturn(dk_s[rows, :] * scale, cos_s[rows, :], sin_s[rows, :])
        dv = dv_s[rows, :]
        sum_k = sum_k + jnp.sum(dk, axis=0, keepdims=True)
        sum_v = sum_v + jnp.sum(dv, axis=0, keepdims=True)
        base = PART + 256 * t
        both = jnp.concatenate([dk.astype(BF16), dv.astype(BF16)], axis=1)
        back_ref[:, base : base + 256] = dot(drop, both).astype(BF16)
        if t == 2:
            for pair in range(4):
                lanes = slice(256 * pair, 256 * (pair + 1))
                back_ref[:, lanes] = dot(drop, dq_s[:, lanes]).astype(BF16)
    bias_ref[8:9, :] = sum_k
    bias_ref[9:10, :] = sum_v
    bias_ref[10:16, :] = jnp.zeros((6, HEAD_DIM), F32)


def join_kernel(col_ref, c0, c1, c2, c3, out_ref):
    j = col_ref[0] % 4
    for s, ref in enumerate((c0, c1, c2, c3)):
        out_ref[:, pl.ds(pl.multiple_of(PART * (j ^ s), PART), PART)] = ref[...]


def unpack_kernel(back_ref, place_ref, gq_ref, gk_ref, gv_ref, q_s, k_s, v_s):
    place_row = place_ref[...].astype(F32)
    place_col = row_to_column(place_row, TOK)
    rank = jnp.sum(jnp.where(place_row < place_col, 1.0, 0.0), axis=1, keepdims=True)
    pick = jnp.where(iota((TOK, TOK), 1).astype(F32) == rank, 1.0, 0.0).astype(BF16)
    for j in range(KV_HEADS):
        head = slice(HEAD_DIM * j, HEAD_DIM * (j + 1))
        for s in range(8):
            rows = slice(16 * s, 16 * s + 16)
            q_s[rows, :] = back_ref[4 * s + j, :, 0:PART]
            total = None
            for t in range(3):
                base = PART + 256 * t
                term = back_ref[4 * ((s + 2 - t) % 8) + j, :, base : base + 256].astype(F32)
                total = term if total is None else total + term
            k_s[rows, head] = total[:, :128].astype(BF16)
            v_s[rows, head] = total[:, 128:].astype(BF16)
        gq_ref[:, PART * j : PART * (j + 1)] = dot(pick, q_s[...]).astype(BF16)
    gk_ref[...] = dot(pick, k_s[...]).astype(BF16)
    gv_ref[...] = dot(pick, v_s[...]).astype(BF16)


def vmem_spec():
    return pl.BlockSpec(memory_space=pltpu.VMEM)


def shape(dims, dtype):
    return jax.ShapeDtypeStruct(dims, dtype)


def swap(values, axis, step, size):
    return lax.ppermute(values, axis, [(c, c ^ step) for c in range(size)])


def rotation_tables():
    offset = jnp.arange(-TOK, 1024 + TOK, dtype=jnp.int32).astype(F32)
    powers = jnp.arange(HEAD_DIM // 2, dtype=F32) * (2.0 / HEAD_DIM)
    rates = ROPE_BASE ** (-powers)
    angle = offset[:, None] * rates[None, :]
    cosine = jnp.cos(angle)
    sine = jnp.sin(angle)
    return (
        jnp.concatenate([cosine, cosine], axis=1),
        jnp.concatenate([-sine, sine], axis=1),
    )


def per_device(q_load, k_load, v_load, q_bias, k_bias, v_bias, place, segment, d_context):
    col = lax.axis_index("col")
    row = lax.axis_index("row")
    j = col % 4
    col_arr = col.reshape(1).astype(jnp.int32)
    smem = pl.BlockSpec(memory_space=pltpu.SMEM)

    packed = pl.pallas_call(
        pack_kernel,
        out_shape=shape((32, 16, SENT), BF16),
        in_specs=[vmem_spec()] * 5,
        out_specs=vmem_spec(),
        compiler_params=pltpu.CompilerParams(vmem_limit_bytes=24 * MIB),
        cost_estimate=pl.CostEstimate(flops=2 * 128 * 128 * 5120, bytes_accessed=5 * MIB, transcendentals=0),
    )(q_load[0], k_load[0], v_load[0], place, segment)
    recv = lax.all_to_all(packed, "col", split_axis=0, concat_axis=0, tiled=True)

    up_own = d_context[0]
    ups = []
    for s in range(4):
        piece = lax.dynamic_slice_in_dim(up_own, PART * (j ^ s), PART, 1)
        ups.append(piece if s == 0 else swap(piece, "col", s, 32))
    cos_table, sin_table = rotation_tables()

    attended = pl.pallas_call(
        attend_kernel,
        out_shape=[shape((TOK, PART), BF16)] * 4
        + [shape((SLAB, BACK), BF16), shape((16, HEAD_DIM), F32)],
        in_specs=[smem] + [vmem_spec()] * 10,
        out_specs=[vmem_spec()] * 6,
        scratch_shapes=[
            pltpu.VMEM((SLAB, PART), BF16),
            pltpu.VMEM((GROUP, SLAB, HEAD_DIM), BF16),
            pltpu.VMEM((3 * SLAB, HEAD_DIM), BF16),
            pltpu.VMEM((3 * SLAB, HEAD_DIM), BF16),
            pltpu.VMEM((HEAD_DIM, 3 * SLAB), BF16),
            pltpu.VMEM((HEAD_DIM, 3 * SLAB), BF16),
            pltpu.VMEM((3 * SLAB, HEAD_DIM), F32),
            pltpu.VMEM((3 * SLAB, HEAD_DIM), F32),
            pltpu.VMEM((2, WINDOW, QBLK), F32),
            pltpu.VMEM((WINDOW, QBLK), F32),
            pltpu.VMEM((WINDOW, QBLK), F32),
            pltpu.VMEM((3 * SLAB, HEAD_DIM), F32),
            pltpu.VMEM((3 * SLAB, HEAD_DIM), F32),
            pltpu.VMEM((SLAB, PART), BF16),
            pltpu.VMEM((SLAB, PART), BF16),
        ],
        compiler_params=pltpu.CompilerParams(vmem_limit_bytes=56 * MIB),
        cost_estimate=pl.CostEstimate(flops=8 * 10**9, bytes_accessed=8 * MIB, transcendentals=5 * 10**6),
    )(
        col_arr, recv.reshape(SLAB, SENT), *ups,
        q_bias.reshape(1, Q_WIDTH), k_bias.reshape(1, KV_WIDTH), v_bias.reshape(1, KV_WIDTH),
        cos_table, sin_table,
    )
    ctx_parts, back, bias = attended[:4], attended[4], attended[5]
    returned = lax.all_to_all(
        back.reshape(32, 16, BACK), "col", split_axis=0, concat_axis=0, tiled=True
    )
    ctx_in = [ctx_parts[0]] + [swap(ctx_parts[s], "col", s, 32) for s in (1, 2, 3)]
    context = pl.pallas_call(
        join_kernel,
        out_shape=shape((TOK, Q_WIDTH), BF16),
        in_specs=[smem] + [vmem_spec()] * 4,
        out_specs=vmem_spec(),
        compiler_params=pltpu.CompilerParams(vmem_limit_bytes=16 * MIB),
        cost_estimate=pl.CostEstimate(flops=0, bytes_accessed=2 * MIB, transcendentals=0),
    )(col_arr, *ctx_in)

    for step in (1, 2, 4):
        bias = bias + swap(bias, "row", step, 8)
    for step in (4, 8, 16):
        bias = bias + swap(bias, "col", step, 32)
    want = row // 2
    bias = jnp.where(j == want, bias, 0.0)
    for step in (1, 2):
        bias = bias + swap(bias, "col", step, 32)
    half = lax.dynamic_slice_in_dim(bias[:8].reshape(PART), 512 * (row % 2), 512, 0)
    bias_q = lax.dynamic_slice_in_dim(half, 16 * col, 16, 0)
    bias_kv = lax.dynamic_slice_in_dim(bias[8:10], 64 * (row % 2) + 2 * col, 2, 1)

    grad_q, grad_k, grad_v = pl.pallas_call(
        unpack_kernel,
        out_shape=[shape((TOK, Q_WIDTH), BF16), shape((TOK, KV_WIDTH), BF16), shape((TOK, KV_WIDTH), BF16)],
        in_specs=[vmem_spec()] * 2,
        out_specs=[vmem_spec()] * 3,
        scratch_shapes=[
            pltpu.VMEM((TOK, PART), BF16),
            pltpu.VMEM((TOK, KV_WIDTH), BF16),
            pltpu.VMEM((TOK, KV_WIDTH), BF16),
        ],
        compiler_params=pltpu.CompilerParams(vmem_limit_bytes=24 * MIB),
        cost_estimate=pl.CostEstimate(flops=2 * 128 * 128 * 5120, bytes_accessed=4 * MIB, transcendentals=0),
    )(returned, place)
    return (context[None], grad_q[None], grad_k[None], grad_v[None], bias_q, bias_kv)


def solution(mesh):
    return jax.shard_map(
        per_device,
        mesh=mesh,
        in_specs=(
            P("row", "col", None),
            P("row", "col", None),
            P("row", "col", None),
            P(),
            P(),
            P(),
            P("row", "col"),
            P("row", "col"),
            P("row", "col", None),
        ),
        out_specs=(
            P("row", "col", None),
            P("row", "col", None),
            P("row", "col", None),
            P("row", "col", None),
            P(("row", "col")),
            P(None, ("row", "col")),
        ),
        check_vma=False,
    )
```

time: 832 us -> 189 us (0.23); the launches traced: 818 us -> 187 us
  waiting for transfers between devices: 235 us -> 95.5 us
  local copies, waits for them, and re-layouts: 146 us -> 7.72 us
  matrix products: 134 us -> 0 us
  blocking collectives: 134 us -> 0 us
  other arithmetic: 78 us -> 3.86 us
  starting transfers between devices: 82.9 us -> 37.8 us
  Pallas kernels: 0 us -> 41.3 us
    all_to_all x15 -> x2, waiting for transfers between devices: 235 us -> 21.3 us  [the longest x1 21.3 us: per_device(): lax.all_to_all(packed, 'col', split_axis=0, concat_axis=0, tiled=True)]
    dot_general x48 -> x0, matrix products: 134 us -> none  [the longest x8 29 us: visit(): lax.dot_general(grad_score, q_part, (((0,), (0,)), ((), ())), preferred_e...]
    unnamed x1 -> x0, blocking collectives: 77.7 us -> none
    ppermute x0 -> x14, waiting for transfers between devices: none -> 74.2 us  [swap(): return lax.ppermute(values, axis, [(c, c ^ step) for c in range(size)])]
    all_to_all x15 -> x2, starting transfers between devices: 82.9 us -> 17.7 us  [the longest x1 11.4 us: per_device(): lax.all_to_all(packed, 'col', split_axis=0, concat_axis=0, tiled=True)]
    scatter x16 -> x0, local copies, waits for them, and re-layouts: 57.7 us -> none  [the longest x8 28.9 us: visit(): lax.dynamic_update_slice_in_dim(grad_keys, lax.dynamic_slice_in_dim(grad_...]
    all_gather x1 -> x0, blocking collectives: 56.5 us -> none  [per_device(): segment_all = lax.all_gather(segment, 'col', axis=1, tiled=True)[0]]
    pallas_call x0 -> x4, Pallas kernels: none -> 41.3 us  [the longest x1 36.8 us: per_device(): pl.pallas_call(attend_kernel, out_shape=[shape((TOK, PART), BF16)] * 4 +...]
  transfers between devices with their start and end apart: 15 -> 16, of which waited for: 13 -> 12; matrix products, arithmetic and copies ran while one was open for 9% -> 3% of each run, Pallas kernels for 0% -> 1%
where the time goes in v1:
time: 189 us; the launch traced here: 187 us
  waiting for transfers between devices  95.5 us (51%)
  Pallas kernels  41.3 us (22%)
  starting transfers between devices  37.8 us (20%)
  local copies, waits for them, and re-layouts  7.72 us (4%)
  other arithmetic  3.86 us (2%)
    ppermute x14, waiting for transfers between devices, swap(): return lax.ppermute(values, axis, [(c, c ^ step) for c in range(size)])  74.2 us
    pallas_call x1, Pallas kernels, per_device(): pl.pallas_call(attend_kernel, out_shape=[shape((TOK, PART), BF16)] * 4 +...  36.8 us
    all_to_all x1, waiting for transfers between devices, per_device(): lax.all_to_all(packed, 'col', split_axis=0, concat_axis=0, tiled=True)  21.3 us
    ppermute x14, starting transfers between devices, swap(): return lax.ppermute(values, axis, [(c, c ^ step) for c in range(size)])  20.1 us
    all_to_all x1, starting transfers between devices, per_device(): lax.all_to_all(packed, 'col', split_axis=0, concat_axis=0, tiled=True)  11.4 us
    all_to_all x1, starting transfers between devices, per_device(): lax.all_to_all(back.reshape(32, 16, BACK), 'col', split_axis=0, concat_ax...  6.27 us
    unnamed x32, local copies, waits for them, and re-layouts  5.68 us
  transfers between devices with their start and end apart: 16, of which 12 were waited for; matrix products, arithmetic and copies ran while one was open for 3% of the time, Pallas kernels for 1%

profile of v1, /device:TPU:16, one launch (start us, length us, event | category | flops | bytes accessed | tf_op | source)
XLA Modules:
  0.0 187.1 jit_solution(14617284542684799743)
XLA Ops:
  0.6 1.2 copy-done
  1.9 0.9 copy-done.2
  2.8 0.9 copy-done.3
  5.0 1.9 %shard_map.136 = bf16[32,16,1920]{2,1,0:T(8,128)(2,1)} custom-call(bf16[128,4096]{1,0:T(8,128)(2,1)S(1)} %bitcast.23, bf16[128,512]{1,0:T(8,128)(2,1)S(1)} %bitcast.24, bf16[128,512]{1,0:T(8,128)(2,1)S(1)} %bitcast.25, s32[1,128]{1,0:T(1,128)S(1)} %copy-done.4, s32[1,128]{1,0:T(1,128)S(1)} %copy-done.6), custom_call_target="tpu_custom_call" | custom-call | flops 167772160 | bytes 5242880 | tf_op jit(solution)/shard_map/pallas_call | solution.py:312
  6.9 11.4 %all-to-all-start = ((bf16[32,16,1920]{2,1,0:T(8,128)(2,1)}), bf16[32,16,1920]{2,1,0:T(8,128)(2,1)S(1)}, u32[]{:S(2)}, u32[]{:S(2)}) async-start(bf16[32,16,1920]{2,1,0:T(8,128)(2,1)} %shard_map.136), calls=%async_computation | async-start | bytes 3932160 | tf_op jit(solution)/shard_map/all_to_all | solution.py:320
  18.4 0.8 dynamic-slice_bitcast_fusion
  19.5 3.2 %collective-permute-start.1 = (bf16[128,1024]{1,0:T(8,128)(2,1)S(1)}, bf16[128,1024]{1,0:T(8,128)(2,1)S(1)}, u32[]{:S(2)}, u32[]{:S(2)}) collective-permute-start(bf16[128,1024]{1,0:T(8,128)(2,1)S(1)} %get-tuple-element.27), channel_id=1, source_target_pairs={{0,2},{1,3},{2,0},{3,1},{4,6},{5,7},{6,4},{7,5},{8,10},{9,11},{10,... | collective-permute-start | bytes 786440 | tf_op jit(solution)/shard_map/ppermute | solution.py:289
  22.7 2.4 %fusion = (f32[1280,64]{1,0:T(8,128)S(1)}, f32[1280,64]{1,0:T(8,128)S(1)}, f32[1280,64]{1,0:T(8,128)S(1)}) fusion(f32[64]{0:T(128)S(1)} %negate_power_fusion, f32[1280]{0:T(1024)S(1)} %add_convert_fusion), kind=kLoop, calls=%fused_computation.8 | loop fusion | flops 163840 | bytes 988416 | tf_op jit(solution)/shard_map/neg | solution.py:301
  25.1 1.5 pad_maximum_fusion
  26.5 13.0 %collective-permute-done.1.up2 = bf16[128,1024]{1,0:T(8,128)(2,1)S(1)} collective-permute-done((bf16[128,1024]{1,0:T(8,128)(2,1)S(1)}, bf16[128,1024]{1,0:T(8,128)(2,1)S(1)}, u32[]{:S(2)}, u32[]{:S(2)}) %collective-permute-start.1) | collective-permute-done | bytes 262176 | tf_op jit(solution)/shard_map/ppermute | solution.py:289
  39.5 5.2 %collective-permute-done.2.up3 = bf16[128,1024]{1,0:T(8,128)(2,1)S(1)} collective-permute-done((bf16[128,1024]{1,0:T(8,128)(2,1)S(1)}, bf16[128,1024]{1,0:T(8,128)(2,1)S(1)}, u32[]{:S(2)}, u32[]{:S(2)}) %collective-permute-start.2) | collective-permute-done | bytes 262176 | tf_op jit(solution)/shard_map/ppermute | solution.py:289
  44.7 21.3 %all-to-all-done = bf16[32,16,1920]{2,1,0:T(8,128)(2,1)S(1)} async-done(((bf16[32,16,1920]{2,1,0:T(8,128)(2,1)}), bf16[32,16,1920]{2,1,0:T(8,128)(2,1)S(1)}, u32[]{:S(2)}, u32[]{:S(2)}) %all-to-all-start) | async-done | bytes 1966112 | tf_op jit(solution)/shard_map/all_to_all | solution.py:320
  66.0 1.3 copy-done.7
  67.3 36.8 %shard_map.137 = (bf16[128,1024]{1,0:T(8,128)(2,1)}, bf16[128,1024]{1,0:T(8,128)(2,1)}, bf16[128,1024]{1,0:T(8,128)(2,1)}, bf16[128,1024]{1,0:T(8,128)(2,1)}, bf...) custom-call(s32[1]{0:T(128)} %bitcast.col_ref, bf16[512,1920]{1,0:T(8,128)(2,1)} %bitcast.26, ...), custom_call_target="tpu_custom_call" | custom-call | flops 8000000000 | bytes 8388608 | tf_op jit(solution)/shard_map/pallas_call | solution.py:329
  104.1 6.3 %all-to-all-start.1 = ((bf16[32,16,1792]{2,1,0:T(8,128)(2,1)}), bf16[32,16,1792]{2,1,0:T(8,128)(2,1)S(1)}, u32[]{:S(2)}, u32[]{:S(2)}) async-start(bf16[32,16,1792]{2,1,0:T(8,128)(2,1)} %bitcast.27), calls=%async_computation.1 | async-start | bytes 3670016 | tf_op jit(solution)/shard_map/all_to_all | solution.py:360
  110.4 0.7 collective-permute-start.6
  111.1 4.5 %collective-permute-done.6 = f32[16,128]{1,0:T(8,128)S(1)} collective-permute-done((f32[16,128]{1,0:T(8,128)S(1)}, f32[16,128]{1,0:T(8,128)S(1)}, u32[]{:S(2)}, u32[]{:S(2)}) %collective-permute-start.6) | collective-permute-done | bytes 8224 | tf_op jit(solution)/shard_map/ppermute | solution.py:289
  115.5 1.3 collective-permute-start.7
  116.8 2.3 %collective-permute-done.7 = f32[16,128]{1,0:T(8,128)S(1)} collective-permute-done((f32[16,128]{1,0:T(8,128)S(1)}, f32[16,128]{1,0:T(8,128)S(1)}, u32[]{:S(2)}, u32[]{:S(2)}) %collective-permute-start.7) | collective-permute-done | bytes 8224 | tf_op jit(solution)/shard_map/ppermute | solution.py:289
  119.5 4.8 %collective-permute-done.8 = f32[16,128]{1,0:T(8,128)S(1)} collective-permute-done((f32[16,128]{1,0:T(8,128)S(1)}, f32[16,128]{1,0:T(8,128)S(1)}, u32[]{:S(2)}, u32[]{:S(2)}) %collective-permute-start.8) | collective-permute-done | bytes 8224 | tf_op jit(solution)/shard_map/ppermute | solution.py:289
  124.4 3.1 %collective-permute-start.9 = (f32[16,128]{1,0:T(8,128)S(1)}, f32[16,128]{1,0:T(8,128)S(1)}, u32[]{:S(2)}, u32[]{:S(2)}) collective-permute-start(f32[16,128]{1,0:T(8,128)S(1)} %add.83), channel_id=1, source_target_pairs={{0,4},{1,5},{2,6},{3,7},{4,0},{5,1},{6,2},{7,3},{8,12},{9,13},{10,... | collective-permute-start | bytes 24584 | tf_op jit(solution)/shard_map/ppermute | solution.py:289
  127.5 25.2 %collective-permute-done.9 = f32[16,128]{1,0:T(8,128)S(1)} collective-permute-done((f32[16,128]{1,0:T(8,128)S(1)}, f32[16,128]{1,0:T(8,128)S(1)}, u32[]{:S(2)}, u32[]{:S(2)}) %collective-permute-start.9) | collective-permute-done | bytes 8224 | tf_op jit(solution)/shard_map/ppermute | solution.py:289
  153.0 4.3 %collective-permute-done.10 = f32[16,128]{1,0:T(8,128)S(1)} collective-permute-done((f32[16,128]{1,0:T(8,128)S(1)}, f32[16,128]{1,0:T(8,128)S(1)}, u32[]{:S(2)}, u32[]{:S(2)}) %collective-permute-start.10) | collective-permute-done | bytes 8224 | tf_op jit(solution)/shard_map/ppermute | solution.py:289
  157.3 4.6 %collective-permute-start.11 = (f32[16,128]{1,0:T(8,128)S(1)}, f32[16,128]{1,0:T(8,128)S(1)}, u32[]{:S(2)}, u32[]{:S(2)}) collective-permute-start(f32[16,128]{1,0:T(8,128)S(1)} %add.85), channel_id=1, source_target_pairs={{0,16},{1,17},{2,18},{3,19},{4,20},{5,21},{6,22},{7,23},{8,24},{9,... | collective-permute-start | bytes 24584 | tf_op jit(solution)/shard_map/ppermute | solution.py:289
  161.9 3.0 %collective-permute-done.11 = f32[16,128]{1,0:T(8,128)S(1)} collective-permute-done((f32[16,128]{1,0:T(8,128)S(1)}, f32[16,128]{1,0:T(8,128)S(1)}, u32[]{:S(2)}, u32[]{:S(2)}) %collective-permute-start.11) | collective-permute-done | bytes 8224 | tf_op jit(solution)/shard_map/ppermute | solution.py:289
  164.9 1.2 collective-permute-done.12
  166.0 3.0 %collective-permute-start.13 = (f32[16,128]{1,0:T(8,128)S(1)}, f32[16,128]{1,0:T(8,128)S(1)}, u32[]{:S(2)}, u32[]{:S(2)}) collective-permute-start(f32[16,128]{1,0:T(8,128)S(1)} %add.87), channel_id=1, source_target_pairs={{0,2},{1,3},{2,0},{3,1},{4,6},{5,7},{6,4},{7,5},{8,10},{9,11},{10,... | collective-permute-start | bytes 24584 | tf_op jit(solution)/shard_map/ppermute | solution.py:289
  169.7 2.7 %collective-permute-start.5 = (bf16[128,1024]{1,0:T(8,128)(2,1)S(1)}, bf16[128,1024]{1,0:T(8,128)(2,1)S(1)}, u32[]{:S(2)}, u32[]{:S(2)}) collective-permute-start(bf16[128,1024]{1,0:T(8,128)(2,1)S(1)} %copy-done.10), channel_id=1, source_target_pairs={{0,3},{1,2},{2,1},{3,0},{4,7},{5,6},{6,5},{7,4},{8,11},{9,10},{10,... | collective-permute-start | bytes 786440 | tf_op jit(solution)/shard_map/ppermute | solution.py:289
  173.6 6.1 %collective-permute-done.4.c2 = bf16[128,1024]{1,0:T(8,128)(2,1)S(1)} collective-permute-done((bf16[128,1024]{1,0:T(8,128)(2,1)S(1)}, bf16[128,1024]{1,0:T(8,128)(2,1)S(1)}, u32[]{:S(2)}, u32[]{:S(2)}) %collective-permute-start.4) | collective-permute-done | bytes 262176 | tf_op jit(solution)/shard_map/ppermute | solution.py:289
  179.7 4.7 %collective-permute-done.5.c3 = bf16[128,1024]{1,0:T(8,128)(2,1)S(1)} collective-permute-done((bf16[128,1024]{1,0:T(8,128)(2,1)S(1)}, bf16[128,1024]{1,0:T(8,128)(2,1)S(1)}, u32[]{:S(2)}, u32[]{:S(2)}) %collective-permute-start.5) | collective-permute-done | bytes 262176 | tf_op jit(solution)/shard_map/ppermute | solution.py:289
  184.4 1.0 shard_map.138
  185.5 1.6 shard_map.139
  (53 shorter events, 4.2 us)
Async XLA Ops:
  0.6 1.2 copy-start
  1.9 0.9 copy-start.2
  2.8 0.9 copy-start.3
  3.7 0.7 copy-start.4
  4.3 0.7 copy-start.6
  6.9 11.5 %copy-start.8 = (bf16[1,128,4096]{2,1,0:T(8,128)(2,1)S(1)}, bf16[1,128,4096]{2,1,0:T(8,128)(2,1)}, u32[]{:S(2)}) copy-start(bf16[1,128,4096]{2,1,0:T(8,128)(2,1)} %param.17) | copy-start | bytes 3145732
  6.9 59.1 %all-to-all-start = ((bf16[32,16,1920]{2,1,0:T(8,128)(2,1)}), bf16[32,16,1920]{2,1,0:T(8,128)(2,1)S(1)}, u32[]{:S(2)}, u32[]{:S(2)}) async-start(bf16[32,16,1920]{2,1,0:T(8,128)(2,1)} %shard_map.136), calls=%async_computation | async-start | bytes 3932160 | tf_op jit(solution)/shard_map/all_to_all | solution.py:320
  19.2 7.3 %collective-permute-start = (bf16[128,1024]{1,0:T(8,128)(2,1)S(1)}, bf16[128,1024]{1,0:T(8,128)(2,1)S(1)}, u32[]{:S(2)}, u32[]{:S(2)}) collective-permute-start(bf16[128,1024]{1,0:T(8,128)(2,1)S(1)} %get-tuple-element.25), channel_id=1, source_target_pairs={{0,1},{1,0},{2,3},{3,2},{4,5},{5,4},{6,7},{7,6},{8,9},{9,8},{10,11... | collective-permute-start | bytes 786440 | tf_op jit(solution)/shard_map/ppermute | solution.py:289
  19.5 20.0 %collective-permute-start.1 = (bf16[128,1024]{1,0:T(8,128)(2,1)S(1)}, bf16[128,1024]{1,0:T(8,128)(2,1)S(1)}, u32[]{:S(2)}, u32[]{:S(2)}) collective-permute-start(bf16[128,1024]{1,0:T(8,128)(2,1)S(1)} %get-tuple-element.27), channel_id=1, source_target_pairs={{0,2},{1,3},{2,0},{3,1},{4,6},{5,7},{6,4},{7,5},{8,10},{9,11},{10,... | collective-permute-start | bytes 786440 | tf_op jit(solution)/shard_map/ppermute | solution.py:289
  22.7 22.0 %collective-permute-start.2 = (bf16[128,1024]{1,0:T(8,128)(2,1)S(1)}, bf16[128,1024]{1,0:T(8,128)(2,1)S(1)}, u32[]{:S(2)}, u32[]{:S(2)}) collective-permute-start(bf16[128,1024]{1,0:T(8,128)(2,1)S(1)} %get-tuple-element.24), channel_id=1, source_target_pairs={{0,3},{1,2},{2,1},{3,0},{4,7},{5,6},{6,5},{7,4},{8,11},{9,10},{10,... | collective-permute-start | bytes 786440 | tf_op jit(solution)/shard_map/ppermute | solution.py:289
  26.5 39.4 %copy-start.13 = (bf16[128,1024]{1,0:T(8,128)(2,1)}, bf16[128,1024]{1,0:T(8,128)(2,1)S(1)}, u32[]{:S(2)}) copy-start(bf16[128,1024]{1,0:T(8,128)(2,1)S(1)} %collective-permute-done.up1) | copy-start | bytes 786436
  39.5 26.5 %copy-start.14 = (bf16[128,1024]{1,0:T(8,128)(2,1)}, bf16[128,1024]{1,0:T(8,128)(2,1)S(1)}, u32[]{:S(2)}) copy-start(bf16[128,1024]{1,0:T(8,128)(2,1)S(1)} %collective-permute-done.1.up2) | copy-start | bytes 786436
  44.7 21.3 %copy-start.15 = (bf16[128,1024]{1,0:T(8,128)(2,1)}, bf16[128,1024]{1,0:T(8,128)(2,1)S(1)}, u32[]{:S(2)}) copy-start(bf16[128,1024]{1,0:T(8,128)(2,1)S(1)} %collective-permute-done.2.up3) | copy-start | bytes 786436
  66.0 1.3 copy-start.7
  104.0 6.3 %copy-start.9 = (f32[16,128]{1,0:T(8,128)S(1)}, f32[16,128]{1,0:T(8,128)}, u32[]{:S(2)}) copy-start(f32[16,128]{1,0:T(8,128)} %get-tuple-element.23) | copy-start | bytes 24580
  104.1 65.0 %copy-start.12 = (bf16[128,1024]{1,0:T(8,128)(2,1)S(1)}, bf16[128,1024]{1,0:T(8,128)(2,1)}, u32[]{:S(2)}) copy-start(bf16[128,1024]{1,0:T(8,128)(2,1)} %get-tuple-element.16) | copy-start | bytes 786436
  104.1 65.0 %copy-start.11 = (bf16[128,1024]{1,0:T(8,128)(2,1)S(1)}, bf16[128,1024]{1,0:T(8,128)(2,1)}, u32[]{:S(2)}) copy-start(bf16[128,1024]{1,0:T(8,128)(2,1)} %get-tuple-element.17) | copy-start | bytes 786436
  104.1 65.6 %copy-start.10 = (bf16[128,1024]{1,0:T(8,128)(2,1)S(1)}, bf16[128,1024]{1,0:T(8,128)(2,1)}, u32[]{:S(2)}) copy-start(bf16[128,1024]{1,0:T(8,128)(2,1)} %get-tuple-element.18) | copy-start | bytes 786436
  104.1 80.3 %copy-start.1 = (bf16[128,1024]{1,0:T(8,128)(2,1)S(1)}, bf16[128,1024]{1,0:T(8,128)(2,1)}, u32[]{:S(2)}) copy-start(bf16[128,1024]{1,0:T(8,128)(2,1)} %get-tuple-element.15.c0) | copy-start | bytes 786436
  104.1 81.4 %all-to-all-start.1 = ((bf16[32,16,1792]{2,1,0:T(8,128)(2,1)}), bf16[32,16,1792]{2,1,0:T(8,128)(2,1)S(1)}, u32[]{:S(2)}, u32[]{:S(2)}) async-start(bf16[32,16,1792]{2,1,0:T(8,128)(2,1)} %bitcast.27), calls=%async_computation.1 | async-start | bytes 3670016 | tf_op jit(solution)/shard_map/all_to_all | solution.py:360
  110.4 75.1 %copy-start.5 = (s32[1,128]{1,0:T(1,128)S(1)}, s32[1,128]{1,0:T(1,128)}, u32[]{:S(2)}) copy-start(s32[1,128]{1,0:T(1,128)} %place_ref.3) | copy-start | bytes 1540
  110.4 5.2 %collective-permute-start.6 = (f32[16,128]{1,0:T(8,128)S(1)}, f32[16,128]{1,0:T(8,128)S(1)}, u32[]{:S(2)}, u32[]{:S(2)}) collective-permute-start(f32[16,128]{1,0:T(8,128)S(1)} %copy-done.9), channel_id=1, source_target_pairs={{0,32},{32,0},{64,96},{96,64},{128,160},{160,128},{192,224},{224,1... | collective-permute-start | bytes 24584 | tf_op jit(solution)/shard_map/ppermute | solution.py:289
  115.5 3.7 %collective-permute-start.7 = (f32[16,128]{1,0:T(8,128)S(1)}, f32[16,128]{1,0:T(8,128)S(1)}, u32[]{:S(2)}, u32[]{:S(2)}) collective-permute-start(f32[16,128]{1,0:T(8,128)S(1)} %add.81), channel_id=1, source_target_pairs={{0,64},{32,96},{64,0},{96,32},{128,192},{160,224},{192,128},{224,1... | collective-permute-start | bytes 24584 | tf_op jit(solution)/shard_map/ppermute | solution.py:289
  119.2 5.2 %collective-permute-start.8 = (f32[16,128]{1,0:T(8,128)S(1)}, f32[16,128]{1,0:T(8,128)S(1)}, u32[]{:S(2)}, u32[]{:S(2)}) collective-permute-start(f32[16,128]{1,0:T(8,128)S(1)} %add.82), channel_id=1, source_target_pairs={{0,128},{32,160},{64,192},{96,224},{128,0},{160,32},{192,64},{224,... | collective-permute-start | bytes 24584 | tf_op jit(solution)/shard_map/ppermute | solution.py:289
  124.4 28.4 %collective-permute-start.9 = (f32[16,128]{1,0:T(8,128)S(1)}, f32[16,128]{1,0:T(8,128)S(1)}, u32[]{:S(2)}, u32[]{:S(2)}) collective-permute-start(f32[16,128]{1,0:T(8,128)S(1)} %add.83), channel_id=1, source_target_pairs={{0,4},{1,5},{2,6},{3,7},{4,0},{5,1},{6,2},{7,3},{8,12},{9,13},{10,... | collective-permute-start | bytes 24584 | tf_op jit(solution)/shard_map/ppermute | solution.py:289
  152.7 4.5 %collective-permute-start.10 = (f32[16,128]{1,0:T(8,128)S(1)}, f32[16,128]{1,0:T(8,128)S(1)}, u32[]{:S(2)}, u32[]{:S(2)}) collective-permute-start(f32[16,128]{1,0:T(8,128)S(1)} %add.84), channel_id=1, source_target_pairs={{0,8},{1,9},{2,10},{3,11},{4,12},{5,13},{6,14},{7,15},{8,0},{9,1},... | collective-permute-start | bytes 24584 | tf_op jit(solution)/shard_map/ppermute | solution.py:289
  157.3 7.6 %collective-permute-start.11 = (f32[16,128]{1,0:T(8,128)S(1)}, f32[16,128]{1,0:T(8,128)S(1)}, u32[]{:S(2)}, u32[]{:S(2)}) collective-permute-start(f32[16,128]{1,0:T(8,128)S(1)} %add.85), channel_id=1, source_target_pairs={{0,16},{1,17},{2,18},{3,19},{4,20},{5,21},{6,22},{7,23},{8,24},{9,... | collective-permute-start | bytes 24584 | tf_op jit(solution)/shard_map/ppermute | solution.py:289
  164.9 1.2 collective-permute-start.12
  166.0 6.4 %collective-permute-start.13 = (f32[16,128]{1,0:T(8,128)S(1)}, f32[16,128]{1,0:T(8,128)S(1)}, u32[]{:S(2)}, u32[]{:S(2)}) collective-permute-start(f32[16,128]{1,0:T(8,128)S(1)} %add.87), channel_id=1, source_target_pairs={{0,2},{1,3},{2,0},{3,1},{4,6},{5,7},{6,4},{7,5},{8,10},{9,11},{10,... | collective-permute-start | bytes 24584 | tf_op jit(solution)/shard_map/ppermute | solution.py:289
  169.0 4.6 %collective-permute-start.3 = (bf16[128,1024]{1,0:T(8,128)(2,1)S(1)}, bf16[128,1024]{1,0:T(8,128)(2,1)S(1)}, u32[]{:S(2)}, u32[]{:S(2)}) collective-permute-start(bf16[128,1024]{1,0:T(8,128)(2,1)S(1)} %copy-done.12), channel_id=1, source_target_pairs={{0,1},{1,0},{2,3},{3,2},{4,5},{5,4},{6,7},{7,6},{8,9},{9,8},{10,11... | collective-permute-start | bytes 786440 | tf_op jit(solution)/shard_map/ppermute | solution.py:289
  169.0 10.7 %collective-permute-start.4 = (bf16[128,1024]{1,0:T(8,128)(2,1)S(1)}, bf16[128,1024]{1,0:T(8,128)(2,1)S(1)}, u32[]{:S(2)}, u32[]{:S(2)}) collective-permute-start(bf16[128,1024]{1,0:T(8,128)(2,1)S(1)} %copy-done.11), channel_id=1, source_target_pairs={{0,2},{1,3},{2,0},{3,1},{4,6},{5,7},{6,4},{7,5},{8,10},{9,11},{10,... | collective-permute-start | bytes 786440 | tf_op jit(solution)/shard_map/ppermute | solution.py:289
  169.7 14.7 %collective-permute-start.5 = (bf16[128,1024]{1,0:T(8,128)(2,1)S(1)}, bf16[128,1024]{1,0:T(8,128)(2,1)S(1)}, u32[]{:S(2)}, u32[]{:S(2)}) collective-permute-start(bf16[128,1024]{1,0:T(8,128)(2,1)S(1)} %copy-done.10), channel_id=1, source_target_pairs={{0,3},{1,2},{2,1},{3,0},{4,7},{5,6},{6,5},{7,4},{8,11},{9,10},{10,... | collective-permute-start | bytes 786440 | tf_op jit(solution)/shard_map/ppermute | solution.py:289

commit v2 on v1

v2 whole, which is shorter than its diff:
```python
import functools

import jax
import jax.numpy as jnp
from jax import lax
from jax.experimental import pallas as pl
from jax.experimental.pallas import tpu as pltpu
from jax.sharding import PartitionSpec as P

HEADS = 32
KV_HEADS = 4
GROUP = 8
HEAD_DIM = 128
SEGS = 8
TOK = 128
SLAB = 512
QBLK = 256
KTILE = 256
WINDOW = 1280
Q_WIDTH = HEADS * HEAD_DIM
KV_WIDTH = KV_HEADS * HEAD_DIM
PART = GROUP * HEAD_DIM
SENT = PART + 6 * HEAD_DIM + 128
BACK = PART + 6 * HEAD_DIM
MIB = 1024 * 1024

ROPE_BASE = 1000000.0
MASKED = -1e30
LOG2E = 1.4426950408889634
F32 = jnp.float32
BF16 = jnp.bfloat16

NN = (((1,), (0,)), ((), ()))
NT = (((1,), (1,)), ((), ()))


def dot(a, b, dims=NN):
    return lax.dot_general(a, b, dims, preferred_element_type=F32)


def iota(shape, axis):
    return lax.broadcasted_iota(jnp.int32, shape, axis)


def row_to_column(row, size):
    same = iota((size, size), 0) == iota((size, size), 1)
    return jnp.sum(jnp.where(same, row, 0.0), axis=1, keepdims=True)


def pack_kernel(q_hbm, k_hbm, v_hbm, place_hbm, seg_hbm, out_hbm, q_s, k_s, v_s, place_s, seg_s, out_s, sems):
    names = [(place_hbm, place_s), (seg_hbm, seg_s), (k_hbm, k_s), (v_hbm, v_s)]
    loads = [pltpu.make_async_copy(src, dst, sems.at[n]) for n, (src, dst) in enumerate(names)]
    for j in range(KV_HEADS):
        lanes = slice(PART * j, PART * (j + 1))
        loads.append(pltpu.make_async_copy(q_hbm.at[:, lanes], q_s.at[:, lanes], sems.at[4 + j]))
    for load in loads:
        load.start()
    loads[0].wait()
    loads[1].wait()
    place_row = place_s[...].astype(F32)
    place_col = row_to_column(place_row, TOK)
    rank = jnp.sum(jnp.where(place_col < place_row, 1.0, 0.0), axis=0, keepdims=True)
    pick = iota((TOK, TOK), 0).astype(F32) == rank
    pick_low = jnp.where(pick, 1.0, 0.0).astype(BF16)
    ranked = jnp.sum(jnp.where(pick, place_row, 0.0), axis=1, keepdims=True)
    inside = ranked - ((iota((TOK, 1), 0) // 16) * SLAB).astype(F32)
    high = jnp.floor(inside * (1.0 / 128.0))
    low = inside - 128.0 * high
    seg_col = row_to_column(seg_s[...].astype(F32), TOK)
    lane = iota((TOK, 128), 1)
    below = jnp.sum(
        jnp.where(seg_col < (lane - 8).astype(F32), 1.0, 0.0), axis=0, keepdims=True
    )
    lane16 = iota((16, 128), 1)
    counts = jnp.where(iota((16, 128), 0) == 0, below, 0.0)
    metas = []
    for z in range(8):
        meta = counts
        for t in range(3):
            s = (z - 2 + t) % 8
            rows = slice(16 * s, 16 * s + 16)
            meta = jnp.where(lane16 == 2 * t, high[rows], meta)
            meta = jnp.where(lane16 == 2 * t + 1, low[rows], meta)
        metas.append(meta.astype(BF16))
    loads[2].wait()
    loads[3].wait()
    keys = dot(pick_low, k_s[...]).astype(BF16)
    vals = dot(pick_low, v_s[...]).astype(BF16)
    stores = []
    for j in range(KV_HEADS):
        loads[4 + j].wait()
        part = dot(pick_low, q_s[:, PART * j : PART * (j + 1)]).astype(BF16)
        head = slice(HEAD_DIM * j, HEAD_DIM * (j + 1))
        for z in range(8):
            out_s[z, j, :, 0:PART] = part[16 * z : 16 * z + 16]
            for t in range(3):
                s = (z - 2 + t) % 8
                rows = slice(16 * s, 16 * s + 16)
                base = PART + 256 * t
                out_s[z, j, :, base : base + 128] = keys[rows, head]
                out_s[z, j, :, base + 128 : base + 256] = vals[rows, head]
            out_s[z, j, :, BACK:SENT] = metas[z]
        store = pltpu.make_async_copy(out_s.at[:, j], out_hbm.at[:, j], sems.at[8 + j])
        store.start()
        stores.append(store)
    for store in stores:
        store.wait()


def turn(values, cosine, sine):
    return values * cosine + pltpu.roll(values, HEAD_DIM // 2, 1) * sine


def unturn(values, cosine, sine):
    return values * cosine - pltpu.roll(values, HEAD_DIM // 2, 1) * sine


def attend_kernel(
    col_ref, recv_hbm, up0, up1, up2, up3, qb_hbm, kb_hbm, vb_hbm, cos_hbm, sin_hbm,
    ctx0, ctx1, ctx2, ctx3, back_hbm, bias_ref,
    recv_s, cos_t, sin_t, qb_s, kb_s, vb_s,
    up_s, q_s, k_s, v_s, kt_s, vt_s, cos_s, sin_s, mask_s, s_s, p_s, dk_s, dv_s, ctx_s, dq_s, back_s, sems,
):
    col = col_ref[0]
    z = col // 4
    j = col % 4
    first = SLAB * (z - 2)
    scale = HEAD_DIM ** (-0.5)

    copies = [
        pltpu.make_async_copy(recv_hbm, recv_s, sems.at[0]),
        pltpu.make_async_copy(cos_hbm, cos_t, sems.at[1]),
        pltpu.make_async_copy(sin_hbm, sin_t, sems.at[2]),
        pltpu.make_async_copy(kb_hbm.at[:, pl.ds(pl.multiple_of(HEAD_DIM * j, HEAD_DIM), HEAD_DIM)], kb_s, sems.at[3]),
        pltpu.make_async_copy(vb_hbm.at[:, pl.ds(pl.multiple_of(HEAD_DIM * j, HEAD_DIM), HEAD_DIM)], vb_s, sems.at[4]),
        pltpu.make_async_copy(qb_hbm.at[:, pl.ds(pl.multiple_of(PART * j, PART), PART)], qb_s, sems.at[5]),
    ]
    for s, ref in enumerate((up0, up1, up2, up3)):
        copies.append(
            pltpu.make_async_copy(
                ref, up_s.at[pl.ds(pl.multiple_of(TOK * (j ^ s), TOK), TOK), :], sems.at[6 + s]
            )
        )
    for copy in copies:
        copy.start()
    dk_s[...] = jnp.zeros_like(dk_s)
    dv_s[...] = jnp.zeros_like(dv_s)
    cos_s[...] = jnp.zeros_like(cos_s)
    sin_s[...] = jnp.zeros_like(sin_s)
    mask_s[...] = jnp.where(iota((QBLK, QBLK), 0) <= iota((QBLK, QBLK), 1), 0.0, MASKED)
    for copy in copies:
        copy.wait()

    meta = recv_s[:, BACK:SENT].astype(F32)
    meta_rows = jnp.transpose(meta)
    sums = jnp.sum(meta, axis=0, keepdims=True)
    starts = [jnp.sum(meta[:, 8 + v : 9 + v]).astype(jnp.int32) for v in range(SEGS)]

    for b in range(12):
        at = first + TOK * b
        rows = slice(TOK * b, TOK * (b + 1))
        for v in range(SEGS):
            begin = starts[v]
            end = starts[v + 1] if v + 1 < SEGS else jnp.int32(8 * SLAB)

            @pl.when((begin < at + TOK) & (end > at))
            def _():
                src = pl.ds(at - begin + TOK, TOK)
                inside = at + iota((TOK, HEAD_DIM), 0) >= begin
                cos_s[rows, :] = jnp.where(inside, cos_t[src, :], cos_s[rows, :])
                sin_s[rows, :] = jnp.where(inside, sin_t[src, :], sin_s[rows, :])

    lane = iota((1, HEAD_DIM), 1)
    named = (lane >= 8) & (lane < 16)
    lower = jnp.where(named, sums, 1e9)
    upper = jnp.where(named, jnp.where(lane == 15, 8.0 * SLAB, pltpu.roll(sums, HEAD_DIM - 1, 1)), -1e9)
    upper = jnp.where(lane == 16, 0.0, upper)
    lower = jnp.where(lane == 16, -1e9, lower)
    spot = iota((SLAB, SLAB), 0).astype(F32)
    for t in range(3):
        pos = meta_rows[2 * t : 2 * t + 1] * 128.0 + meta_rows[2 * t + 1 : 2 * t + 2]
        pick = jnp.where(spot == pos, 1.0, 0.0).astype(BF16)
        rows = slice(SLAB * t, SLAB * (t + 1))
        base = PART + 256 * t
        both = dot(pick, recv_s[:, base : base + 256])
        keys = turn(both[:, :128] + kb_s[...], cos_s[rows, :], sin_s[rows, :])
        vals = both[:, 128:] + vb_s[...]
        at = (first + SLAB * t + iota((SLAB, HEAD_DIM), 0)).astype(F32)
        name = jnp.where((at >= lower) & (at < upper), 1.0, 0.0)
        k_s[rows, 0:HEAD_DIM] = keys.astype(BF16)
        k_s[rows, HEAD_DIM:] = name.astype(BF16)
        v_s[rows, :] = vals.astype(BF16)
        kt_s[:, rows] = jnp.transpose(keys).astype(BF16)
        vt_s[:, rows] = jnp.transpose(vals).astype(BF16)
        if t == 2:
            other = jnp.where((lane >= 8) & (lane < 17), MASKED * (1.0 - name), 0.0).astype(BF16)
            for pair in range(4):
                lanes = slice(256 * pair, 256 * (pair + 1))
                both = dot(pick, recv_s[:, lanes]) + qb_s[:, lanes]
                for u in range(2):
                    one = both[:, 128 * u : 128 * (u + 1)]
                    q_s[2 * pair + u, :, 0:HEAD_DIM] = turn(one, cos_s[rows, :], sin_s[rows, :]).astype(BF16)
                    q_s[2 * pair + u, :, HEAD_DIM:] = other

    def one_head(h, _):
        lanes = pl.ds(pl.multiple_of(h * HEAD_DIM, HEAD_DIM), HEAD_DIM)
        blocks = range(2)
        q_rows = [slice(QBLK * i, QBLK * (i + 1)) for i in blocks]
        k_rows = [slice(QBLK * i, QBLK * i + WINDOW) for i in blocks]
        query = [q_s[h, q_rows[i], 0:HEAD_DIM] for i in blocks]
        up = [up_s[q_rows[i], lanes] for i in blocks]
        up_t = [jnp.transpose(up[i].astype(F32)) for i in blocks]
        top = [None, None]
        invert = [None, None]
        out_low = [None, None]
        dq_t = [None, None]
        for i in blocks:
            score = dot(k_s[k_rows[i], :], q_s[h, q_rows[i], :], NT)
            s_s[i, 0 : WINDOW - QBLK, :] = score[: WINDOW - QBLK]
            last = score[WINDOW - QBLK :] + mask_s[...]
            s_s[i, WINDOW - QBLK :, :] = last
            top[i] = jnp.maximum(
                jnp.max(score[: WINDOW - QBLK], axis=0, keepdims=True), jnp.max(last, axis=0, keepdims=True)
            )
        for i in blocks:
            p_s[i] = dot(v_s[k_rows[i], :], up[i], NT)
        for i in blocks:
            weight = jnp.exp2((s_s[i] - top[i]) * (scale * LOG2E))
            s_s[i] = weight
            invert[i] = 1.0 / jnp.sum(weight, axis=0, keepdims=True)
        for i in blocks:
            prob = s_s[i] * invert[i]
            s_s[i] = prob
            prob_low = prob.astype(BF16)
            out_t = dot(vt_s[:, k_rows[i]], prob_low)
            dv_s[k_rows[i], :] += dot(prob_low, up[i])
            out_low[i] = out_t.astype(BF16).astype(F32)
        for i in blocks:
            ctx_s[q_rows[i], lanes] = jnp.transpose(out_low[i]).astype(BF16)
            delta = jnp.sum(up_t[i] * out_low[i], axis=0, keepdims=True)
            dscore = (s_s[i] * (p_s[i] - delta)).astype(BF16)
            dq_t[i] = dot(kt_s[:, k_rows[i]], dscore)
            dk_s[k_rows[i], :] += dot(dscore, query[i])
        total = None
        for i in blocks:
            dq = jnp.transpose(dq_t[i]) * scale
            w_rows = slice(2 * SLAB + QBLK * i, 2 * SLAB + QBLK * (i + 1))
            dq = unturn(dq, cos_s[w_rows, :], sin_s[w_rows, :])
            dq_s[q_rows[i], lanes] = dq.astype(BF16)
            mine = jnp.sum(dq, axis=0, keepdims=True)
            total = mine if total is None else total + mine
        bias_ref[pl.ds(h, 1), :] = total
        return 0

    lax.fori_loop(0, GROUP, one_head, 0, unroll=2)

    outs = []
    for s, ref in enumerate((ctx0, ctx1, ctx2, ctx3)):
        outs.append(
            pltpu.make_async_copy(
                ctx_s.at[pl.ds(pl.multiple_of(TOK * (j ^ s), TOK), TOK), :], ref, sems.at[6 + s]
            )
        )
    for copy in outs:
        copy.start()

    sum_k = jnp.zeros((1, HEAD_DIM), F32)
    sum_v = jnp.zeros((1, HEAD_DIM), F32)
    across = iota((SLAB, SLAB), 1).astype(F32)
    for t in (2, 0, 1):
        rows = slice(SLAB * t, SLAB * (t + 1))
        pos = meta[:, 2 * t : 2 * t + 1] * 128.0 + meta[:, 2 * t + 1 : 2 * t + 2]
        drop = jnp.where(across == pos, 1.0, 0.0).astype(BF16)
        if t == 2:
            back_s[:, 0:PART] = dot(drop, dq_s[...]).astype(BF16)
            main = pltpu.make_async_copy(back_s.at[:, 0:PART], back_hbm.at[:, 0:PART], sems.at[0])
            main.start()
            outs.append(main)
        dk = unturn(dk_s[rows, :] * scale, cos_s[rows, :], sin_s[rows, :])
        dv = dv_s[rows, :]
        sum_k = sum_k + jnp.sum(dk, axis=0, keepdims=True)
        sum_v = sum_v + jnp.sum(dv, axis=0, keepdims=True)
        base = PART + 256 * t
        both = jnp.concatenate([dk.astype(BF16), dv.astype(BF16)], axis=1)
        back_s[:, base : base + 256] = dot(drop, both).astype(BF16)
        side = pltpu.make_async_copy(back_s.at[:, base : base + 256], back_hbm.at[:, base : base + 256], sems.at[1 + t])
        side.start()
        outs.append(side)
    bias_ref[8:9, :] = sum_k
    bias_ref[9:10, :] = sum_v
    bias_ref[10:16, :] = jnp.zeros((6, HEAD_DIM), F32)
    for copy in outs:
        copy.wait()


def join_kernel(col_ref, c0, c1, c2, c3, out_ref):
    j = col_ref[0] % 4
    for s, ref in enumerate((c0, c1, c2, c3)):
        out_ref[:, pl.ds(pl.multiple_of(PART * (j ^ s), PART), PART)] = ref[...]


def finish_kernel(at_ref, mine_ref, other_ref, q_ref, kv_ref):
    col = at_ref[0]
    half = at_ref[1] % 2
    total = mine_ref[...] + other_ref[...]
    line = jnp.sum(
        jnp.where(iota((16, 128), 0) == 4 * half + col // 8, total, 0.0), axis=0, keepdims=True
    )
    q_ref[...] = pltpu.roll(line, (128 - 16 * (col % 8)) % 128, 1)[:, :16]
    kv_ref[...] = pltpu.roll(total[8:16], (128 - 64 * half - 2 * col) % 128, 1)[:2, :2]


def unpack_kernel(back_ref, place_ref, gq_ref, gk_ref, gv_ref, q_s, k_s, v_s):
    place_row = place_ref[...].astype(F32)
    place_col = row_to_column(place_row, TOK)
    rank = jnp.sum(jnp.where(place_row < place_col, 1.0, 0.0), axis=1, keepdims=True)
    pick = jnp.where(iota((TOK, TOK), 1).astype(F32) == rank, 1.0, 0.0).astype(BF16)
    for j in range(KV_HEADS):
        head = slice(HEAD_DIM * j, HEAD_DIM * (j + 1))
        for s in range(8):
            rows = slice(16 * s, 16 * s + 16)
            q_s[rows, :] = back_ref[4 * s + j, :, 0:PART]
            total = None
            for t in range(3):
                base = PART + 256 * t
                term = back_ref[4 * ((s + 2 - t) % 8) + j, :, base : base + 256].astype(F32)
                total = term if total is None else total + term
            k_s[rows, head] = total[:, :128].astype(BF16)
            v_s[rows, head] = total[:, 128:].astype(BF16)
        gq_ref[:, PART * j : PART * (j + 1)] = dot(pick, q_s[...]).astype(BF16)
    gk_ref[...] = dot(pick, k_s[...]).astype(BF16)
    gv_ref[...] = dot(pick, v_s[...]).astype(BF16)


def any_spec():
    return pl.BlockSpec(memory_space=pltpu.HBM)


def vmem_spec():
    return pl.BlockSpec(memory_space=pltpu.VMEM)


def shape(dims, dtype):
    return jax.ShapeDtypeStruct(dims, dtype)


def swap(values, axis, step, size):
    return lax.ppermute(values, axis, [(c, c ^ step) for c in range(size)])


def rotation_tables():
    offset = jnp.arange(-TOK, 1024 + TOK, dtype=jnp.int32).astype(F32)
    powers = jnp.arange(HEAD_DIM // 2, dtype=F32) * (2.0 / HEAD_DIM)
    rates = ROPE_BASE ** (-powers)
    angle = offset[:, None] * rates[None, :]
    cosine = jnp.cos(angle)
    sine = jnp.sin(angle)
    return (
        jnp.concatenate([cosine, cosine], axis=1),
        jnp.concatenate([-sine, sine], axis=1),
    )


def attend(col_arr, recv, ups, q_bias, k_bias, v_bias):
    cos_table, sin_table = rotation_tables()
    return pl.pallas_call(
        attend_kernel,
        out_shape=[shape((TOK, PART), BF16)] * 4
        + [shape((SLAB, BACK), BF16), shape((16, HEAD_DIM), F32)],
        in_specs=[pl.BlockSpec(memory_space=pltpu.SMEM)] + [any_spec()] * 10,
        out_specs=[any_spec()] * 5 + [vmem_spec()],
        scratch_shapes=[
            pltpu.VMEM((SLAB, SENT), BF16),
            pltpu.VMEM((1280, HEAD_DIM), F32),
            pltpu.VMEM((1280, HEAD_DIM), F32),
            pltpu.VMEM((1, PART), F32),
            pltpu.VMEM((1, HEAD_DIM), F32),
            pltpu.VMEM((1, HEAD_DIM), F32),
            pltpu.VMEM((SLAB, PART), BF16),
            pltpu.VMEM((GROUP, SLAB, 2 * HEAD_DIM), BF16),
            pltpu.VMEM((3 * SLAB, 2 * HEAD_DIM), BF16),
            pltpu.VMEM((3 * SLAB, HEAD_DIM), BF16),
            pltpu.VMEM((HEAD_DIM, 3 * SLAB), BF16),
            pltpu.VMEM((HEAD_DIM, 3 * SLAB), BF16),
            pltpu.VMEM((3 * SLAB, HEAD_DIM), F32),
            pltpu.VMEM((3 * SLAB, HEAD_DIM), F32),
            pltpu.VMEM((QBLK, QBLK), F32),
            pltpu.VMEM((2, WINDOW, QBLK), F32),
            pltpu.VMEM((2, WINDOW, QBLK), F32),
            pltpu.VMEM((3 * SLAB, HEAD_DIM), F32),
            pltpu.VMEM((3 * SLAB, HEAD_DIM), F32),
            pltpu.VMEM((SLAB, PART), BF16),
            pltpu.VMEM((SLAB, PART), BF16),
            pltpu.VMEM((SLAB, BACK), BF16),
            pltpu.SemaphoreType.DMA((10,)),
        ],
        compiler_params=pltpu.CompilerParams(vmem_limit_bytes=60 * MIB),
        cost_estimate=pl.CostEstimate(flops=8 * 10**9, bytes_accessed=8 * MIB, transcendentals=5 * 10**6),
    )(col_arr, recv, *ups, q_bias, k_bias, v_bias, cos_table, sin_table)


def per_device(q_load, k_load, v_load, q_bias, k_bias, v_bias, place, segment, d_context):
    col = lax.axis_index("col")
    row = lax.axis_index("row")
    j = col % 4
    col_arr = col.reshape(1).astype(jnp.int32)
    smem = pl.BlockSpec(memory_space=pltpu.SMEM)

    packed = pl.pallas_call(
        pack_kernel,
        out_shape=shape((8, KV_HEADS, 16, SENT), BF16),
        in_specs=[any_spec()] * 5,
        out_specs=any_spec(),
        scratch_shapes=[
            pltpu.VMEM((TOK, Q_WIDTH), BF16),
            pltpu.VMEM((TOK, KV_WIDTH), BF16),
            pltpu.VMEM((TOK, KV_WIDTH), BF16),
            pltpu.VMEM((1, TOK), jnp.int32),
            pltpu.VMEM((1, TOK), jnp.int32),
            pltpu.VMEM((8, KV_HEADS, 16, SENT), BF16),
            pltpu.SemaphoreType.DMA((12,)),
        ],
        compiler_params=pltpu.CompilerParams(vmem_limit_bytes=60 * MIB),
        cost_estimate=pl.CostEstimate(flops=2 * 128 * 128 * 5120, bytes_accessed=5 * MIB, transcendentals=0),
    )(q_load[0], k_load[0], v_load[0], place, segment)
    recv = lax.all_to_all(
        packed.reshape(32, 16, SENT), "col", split_axis=0, concat_axis=0, tiled=True
    )

    up_own = d_context[0]
    ups = []
    for s in range(4):
        piece = lax.dynamic_slice_in_dim(up_own, PART * (j ^ s), PART, 1)
        ups.append(piece if s == 0 else swap(piece, "col", s, 32))
    attended = attend(
        col_arr, recv.reshape(SLAB, SENT), ups,
        q_bias.reshape(1, Q_WIDTH), k_bias.reshape(1, KV_WIDTH), v_bias.reshape(1, KV_WIDTH),
    )
    ctx_parts, back, bias = attended[:4], attended[4], attended[5]
    returned = lax.all_to_all(
        back.reshape(32, 16, BACK), "col", split_axis=0, concat_axis=0, tiled=True
    )
    ctx_in = [ctx_parts[0], swap(ctx_parts[1], "col", 1, 32)]
    ctx_in += [swap(ctx_parts[2], "col", 2, 32), swap(ctx_parts[3], "col", 3, 32)]
    for step in (2, 4):
        bias = bias + swap(bias, "row", step, 8)
    bias, ctx_in[2], ctx_in[3] = lax.optimization_barrier((bias, ctx_in[2], ctx_in[3]))
    context = pl.pallas_call(
        join_kernel,
        out_shape=shape((TOK, Q_WIDTH), BF16),
        in_specs=[smem] + [vmem_spec()] * 4,
        out_specs=vmem_spec(),
        compiler_params=pltpu.CompilerParams(vmem_limit_bytes=16 * MIB),
        cost_estimate=pl.CostEstimate(flops=0, bytes_accessed=2 * MIB, transcendentals=0),
    )(col_arr, *ctx_in)
    bias = bias + swap(bias, "row", 1, 8)
    bias = jnp.where(j == row // 2, bias, 0.0)
    for step in (1, 2):
        bias = bias + swap(bias, "col", step, 32)
    bias = bias + (swap(bias, "col", 8, 32) + swap(bias, "col", 16, 32) + swap(bias, "col", 24, 32))
    other = swap(bias, "col", 4, 32)
    bias_q, bias_kv = pl.pallas_call(
        finish_kernel,
        out_shape=[shape((1, 16), F32), shape((2, 2), F32)],
        in_specs=[smem, vmem_spec(), vmem_spec()],
        out_specs=[vmem_spec()] * 2,
        compiler_params=pltpu.CompilerParams(vmem_limit_bytes=8 * MIB),
        cost_estimate=pl.CostEstimate(flops=0, bytes_accessed=32768, transcendentals=0),
    )(jnp.stack([col, row]).astype(jnp.int32), bias, other)
    bias_q = bias_q.reshape(16)

    grad_q, grad_k, grad_v = pl.pallas_call(
        unpack_kernel,
        out_shape=[shape((TOK, Q_WIDTH), BF16), shape((TOK, KV_WIDTH), BF16), shape((TOK, KV_WIDTH), BF16)],
        in_specs=[vmem_spec()] * 2,
        out_specs=[vmem_spec()] * 3,
        scratch_shapes=[
            pltpu.VMEM((TOK, PART), BF16),
            pltpu.VMEM((TOK, KV_WIDTH), BF16),
            pltpu.VMEM((TOK, KV_WIDTH), BF16),
        ],
        compiler_params=pltpu.CompilerParams(vmem_limit_bytes=24 * MIB),
        cost_estimate=pl.CostEstimate(flops=2 * 128 * 128 * 5120, bytes_accessed=4 * MIB, transcendentals=0),
    )(returned, place)
    return (context[None], grad_q[None], grad_k[None], grad_v[None], bias_q, bias_kv)


def solution(mesh):
    return jax.shard_map(
        per_device,
        mesh=mesh,
        in_specs=(
            P("row", "col", None),
            P("row", "col", None),
            P("row", "col", None),
            P(),
            P(),
            P(),
            P("row", "col"),
            P("row", "col"),
            P("row", "col", None),
        ),
        out_specs=(
            P("row", "col", None),
            P("row", "col", None),
            P("row", "col", None),
            P("row", "col", None),
            P(("row", "col")),
            P(None, ("row", "col")),
        ),
        check_vma=False,
    )
```

time: 189 us -> 157 us (0.83); the launches traced: 187 us -> 157 us
  waiting for transfers between devices: 95.5 us -> 76.5 us
  local copies, waits for them, and re-layouts: 7.72 us -> 2.13 us
  Pallas kernels: 41.3 us -> 36.4 us
    ppermute x14 -> x15, waiting for transfers between devices: 74.2 us -> 55.9 us  [swap(): return lax.ppermute(values, axis, [(c, c ^ step) for c in range(size)])]
    pallas_call x2 -> x3, Pallas kernels: 38.7 us -> 33.8 us  [the longest x1 29.5 us: attend(): pl.pallas_call(attend_kernel, out_shape=[shape((TOK, PART), BF16)] * 4 +...]
    unnamed x32 -> x22, local copies, waits for them, and re-layouts: 5.68 us -> 1.33 us
    ppermute x14 -> x15, starting transfers between devices: 20.1 us -> 19.5 us  [swap(): return lax.ppermute(values, axis, [(c, c ^ step) for c in range(size)])]
  transfers between devices with their start and end apart: 16 -> 17, of which waited for: 12 -> 12; matrix products, arithmetic and copies ran while one was open for 3% -> 3% of each run, Pallas kernels for 1% -> 1%
where the time goes in v2:
time: 157 us
  waiting for transfers between devices  76.5 us (49%)
  starting transfers between devices  37.3 us (24%)
  Pallas kernels  36.4 us (23%)
  other arithmetic  3.94 us (3%)
  local copies, waits for them, and re-layouts  2.13 us (1%)
    ppermute x15, waiting for transfers between devices, swap(): return lax.ppermute(values, axis, [(c, c ^ step) for c in range(size)])  55.9 us
    pallas_call x1, Pallas kernels, attend(): pl.pallas_call(attend_kernel, out_shape=[shape((TOK, PART), BF16)] * 4 +...  29.5 us
    all_to_all x1, waiting for transfers between devices, per_device(): lax.all_to_all(packed.reshape(32, 16, SENT), 'col', split_axis=0, concat_...  20.7 us
    ppermute x15, starting transfers between devices, swap(): return lax.ppermute(values, axis, [(c, c ^ step) for c in range(size)])  19.5 us
    all_to_all x1, starting transfers between devices, per_device(): lax.all_to_all(packed.reshape(32, 16, SENT), 'col', split_axis=0, concat_...  11.5 us
    all_to_all x1, starting transfers between devices, per_device(): lax.all_to_all(back.reshape(32, 16, BACK), 'col', split_axis=0, concat_ax...  6.27 us
  transfers between devices with their start and end apart: 17, of which 12 were waited for; matrix products, arithmetic and copies ran while one was open for 3% of the time, Pallas kernels for 1%

profile of v2, /device:TPU:16, one launch (start us, length us, event | category | flops | bytes accessed | tf_op | source)
XLA Modules:
  0.0 157.1 jit_solution(15343403833290642578)
XLA Ops:
  0.6 3.0 %shard_map.136 = bf16[8,4,16,1920]{3,2,1,0:T(8,128)(2,1)} custom-call(bf16[128,4096]{1,0:T(8,128)(2,1)} %bitcast.28, bf16[128,512]{1,0:T(8,128)(2,1)} %bitcast.29, bf16[128,512]{1,0:T(8,128)(2,1)} %bitcast.30, s32[1,128]{1,0:T(1,128)} %place_ref.1, s32[1,128]{1,0:T(1,128)} %seg_hbm.1), custom_call_target="tpu_custom_call" | custom-call | flops 167772160 | bytes 5242880 | tf_op jit(solution)/shard_map/pallas_call | solution.py:409
  3.7 11.5 %all-to-all-start = ((bf16[32,16,1920]{2,1,0:T(8,128)(2,1)}), bf16[32,16,1920]{2,1,0:T(8,128)(2,1)S(1)}, u32[]{:S(2)}, u32[]{:S(2)}) async-start(bf16[32,16,1920]{2,1,0:T(8,128)(2,1)} %bitcast.24), calls=%async_computation | async-start | bytes 3932160 | tf_op jit(solution)/shard_map/all_to_all | solution.py:426
  15.2 0.8 dynamic-slice_bitcast_fusion
  16.0 3.0 %collective-permute-start.2 = (bf16[128,1024]{1,0:T(8,128)(2,1)S(1)}, bf16[128,1024]{1,0:T(8,128)(2,1)S(1)}, u32[]{:S(2)}, u32[]{:S(2)}) collective-permute-start(bf16[128,1024]{1,0:T(8,128)(2,1)S(1)} %get-tuple-element.34), channel_id=1, source_target_pairs={{0,3},{1,2},{2,1},{3,0},{4,7},{5,6},{6,5},{7,4},{8,11},{9,10},{10,... | collective-permute-start | bytes 786440 | tf_op jit(solution)/shard_map/ppermute | solution.py:348
  19.0 0.4 collective-permute-start
  19.7 2.4 %fusion = (f32[1280,64]{1,0:T(8,128)S(1)}, f32[1280,64]{1,0:T(8,128)S(1)}, f32[1280,64]{1,0:T(8,128)S(1)}) fusion(f32[64]{0:T(128)S(1)} %negate_power_fusion, f32[1280]{0:T(1024)S(1)} %add_convert_fusion), kind=kLoop, calls=%fused_computation.8 | loop fusion | flops 163840 | bytes 988416 | tf_op jit(solution)/shard_map/neg | solution.py:360
  22.0 1.5 pad_maximum_fusion
  23.5 8.6 %collective-permute-done.2.up3 = bf16[128,1024]{1,0:T(8,128)(2,1)S(1)} collective-permute-done((bf16[128,1024]{1,0:T(8,128)(2,1)S(1)}, bf16[128,1024]{1,0:T(8,128)(2,1)S(1)}, u32[]{:S(2)}, u32[]{:S(2)}) %collective-permute-start.2) | collective-permute-done | bytes 262176 | tf_op jit(solution)/shard_map/ppermute | solution.py:348
  32.1 9.9 %collective-permute-done.1.up2 = bf16[128,1024]{1,0:T(8,128)(2,1)S(1)} collective-permute-done((bf16[128,1024]{1,0:T(8,128)(2,1)S(1)}, bf16[128,1024]{1,0:T(8,128)(2,1)S(1)}, u32[]{:S(2)}, u32[]{:S(2)}) %collective-permute-start.1) | collective-permute-done | bytes 262176 | tf_op jit(solution)/shard_map/ppermute | solution.py:348
  42.1 20.7 %all-to-all-done = bf16[32,16,1920]{2,1,0:T(8,128)(2,1)S(1)} async-done(((bf16[32,16,1920]{2,1,0:T(8,128)(2,1)}), bf16[32,16,1920]{2,1,0:T(8,128)(2,1)S(1)}, u32[]{:S(2)}, u32[]{:S(2)}) %all-to-all-start) | async-done | bytes 1966112 | tf_op jit(solution)/shard_map/all_to_all | solution.py:426
  62.8 1.3 copy-done.2
  64.0 29.5 %shard_map.137 = (bf16[128,1024]{1,0:T(8,128)(2,1)}, bf16[128,1024]{1,0:T(8,128)(2,1)}, bf16[128,1024]{1,0:T(8,128)(2,1)}, bf16[128,1024]{1,0:T(8,128)(2,1)}, bf...) custom-call(s32[1]{0:T(128)} %bitcast.col_ref, bf16[512,1920]{1,0:T(8,128)(2,1)} %bitcast.25, ...), custom_call_target="tpu_custom_call" | custom-call | flops 8000000000 | bytes 8388608 | tf_op jit(solution)/shard_map/pallas_call | solution.py:366
  93.6 6.3 %all-to-all-start.1 = ((bf16[32,16,1792]{2,1,0:T(8,128)(2,1)}), bf16[32,16,1792]{2,1,0:T(8,128)(2,1)S(1)}, u32[]{:S(2)}, u32[]{:S(2)}) async-start(bf16[32,16,1792]{2,1,0:T(8,128)(2,1)} %bitcast.26), calls=%async_computation.1 | async-start | bytes 3670016 | tf_op jit(solution)/shard_map/all_to_all | solution.py:440
  99.9 3.4 %collective-permute-start.6 = (bf16[128,1024]{1,0:T(8,128)(2,1)S(1)}, bf16[128,1024]{1,0:T(8,128)(2,1)S(1)}, u32[]{:S(2)}, u32[]{:S(2)}) collective-permute-start(bf16[128,1024]{1,0:T(8,128)(2,1)S(1)} %copy-done.10), channel_id=1, source_target_pairs={{0,2},{1,3},{2,0},{3,1},{4,6},{5,7},{6,4},{7,5},{8,10},{9,11},{10,... | collective-permute-start | bytes 786440 | tf_op jit(solution)/shard_map/ppermute | solution.py:348
  103.3 1.4 collective-permute-start.4
  104.7 2.4 %collective-permute-done.4 = f32[16,128]{1,0:T(8,128)S(1)} collective-permute-done((f32[16,128]{1,0:T(8,128)S(1)}, f32[16,128]{1,0:T(8,128)S(1)}, u32[]{:S(2)}, u32[]{:S(2)}) %collective-permute-start.4) | collective-permute-done | bytes 8224 | tf_op jit(solution)/shard_map/ppermute | solution.py:348
  107.4 4.9 %collective-permute-done.5 = f32[16,128]{1,0:T(8,128)S(1)} collective-permute-done((f32[16,128]{1,0:T(8,128)S(1)}, f32[16,128]{1,0:T(8,128)S(1)}, u32[]{:S(2)}, u32[]{:S(2)}) %collective-permute-start.5) | collective-permute-done | bytes 8224 | tf_op jit(solution)/shard_map/ppermute | solution.py:348
  112.2 8.5 %collective-permute-done.6.c2 = bf16[128,1024]{1,0:T(8,128)(2,1)S(1)} collective-permute-done((bf16[128,1024]{1,0:T(8,128)(2,1)S(1)}, bf16[128,1024]{1,0:T(8,128)(2,1)S(1)}, u32[]{:S(2)}, u32[]{:S(2)}) %collective-permute-start.6) | collective-permute-done | bytes 262176 | tf_op jit(solution)/shard_map/ppermute | solution.py:348
  120.7 4.9 %collective-permute-done.7.c3 = bf16[128,1024]{1,0:T(8,128)(2,1)S(1)} collective-permute-done((bf16[128,1024]{1,0:T(8,128)(2,1)S(1)}, bf16[128,1024]{1,0:T(8,128)(2,1)S(1)}, u32[]{:S(2)}, u32[]{:S(2)}) %collective-permute-start.7) | collective-permute-done | bytes 262176 | tf_op jit(solution)/shard_map/ppermute | solution.py:348
  125.7 0.6 collective-permute-start.8
  126.2 3.5 %collective-permute-done.8 = f32[16,128]{1,0:T(8,128)S(1)} collective-permute-done((f32[16,128]{1,0:T(8,128)S(1)}, f32[16,128]{1,0:T(8,128)S(1)}, u32[]{:S(2)}, u32[]{:S(2)}) %collective-permute-start.8) | collective-permute-done | bytes 8224 | tf_op jit(solution)/shard_map/ppermute | solution.py:348
  129.8 1.2 collective-permute-done.9
  130.9 1.0 collective-permute-start.10
  132.0 4.2 %collective-permute-done.10 = f32[16,128]{1,0:T(8,128)S(1)} collective-permute-done((f32[16,128]{1,0:T(8,128)S(1)}, f32[16,128]{1,0:T(8,128)S(1)}, u32[]{:S(2)}, u32[]{:S(2)}) %collective-permute-start.10) | collective-permute-done | bytes 8224 | tf_op jit(solution)/shard_map/ppermute | solution.py:348
  136.2 6.8 %collective-permute-start.13 = (f32[16,128]{1,0:T(8,128)S(1)}, f32[16,128]{1,0:T(8,128)S(1)}, u32[]{:S(2)}, u32[]{:S(2)}) collective-permute-start(f32[16,128]{1,0:T(8,128)S(1)} %add.68), channel_id=1, source_target_pairs={{0,24},{1,25},{2,26},{3,27},{4,28},{5,29},{6,30},{7,31},{8,16},{9,... | collective-permute-start | bytes 24584 | tf_op jit(solution)/shard_map/ppermute | solution.py:348
  142.9 1.2 collective-permute-start.12
  144.2 1.1 collective-permute-start.11
  145.3 5.2 %collective-permute-done.12 = f32[16,128]{1,0:T(8,128)S(1)} collective-permute-done((f32[16,128]{1,0:T(8,128)S(1)}, f32[16,128]{1,0:T(8,128)S(1)}, u32[]{:S(2)}, u32[]{:S(2)}) %collective-permute-start.12) | collective-permute-done | bytes 8224 | tf_op jit(solution)/shard_map/ppermute | solution.py:348
  150.7 1.0 shard_map.138
  151.8 2.5 %collective-permute-done.14.other_ref = f32[16,128]{1,0:T(8,128)S(1)} collective-permute-done((f32[16,128]{1,0:T(8,128)S(1)}, f32[16,128]{1,0:T(8,128)S(1)}, u32[]{:S(2)}, u32[]{:S(2)}) %collective-permute-start.14) | collective-permute-done | bytes 8224 | tf_op jit(solution)/shard_map/ppermute | solution.py:348
  154.3 1.2 shard_map.140
  155.5 1.6 %shard_map.139 = (bf16[128,4096]{1,0:T(8,128)(2,1)}, bf16[128,512]{1,0:T(8,128)(2,1)}, bf16[128,512]{1,0:T(8,128)(2,1)}) custom-call(bf16[32,16,1792]{2,1,0:T(8,128)(2,1)S(1)} %all-to-all-done.1.back_ref, s32[1,128]{1,0:T(1,128)S(1)} %copy-done.1), custom_call_target="tpu_custom_call" | custom-call | flops 167772160 | bytes 4194304 | tf_op jit(solution)/shard_map/pallas_call | solution.py:472
  (41 shorter events, 0.8 us)
Async XLA Ops:
  3.7 11.5 %copy-start.3 = (bf16[1,128,4096]{2,1,0:T(8,128)(2,1)S(1)}, bf16[1,128,4096]{2,1,0:T(8,128)(2,1)}, u32[]{:S(2)}) copy-start(bf16[1,128,4096]{2,1,0:T(8,128)(2,1)} %param.17) | copy-start | bytes 3145732
  3.7 59.1 %all-to-all-start = ((bf16[32,16,1920]{2,1,0:T(8,128)(2,1)}), bf16[32,16,1920]{2,1,0:T(8,128)(2,1)S(1)}, u32[]{:S(2)}, u32[]{:S(2)}) async-start(bf16[32,16,1920]{2,1,0:T(8,128)(2,1)} %bitcast.24), calls=%async_computation | async-start | bytes 3932160 | tf_op jit(solution)/shard_map/all_to_all | solution.py:426
  16.0 16.1 %collective-permute-start.2 = (bf16[128,1024]{1,0:T(8,128)(2,1)S(1)}, bf16[128,1024]{1,0:T(8,128)(2,1)S(1)}, u32[]{:S(2)}, u32[]{:S(2)}) collective-permute-start(bf16[128,1024]{1,0:T(8,128)(2,1)S(1)} %get-tuple-element.34), channel_id=1, source_target_pairs={{0,3},{1,2},{2,1},{3,0},{4,7},{5,6},{6,5},{7,4},{8,11},{9,10},{10,... | collective-permute-start | bytes 786440 | tf_op jit(solution)/shard_map/ppermute | solution.py:348
  19.0 13.1 %collective-permute-start = (bf16[128,1024]{1,0:T(8,128)(2,1)S(1)}, bf16[128,1024]{1,0:T(8,128)(2,1)S(1)}, u32[]{:S(2)}, u32[]{:S(2)}) collective-permute-start(bf16[128,1024]{1,0:T(8,128)(2,1)S(1)} %get-tuple-element.35), channel_id=1, source_target_pairs={{0,1},{1,0},{2,3},{3,2},{4,5},{5,4},{6,7},{7,6},{8,9},{9,8},{10,11... | collective-permute-start | bytes 786440 | tf_op jit(solution)/shard_map/ppermute | solution.py:348
  19.4 22.7 %collective-permute-start.1 = (bf16[128,1024]{1,0:T(8,128)(2,1)S(1)}, bf16[128,1024]{1,0:T(8,128)(2,1)S(1)}, u32[]{:S(2)}, u32[]{:S(2)}) collective-permute-start(bf16[128,1024]{1,0:T(8,128)(2,1)S(1)} %get-tuple-element.37), channel_id=1, source_target_pairs={{0,2},{1,3},{2,0},{3,1},{4,6},{5,7},{6,4},{7,5},{8,10},{9,11},{10,... | collective-permute-start | bytes 786440 | tf_op jit(solution)/shard_map/ppermute | solution.py:348
  32.1 30.6 %copy-start.6 = (bf16[128,1024]{1,0:T(8,128)(2,1)}, bf16[128,1024]{1,0:T(8,128)(2,1)S(1)}, u32[]{:S(2)}) copy-start(bf16[128,1024]{1,0:T(8,128)(2,1)S(1)} %collective-permute-done.2.up3) | copy-start | bytes 786436
  32.1 30.6 %copy-start.7 = (bf16[128,1024]{1,0:T(8,128)(2,1)}, bf16[128,1024]{1,0:T(8,128)(2,1)S(1)}, u32[]{:S(2)}) copy-start(bf16[128,1024]{1,0:T(8,128)(2,1)S(1)} %collective-permute-done.up1) | copy-start | bytes 786436
  42.1 20.7 %copy-start.9 = (bf16[128,1024]{1,0:T(8,128)(2,1)}, bf16[128,1024]{1,0:T(8,128)(2,1)S(1)}, u32[]{:S(2)}) copy-start(bf16[128,1024]{1,0:T(8,128)(2,1)S(1)} %collective-permute-done.1.up2) | copy-start | bytes 786436
  62.8 1.3 copy-start.2
  93.6 6.3 %copy-start.10 = (bf16[128,1024]{1,0:T(8,128)(2,1)S(1)}, bf16[128,1024]{1,0:T(8,128)(2,1)}, u32[]{:S(2)}) copy-start(bf16[128,1024]{1,0:T(8,128)(2,1)} %get-tuple-element.23) | copy-start | bytes 786436
  93.6 9.7 %copy-start.8 = (bf16[128,1024]{1,0:T(8,128)(2,1)S(1)}, bf16[128,1024]{1,0:T(8,128)(2,1)}, u32[]{:S(2)}) copy-start(bf16[128,1024]{1,0:T(8,128)(2,1)} %get-tuple-element.24) | copy-start | bytes 786436
  93.6 9.7 %copy-start.4 = (f32[16,128]{1,0:T(8,128)S(1)}, f32[16,128]{1,0:T(8,128)}, u32[]{:S(2)}) copy-start(f32[16,128]{1,0:T(8,128)} %get-tuple-element.22) | copy-start | bytes 24580
  93.6 51.7 %copy-start.5 = (bf16[128,1024]{1,0:T(8,128)(2,1)S(1)}, bf16[128,1024]{1,0:T(8,128)(2,1)}, u32[]{:S(2)}) copy-start(bf16[128,1024]{1,0:T(8,128)(2,1)} %get-tuple-element.21) | copy-start | bytes 786436
  93.6 57.1 %copy-start = (bf16[128,1024]{1,0:T(8,128)(2,1)S(1)}, bf16[128,1024]{1,0:T(8,128)(2,1)}, u32[]{:S(2)}) copy-start(bf16[128,1024]{1,0:T(8,128)(2,1)} %get-tuple-element.20.c0) | copy-start | bytes 786436
  93.6 61.8 %all-to-all-start.1 = ((bf16[32,16,1792]{2,1,0:T(8,128)(2,1)}), bf16[32,16,1792]{2,1,0:T(8,128)(2,1)S(1)}, u32[]{:S(2)}, u32[]{:S(2)}) async-start(bf16[32,16,1792]{2,1,0:T(8,128)(2,1)} %bitcast.26), calls=%async_computation.1 | async-start | bytes 3670016 | tf_op jit(solution)/shard_map/all_to_all | solution.py:440
  99.9 55.6 %copy-start.1 = (s32[1,128]{1,0:T(1,128)S(1)}, s32[1,128]{1,0:T(1,128)}, u32[]{:S(2)}) copy-start(s32[1,128]{1,0:T(1,128)} %place_ref.1) | copy-start | bytes 1540
  99.9 20.8 %collective-permute-start.6 = (bf16[128,1024]{1,0:T(8,128)(2,1)S(1)}, bf16[128,1024]{1,0:T(8,128)(2,1)S(1)}, u32[]{:S(2)}, u32[]{:S(2)}) collective-permute-start(bf16[128,1024]{1,0:T(8,128)(2,1)S(1)} %copy-done.10), channel_id=1, source_target_pairs={{0,2},{1,3},{2,0},{3,1},{4,6},{5,7},{6,4},{7,5},{8,10},{9,11},{10,... | collective-permute-start | bytes 786440 | tf_op jit(solution)/shard_map/ppermute | solution.py:348
  103.3 22.3 %collective-permute-start.7 = (bf16[128,1024]{1,0:T(8,128)(2,1)S(1)}, bf16[128,1024]{1,0:T(8,128)(2,1)S(1)}, u32[]{:S(2)}, u32[]{:S(2)}) collective-permute-start(bf16[128,1024]{1,0:T(8,128)(2,1)S(1)} %copy-done.8), channel_id=1, source_target_pairs={{0,3},{1,2},{2,1},{3,0},{4,7},{5,6},{6,5},{7,4},{8,11},{9,10},{10,... | collective-permute-start | bytes 786440 | tf_op jit(solution)/shard_map/ppermute | solution.py:348
  103.3 3.7 %collective-permute-start.4 = (f32[16,128]{1,0:T(8,128)S(1)}, f32[16,128]{1,0:T(8,128)S(1)}, u32[]{:S(2)}, u32[]{:S(2)}) collective-permute-start(f32[16,128]{1,0:T(8,128)S(1)} %copy-done.4), channel_id=1, source_target_pairs={{0,64},{32,96},{64,0},{96,32},{128,192},{160,224},{192,128},{224,1... | collective-permute-start | bytes 24584 | tf_op jit(solution)/shard_map/ppermute | solution.py:348
  107.1 5.2 %collective-permute-start.5 = (f32[16,128]{1,0:T(8,128)S(1)}, f32[16,128]{1,0:T(8,128)S(1)}, u32[]{:S(2)}, u32[]{:S(2)}) collective-permute-start(f32[16,128]{1,0:T(8,128)S(1)} %add.64), channel_id=1, source_target_pairs={{0,128},{32,160},{64,192},{96,224},{128,0},{160,32},{192,64},{224,... | collective-permute-start | bytes 24584 | tf_op jit(solution)/shard_map/ppermute | solution.py:348
  125.7 4.1 %collective-permute-start.8 = (f32[16,128]{1,0:T(8,128)S(1)}, f32[16,128]{1,0:T(8,128)S(1)}, u32[]{:S(2)}, u32[]{:S(2)}) collective-permute-start(f32[16,128]{1,0:T(8,128)S(1)} %add.65), channel_id=1, source_target_pairs={{0,32},{32,0},{64,96},{96,64},{128,160},{160,128},{192,224},{224,1... | collective-permute-start | bytes 24584 | tf_op jit(solution)/shard_map/ppermute | solution.py:348
  129.8 1.2 collective-permute-start.9
  130.9 5.2 %collective-permute-start.10 = (f32[16,128]{1,0:T(8,128)S(1)}, f32[16,128]{1,0:T(8,128)S(1)}, u32[]{:S(2)}, u32[]{:S(2)}) collective-permute-start(f32[16,128]{1,0:T(8,128)S(1)} %add.67), channel_id=1, source_target_pairs={{0,2},{1,3},{2,0},{3,1},{4,6},{5,7},{6,4},{7,5},{8,10},{9,11},{10,... | collective-permute-start | bytes 24584 | tf_op jit(solution)/shard_map/ppermute | solution.py:348
  136.2 9.1 %collective-permute-start.13 = (f32[16,128]{1,0:T(8,128)S(1)}, f32[16,128]{1,0:T(8,128)S(1)}, u32[]{:S(2)}, u32[]{:S(2)}) collective-permute-start(f32[16,128]{1,0:T(8,128)S(1)} %add.68), channel_id=1, source_target_pairs={{0,24},{1,25},{2,26},{3,27},{4,28},{5,29},{6,30},{7,31},{8,16},{9,... | collective-permute-start | bytes 24584 | tf_op jit(solution)/shard_map/ppermute | solution.py:348
  142.9 7.6 %collective-permute-start.12 = (f32[16,128]{1,0:T(8,128)S(1)}, f32[16,128]{1,0:T(8,128)S(1)}, u32[]{:S(2)}, u32[]{:S(2)}) collective-permute-start(f32[16,128]{1,0:T(8,128)S(1)} %add.68), channel_id=1, source_target_pairs={{0,16},{1,17},{2,18},{3,19},{4,20},{5,21},{6,22},{7,23},{8,24},{9,... | collective-permute-start | bytes 24584 | tf_op jit(solution)/shard_map/ppermute | solution.py:348
  144.2 6.4 %collective-permute-start.11 = (f32[16,128]{1,0:T(8,128)S(1)}, f32[16,128]{1,0:T(8,128)S(1)}, u32[]{:S(2)}, u32[]{:S(2)}) collective-permute-start(f32[16,128]{1,0:T(8,128)S(1)} %add.68), channel_id=1, source_target_pairs={{0,8},{1,9},{2,10},{3,11},{4,12},{5,13},{6,14},{7,15},{8,0},{9,1},... | collective-permute-start | bytes 24584 | tf_op jit(solution)/shard_map/ppermute | solution.py:348
  145.3 5.4 %collective-permute-start.3 = (bf16[128,1024]{1,0:T(8,128)(2,1)S(1)}, bf16[128,1024]{1,0:T(8,128)(2,1)S(1)}, u32[]{:S(2)}, u32[]{:S(2)}) collective-permute-start(bf16[128,1024]{1,0:T(8,128)(2,1)S(1)} %copy-done.5), channel_id=1, source_target_pairs={{0,1},{1,0},{2,3},{3,2},{4,5},{5,4},{6,7},{7,6},{8,9},{9,8},{10,11... | collective-permute-start | bytes 786440 | tf_op jit(solution)/shard_map/ppermute | solution.py:348
  150.5 3.7 %collective-permute-start.14 = (f32[16,128]{1,0:T(8,128)S(1)}, f32[16,128]{1,0:T(8,128)S(1)}, u32[]{:S(2)}, u32[]{:S(2)}) collective-permute-start(f32[16,128]{1,0:T(8,128)S(1)} %add_add_fusion.mine_ref), channel_id=1, source_target_pairs={{0,4},{1,5},{2,6},{3,7},{4,0},{5,1},{6,2},{7,3},{8,12},{9,13},{10,... | collective-permute-start | bytes 24584 | tf_op jit(solution)/shard_map/ppermute | solution.py:348

commit v3 on v2

--- a/solution.py
+++ b/solution.py
@@ -148,7 +148,7 @@
     cos_s[...] = jnp.zeros_like(cos_s)
     sin_s[...] = jnp.zeros_like(sin_s)
     mask_s[...] = jnp.where(iota((QBLK, QBLK), 0) <= iota((QBLK, QBLK), 1), 0.0, MASKED)
-    for copy in copies:
+    for copy in copies[:6]:
         copy.wait()
 
     meta = recv_s[:, BACK:SENT].astype(F32)
@@ -202,11 +202,15 @@
                     q_s[2 * pair + u, :, 0:HEAD_DIM] = turn(one, cos_s[rows, :], sin_s[rows, :]).astype(BF16)
                     q_s[2 * pair + u, :, HEAD_DIM:] = other
 
-    def one_head(h, _):
+    for copy in copies[6:]:
+        copy.wait()
+
+    def one_head(h, spans):
         lanes = pl.ds(pl.multiple_of(h * HEAD_DIM, HEAD_DIM), HEAD_DIM)
         blocks = range(2)
         q_rows = [slice(QBLK * i, QBLK * (i + 1)) for i in blocks]
-        k_rows = [slice(QBLK * i, QBLK * i + WINDOW) for i in blocks]
+        k_rows = [slice(begin, begin + size) for begin, size in spans]
+        size = [span[1] for span in spans]
         query = [q_s[h, q_rows[i], 0:HEAD_DIM] for i in blocks]
         up = [up_s[q_rows[i], lanes] for i in blocks]
         up_t = [jnp.transpose(up[i].astype(F32)) for i in blocks]
@@ -215,30 +219,30 @@
         out_low = [None, None]
         dq_t = [None, None]
         for i in blocks:
+            edge = size[i] - QBLK
             score = dot(k_s[k_rows[i], :], q_s[h, q_rows[i], :], NT)
-            s_s[i, 0 : WINDOW - QBLK, :] = score[: WINDOW - QBLK]
-            last = score[WINDOW - QBLK :] + mask_s[...]
-            s_s[i, WINDOW - QBLK :, :] = last
+            s_s[i, 0:edge, :] = score[:edge]
+            last = score[edge:] + mask_s[...]
+            s_s[i, edge : size[i], :] = last
             top[i] = jnp.maximum(
-                jnp.max(score[: WINDOW - QBLK], axis=0, keepdims=True), jnp.max(last, axis=0, keepdims=True)
+                jnp.max(score[:edge], axis=0, keepdims=True), jnp.max(last, axis=0, keepdims=True)
             )
         for i in blocks:
-            p_s[i] = dot(v_s[k_rows[i], :], up[i], NT)
+            p_s[i, 0 : size[i], :] = dot(v_s[k_rows[i], :], up[i], NT)
         for i in blocks:
-            weight = jnp.exp2((s_s[i] - top[i]) * (scale * LOG2E))
-            s_s[i] = weight
+            weight = jnp.exp2((s_s[i, 0 : size[i], :] - top[i]) * (scale * LOG2E))
+            s_s[i, 0 : size[i], :] = weight
             invert[i] = 1.0 / jnp.sum(weight, axis=0, keepdims=True)
         for i in blocks:
-            prob = s_s[i] * invert[i]
-            s_s[i] = prob
-            prob_low = prob.astype(BF16)
+            prob_low = (s_s[i, 0 : size[i], :] * invert[i]).astype(BF16)
             out_t = dot(vt_s[:, k_rows[i]], prob_low)
             dv_s[k_rows[i], :] += dot(prob_low, up[i])
             out_low[i] = out_t.astype(BF16).astype(F32)
         for i in blocks:
             ctx_s[q_rows[i], lanes] = jnp.transpose(out_low[i]).astype(BF16)
             delta = jnp.sum(up_t[i] * out_low[i], axis=0, keepdims=True)
-            dscore = (s_s[i] * (p_s[i] - delta)).astype(BF16)
+            prob = s_s[i, 0 : size[i], :] * invert[i]
+            dscore = (prob * (p_s[i, 0 : size[i], :] - delta)).astype(BF16)
             dq_t[i] = dot(kt_s[:, k_rows[i]], dscore)
             dk_s[k_rows[i], :] += dot(dscore, query[i])
         total = None
@@ -250,9 +254,27 @@
             mine = jnp.sum(dq, axis=0, keepdims=True)
             total = mine if total is None else total + mine
         bias_ref[pl.ds(h, 1), :] = total
-        return 0
-
-    lax.fori_loop(0, GROUP, one_head, 0, unroll=2)
+
+    def all_heads(spans):
+        def step(h, _):
+            one_head(h, spans)
+            return 0
+
+        lax.fori_loop(0, GROUP, step, 0, unroll=2)
+
+    middle = SLAB * z + QBLK
+    begin = jnp.int32(0)
+    for v in range(1, SEGS):
+        begin = jnp.where(starts[v] <= middle, starts[v], begin)
+    far = begin < middle - (WINDOW - 2 * QBLK)
+
+    @pl.when(far)
+    def _():
+        all_heads(((QBLK, WINDOW - QBLK), (QBLK, WINDOW)))
+
+    @pl.when(jnp.logical_not(far))
+    def _():
+        all_heads(((0, WINDOW), (2 * QBLK, WINDOW - QBLK)))
 
     outs = []
     for s, ref in enumerate((ctx0, ctx1, ctx2, ctx3)):
@@ -367,7 +389,7 @@
         attend_kernel,
         out_shape=[shape((TOK, PART), BF16)] * 4
         + [shape((SLAB, BACK), BF16), shape((16, HEAD_DIM), F32)],
-        in_specs=[pl.BlockSpec(memory_space=pltpu.SMEM)] + [any_spec()] * 10,
+        in_specs=[pl.BlockSpec(memory_space=pltpu.SMEM), pl.BlockSpec(memory_space=pl.ANY)] + [any_spec()] * 9,
         out_specs=[any_spec()] * 5 + [vmem_spec()],
         scratch_shapes=[
             pltpu.VMEM((SLAB, SENT), BF16),
@@ -454,21 +476,12 @@
         cost_estimate=pl.CostEstimate(flops=0, bytes_accessed=2 * MIB, transcendentals=0),
     )(col_arr, *ctx_in)
     bias = bias + swap(bias, "row", 1, 8)
+    bias, context = lax.optimization_barrier((bias, context))
     bias = jnp.where(j == row // 2, bias, 0.0)
     for step in (1, 2):
         bias = bias + swap(bias, "col", step, 32)
     bias = bias + (swap(bias, "col", 8, 32) + swap(bias, "col", 16, 32) + swap(bias, "col", 24, 32))
     other = swap(bias, "col", 4, 32)
-    bias_q, bias_kv = pl.pallas_call(
-        finish_kernel,
-        out_shape=[shape((1, 16), F32), shape((2, 2), F32)],
-        in_specs=[smem, vmem_spec(), vmem_spec()],
-        out_specs=[vmem_spec()] * 2,
-        compiler_params=pltpu.CompilerParams(vmem_limit_bytes=8 * MIB),
-        cost_estimate=pl.CostEstimate(flops=0, bytes_accessed=32768, transcendentals=0),
-    )(jnp.stack([col, row]).astype(jnp.int32), bias, other)
-    bias_q = bias_q.reshape(16)
-
     grad_q, grad_k, grad_v = pl.pallas_call(
         unpack_kernel,
         out_shape=[shape((TOK, Q_WIDTH), BF16), shape((TOK, KV_WIDTH), BF16), shape((TOK, KV_WIDTH), BF16)],
@@ -482,6 +495,16 @@
         compiler_params=pltpu.CompilerParams(vmem_limit_bytes=24 * MIB),
         cost_estimate=pl.CostEstimate(flops=2 * 128 * 128 * 5120, bytes_accessed=4 * MIB, transcendentals=0),
     )(returned, place)
+    other, grad_v = lax.optimization_barrier((other, grad_v))
+    bias_q, bias_kv = pl.pallas_call(
+        finish_kernel,
+        out_shape=[shape((1, 16), F32), shape((2, 2), F32)],
+        in_specs=[smem, vmem_spec(), vmem_spec()],
+        out_specs=[vmem_spec()] * 2,
+        compiler_params=pltpu.CompilerParams(vmem_limit_bytes=8 * MIB),
+        cost_estimate=pl.CostEstimate(flops=0, bytes_accessed=32768, transcendentals=0),
+    )(jnp.stack([col, row]).astype(jnp.int32), bias, other)
+    bias_q = bias_q.reshape(16)
     return (context[None], grad_q[None], grad_k[None], grad_v[None], bias_q, bias_kv)
 
 

time: 157 us -> 152 us (0.968)
  Pallas kernels: 36.4 us -> 32.9 us
  waiting for transfers between devices: 76.5 us -> 74.7 us
    pallas_call x1, Pallas kernels: 29.5 us -> 26.1 us  [attend(): pl.pallas_call(attend_kernel, out_shape=[shape((TOK, PART), BF16)] * 4 +...]
    ppermute x15, waiting for transfers between devices: 55.9 us -> 54 us  [swap(): return lax.ppermute(values, axis, [(c, c ^ step) for c in range(size)])]
  transfers between devices with their start and end apart: 17 -> 17, of which waited for: 12 -> 12; matrix products, arithmetic and copies ran while one was open for 3% -> 3% of each run, Pallas kernels for 1% -> 2%
where the time goes in v3:
time: 152 us
  waiting for transfers between devices  74.7 us (49%)
  starting transfers between devices  37.5 us (25%)
  Pallas kernels  32.9 us (22%)
  other arithmetic  3.94 us (3%)
  local copies, waits for them, and re-layouts  2.12 us (1%)
    ppermute x15, waiting for transfers between devices, swap(): return lax.ppermute(values, axis, [(c, c ^ step) for c in range(size)])  54 us
    pallas_call x1, Pallas kernels, attend(): pl.pallas_call(attend_kernel, out_shape=[shape((TOK, PART), BF16)] * 4 +...  26.1 us
    all_to_all x1, waiting for transfers between devices, per_device(): lax.all_to_all(packed.reshape(32, 16, SENT), 'col', split_axis=0, concat_...  20.7 us
    ppermute x15, starting transfers between devices, swap(): return lax.ppermute(values, axis, [(c, c ^ step) for c in range(size)])  19.7 us
    all_to_all x1, starting transfers between devices, per_device(): lax.all_to_all(packed.reshape(32, 16, SENT), 'col', split_axis=0, concat_...  11.5 us
    all_to_all x1, starting transfers between devices, per_device(): lax.all_to_all(back.reshape(32, 16, BACK), 'col', split_axis=0, concat_ax...  6.27 us
  transfers between devices with their start and end apart: 17, of which 12 were waited for; matrix products, arithmetic and copies ran while one was open for 3% of the time, Pallas kernels for 2%

profile of v3, /device:TPU:16, one launch (start us, length us, event | category | flops | bytes accessed | tf_op | source)
XLA Modules:
  0.0 151.9 jit_solution(14296809771624632463)
XLA Ops:
  0.6 3.0 %shard_map.136 = bf16[8,4,16,1920]{3,2,1,0:T(8,128)(2,1)} custom-call(bf16[128,4096]{1,0:T(8,128)(2,1)} %bitcast.28, bf16[128,512]{1,0:T(8,128)(2,1)} %bitcast.29, bf16[128,512]{1,0:T(8,128)(2,1)} %bitcast.30, s32[1,128]{1,0:T(1,128)} %place_ref.1, s32[1,128]{1,0:T(1,128)} %seg_hbm.1), custom_call_target="tpu_custom_call" | custom-call | flops 167772160 | bytes 5242880 | tf_op jit(solution)/shard_map/pallas_call | solution.py:431
  3.6 11.5 %all-to-all-start = ((bf16[32,16,1920]{2,1,0:T(8,128)(2,1)}), bf16[32,16,1920]{2,1,0:T(8,128)(2,1)S(1)}, u32[]{:S(2)}, u32[]{:S(2)}) async-start(bf16[32,16,1920]{2,1,0:T(8,128)(2,1)} %bitcast.24), calls=%async_computation | async-start | bytes 3932160 | tf_op jit(solution)/shard_map/all_to_all | solution.py:448
  15.1 0.8 dynamic-slice_bitcast_fusion
  15.9 3.0 %collective-permute-start.2 = (bf16[128,1024]{1,0:T(8,128)(2,1)S(1)}, bf16[128,1024]{1,0:T(8,128)(2,1)S(1)}, u32[]{:S(2)}, u32[]{:S(2)}) collective-permute-start(bf16[128,1024]{1,0:T(8,128)(2,1)S(1)} %get-tuple-element.42), channel_id=1, source_target_pairs={{0,3},{1,2},{2,1},{3,0},{4,7},{5,6},{6,5},{7,4},{8,11},{9,10},{10,... | collective-permute-start | bytes 786440 | tf_op jit(solution)/shard_map/ppermute | solution.py:370
  19.0 0.4 collective-permute-start
  19.6 2.4 %fusion = (f32[1280,64]{1,0:T(8,128)S(1)}, f32[1280,64]{1,0:T(8,128)S(1)}, f32[1280,64]{1,0:T(8,128)S(1)}) fusion(f32[64]{0:T(128)S(1)} %negate_power_fusion, f32[1280]{0:T(1024)S(1)} %add_convert_fusion), kind=kLoop, calls=%fused_computation.8 | loop fusion | flops 163840 | bytes 988416 | tf_op jit(solution)/shard_map/neg | solution.py:382
  22.0 1.5 pad_maximum_fusion
  23.4 8.7 %collective-permute-done.2.up3 = bf16[128,1024]{1,0:T(8,128)(2,1)S(1)} collective-permute-done((bf16[128,1024]{1,0:T(8,128)(2,1)S(1)}, bf16[128,1024]{1,0:T(8,128)(2,1)S(1)}, u32[]{:S(2)}, u32[]{:S(2)}) %collective-permute-start.2) | collective-permute-done | bytes 262176 | tf_op jit(solution)/shard_map/ppermute | solution.py:370
  32.1 9.9 %collective-permute-done.1.up2 = bf16[128,1024]{1,0:T(8,128)(2,1)S(1)} collective-permute-done((bf16[128,1024]{1,0:T(8,128)(2,1)S(1)}, bf16[128,1024]{1,0:T(8,128)(2,1)S(1)}, u32[]{:S(2)}, u32[]{:S(2)}) %collective-permute-start.1) | collective-permute-done | bytes 262176 | tf_op jit(solution)/shard_map/ppermute | solution.py:370
  42.0 20.7 %all-to-all-done = bf16[32,16,1920]{2,1,0:T(8,128)(2,1)S(1)} async-done(((bf16[32,16,1920]{2,1,0:T(8,128)(2,1)}), bf16[32,16,1920]{2,1,0:T(8,128)(2,1)S(1)}, u32[]{:S(2)}, u32[]{:S(2)}) %all-to-all-start) | async-done | bytes 1966112 | tf_op jit(solution)/shard_map/all_to_all | solution.py:448
  62.7 1.3 copy-done.2
  64.0 26.1 %shard_map.137 = (bf16[128,1024]{1,0:T(8,128)(2,1)}, bf16[128,1024]{1,0:T(8,128)(2,1)}, bf16[128,1024]{1,0:T(8,128)(2,1)}, bf16[128,1024]{1,0:T(8,128)(2,1)}, bf...) custom-call(s32[1]{0:T(128)} %bitcast.col_ref, bf16[512,1920]{1,0:T(8,128)(2,1)} %bitcast.25, ...), custom_call_target="tpu_custom_call" | custom-call | flops 8000000000 | bytes 8388608 | tf_op jit(solution)/shard_map/pallas_call | solution.py:388
  90.1 6.3 %all-to-all-start.1 = ((bf16[32,16,1792]{2,1,0:T(8,128)(2,1)}), bf16[32,16,1792]{2,1,0:T(8,128)(2,1)S(1)}, u32[]{:S(2)}, u32[]{:S(2)}) async-start(bf16[32,16,1792]{2,1,0:T(8,128)(2,1)} %bitcast.26), calls=%async_computation.1 | async-start | bytes 3670016 | tf_op jit(solution)/shard_map/all_to_all | solution.py:462
  96.4 3.4 %collective-permute-start.5 = (bf16[128,1024]{1,0:T(8,128)(2,1)}, bf16[128,1024]{1,0:T(8,128)(2,1)S(1)}, u32[]{:S(2)}, u32[]{:S(2)}) collective-permute-start(bf16[128,1024]{1,0:T(8,128)(2,1)} %get-tuple-element.25), channel_id=1, source_target_pairs={{0,2},{1,3},{2,0},{3,1},{4,6},{5,7},{6,4},{7,5},{8,10},{9,11},{10,... | collective-permute-start | bytes 786440 | tf_op jit(solution)/shard_map/ppermute | solution.py:370
  100.1 1.3 collective-permute-start.3
  101.5 2.3 %collective-permute-done.3 = f32[16,128]{1,0:T(8,128)S(1)} collective-permute-done((f32[16,128]{1,0:T(8,128)S(1)}, f32[16,128]{1,0:T(8,128)S(1)}, u32[]{:S(2)}, u32[]{:S(2)}) %collective-permute-start.3) | collective-permute-done | bytes 8224 | tf_op jit(solution)/shard_map/ppermute | solution.py:370
  104.1 4.8 %collective-permute-done.4 = f32[16,128]{1,0:T(8,128)S(1)} collective-permute-done((f32[16,128]{1,0:T(8,128)S(1)}, f32[16,128]{1,0:T(8,128)S(1)}, u32[]{:S(2)}, u32[]{:S(2)}) %collective-permute-start.4) | collective-permute-done | bytes 8224 | tf_op jit(solution)/shard_map/ppermute | solution.py:370
  109.0 8.3 %collective-permute-done.5.c2 = bf16[128,1024]{1,0:T(8,128)(2,1)S(1)} collective-permute-done((bf16[128,1024]{1,0:T(8,128)(2,1)}, bf16[128,1024]{1,0:T(8,128)(2,1)S(1)}, u32[]{:S(2)}, u32[]{:S(2)}) %collective-permute-start.5) | collective-permute-done | bytes 262176 | tf_op jit(solution)/shard_map/ppermute | solution.py:370
  117.2 4.9 %collective-permute-done.6.c3 = bf16[128,1024]{1,0:T(8,128)(2,1)S(1)} collective-permute-done((bf16[128,1024]{1,0:T(8,128)(2,1)S(1)}, bf16[128,1024]{1,0:T(8,128)(2,1)S(1)}, u32[]{:S(2)}, u32[]{:S(2)}) %collective-permute-start.6) | collective-permute-done | bytes 262176 | tf_op jit(solution)/shard_map/ppermute | solution.py:370
  122.1 0.6 collective-permute-start.7
  122.7 1.0 shard_map.138
  123.8 2.5 %collective-permute-done.7 = f32[16,128]{1,0:T(8,128)S(1)} collective-permute-done((f32[16,128]{1,0:T(8,128)S(1)}, f32[16,128]{1,0:T(8,128)S(1)}, u32[]{:S(2)}, u32[]{:S(2)}) %collective-permute-start.7) | collective-permute-done | bytes 8224 | tf_op jit(solution)/shard_map/ppermute | solution.py:370
  126.3 1.2 collective-permute-done.9
  127.4 0.9 collective-permute-start.10
  128.3 4.3 %collective-permute-done.10 = f32[16,128]{1,0:T(8,128)S(1)} collective-permute-done((f32[16,128]{1,0:T(8,128)S(1)}, f32[16,128]{1,0:T(8,128)S(1)}, u32[]{:S(2)}, u32[]{:S(2)}) %collective-permute-start.10) | collective-permute-done | bytes 8224 | tf_op jit(solution)/shard_map/ppermute | solution.py:370
  132.6 6.8 %collective-permute-start.13 = (f32[16,128]{1,0:T(8,128)S(1)}, f32[16,128]{1,0:T(8,128)S(1)}, u32[]{:S(2)}, u32[]{:S(2)}) collective-permute-start(f32[16,128]{1,0:T(8,128)S(1)} %add.68), channel_id=1, source_target_pairs={{0,24},{1,25},{2,26},{3,27},{4,28},{5,29},{6,30},{7,31},{8,16},{9,... | collective-permute-start | bytes 24584 | tf_op jit(solution)/shard_map/ppermute | solution.py:370
  139.4 1.2 collective-permute-start.12
  140.6 1.1 collective-permute-start.11
  141.8 5.2 %collective-permute-done.12 = f32[16,128]{1,0:T(8,128)S(1)} collective-permute-done((f32[16,128]{1,0:T(8,128)S(1)}, f32[16,128]{1,0:T(8,128)S(1)}, u32[]{:S(2)}, u32[]{:S(2)}) %collective-permute-start.12) | collective-permute-done | bytes 8224 | tf_op jit(solution)/shard_map/ppermute | solution.py:370
  147.1 1.6 %shard_map.139 = (bf16[128,4096]{1,0:T(8,128)(2,1)}, bf16[128,512]{1,0:T(8,128)(2,1)}, bf16[128,512]{1,0:T(8,128)(2,1)}) custom-call(bf16[32,16,1792]{2,1,0:T(8,128)(2,1)S(1)} %all-to-all-done.1.back_ref, s32[1,128]{1,0:T(1,128)S(1)} %copy-done.1), custom_call_target="tpu_custom_call" | custom-call | flops 167772160 | bytes 4194304 | tf_op jit(solution)/shard_map/pallas_call | solution.py:485
  148.7 2.0 %collective-permute-done.14.other_ref = f32[16,128]{1,0:T(8,128)S(1)} collective-permute-done((f32[16,128]{1,0:T(8,128)S(1)}, f32[16,128]{1,0:T(8,128)S(1)}, u32[]{:S(2)}, u32[]{:S(2)}) %collective-permute-start.14) | collective-permute-done | bytes 8224 | tf_op jit(solution)/shard_map/ppermute | solution.py:370
  150.7 1.2 shard_map.140
  (40 shorter events, 1.2 us)
Async XLA Ops:
  3.6 11.5 %copy-start.3 = (bf16[1,128,4096]{2,1,0:T(8,128)(2,1)S(1)}, bf16[1,128,4096]{2,1,0:T(8,128)(2,1)}, u32[]{:S(2)}) copy-start(bf16[1,128,4096]{2,1,0:T(8,128)(2,1)} %param.17) | copy-start | bytes 3145732
  3.6 59.1 %all-to-all-start = ((bf16[32,16,1920]{2,1,0:T(8,128)(2,1)}), bf16[32,16,1920]{2,1,0:T(8,128)(2,1)S(1)}, u32[]{:S(2)}, u32[]{:S(2)}) async-start(bf16[32,16,1920]{2,1,0:T(8,128)(2,1)} %bitcast.24), calls=%async_computation | async-start | bytes 3932160 | tf_op jit(solution)/shard_map/all_to_all | solution.py:448
  15.9 16.1 %collective-permute-start.2 = (bf16[128,1024]{1,0:T(8,128)(2,1)S(1)}, bf16[128,1024]{1,0:T(8,128)(2,1)S(1)}, u32[]{:S(2)}, u32[]{:S(2)}) collective-permute-start(bf16[128,1024]{1,0:T(8,128)(2,1)S(1)} %get-tuple-element.42), channel_id=1, source_target_pairs={{0,3},{1,2},{2,1},{3,0},{4,7},{5,6},{6,5},{7,4},{8,11},{9,10},{10,... | collective-permute-start | bytes 786440 | tf_op jit(solution)/shard_map/ppermute | solution.py:370
  19.0 13.1 %collective-permute-start = (bf16[128,1024]{1,0:T(8,128)(2,1)S(1)}, bf16[128,1024]{1,0:T(8,128)(2,1)S(1)}, u32[]{:S(2)}, u32[]{:S(2)}) collective-permute-start(bf16[128,1024]{1,0:T(8,128)(2,1)S(1)} %get-tuple-element.43), channel_id=1, source_target_pairs={{0,1},{1,0},{2,3},{3,2},{4,5},{5,4},{6,7},{7,6},{8,9},{9,8},{10,11... | collective-permute-start | bytes 786440 | tf_op jit(solution)/shard_map/ppermute | solution.py:370
  19.4 22.7 %collective-permute-start.1 = (bf16[128,1024]{1,0:T(8,128)(2,1)S(1)}, bf16[128,1024]{1,0:T(8,128)(2,1)S(1)}, u32[]{:S(2)}, u32[]{:S(2)}) collective-permute-start(bf16[128,1024]{1,0:T(8,128)(2,1)S(1)} %get-tuple-element.45), channel_id=1, source_target_pairs={{0,2},{1,3},{2,0},{3,1},{4,6},{5,7},{6,4},{7,5},{8,10},{9,11},{10,... | collective-permute-start | bytes 786440 | tf_op jit(solution)/shard_map/ppermute | solution.py:370
  32.1 30.6 %copy-start.7 = (bf16[128,1024]{1,0:T(8,128)(2,1)}, bf16[128,1024]{1,0:T(8,128)(2,1)S(1)}, u32[]{:S(2)}) copy-start(bf16[128,1024]{1,0:T(8,128)(2,1)S(1)} %collective-permute-done.2.up3) | copy-start | bytes 786436
  32.1 30.6 %copy-start.8 = (bf16[128,1024]{1,0:T(8,128)(2,1)}, bf16[128,1024]{1,0:T(8,128)(2,1)S(1)}, u32[]{:S(2)}) copy-start(bf16[128,1024]{1,0:T(8,128)(2,1)S(1)} %collective-permute-done.up1) | copy-start | bytes 786436
  42.0 20.7 %copy-start.9 = (bf16[128,1024]{1,0:T(8,128)(2,1)}, bf16[128,1024]{1,0:T(8,128)(2,1)S(1)}, u32[]{:S(2)}) copy-start(bf16[128,1024]{1,0:T(8,128)(2,1)S(1)} %collective-permute-done.1.up2) | copy-start | bytes 786436
  62.7 1.3 copy-start.2
  90.1 9.7 %copy-start.6 = (bf16[128,1024]{1,0:T(8,128)(2,1)S(1)}, bf16[128,1024]{1,0:T(8,128)(2,1)}, u32[]{:S(2)}) copy-start(bf16[128,1024]{1,0:T(8,128)(2,1)} %get-tuple-element.26) | copy-start | bytes 786436
  90.1 9.7 %copy-start.5 = (bf16[128,1024]{1,0:T(8,128)(2,1)S(1)}, bf16[128,1024]{1,0:T(8,128)(2,1)}, u32[]{:S(2)}) copy-start(bf16[128,1024]{1,0:T(8,128)(2,1)} %get-tuple-element.29) | copy-start | bytes 786436
  90.1 10.1 %copy-start.4 = (f32[16,128]{1,0:T(8,128)S(1)}, f32[16,128]{1,0:T(8,128)}, u32[]{:S(2)}) copy-start(f32[16,128]{1,0:T(8,128)} %get-tuple-element.24) | copy-start | bytes 24580
  90.1 32.6 %copy-start = (bf16[128,1024]{1,0:T(8,128)(2,1)S(1)}, bf16[128,1024]{1,0:T(8,128)(2,1)}, u32[]{:S(2)}) copy-start(bf16[128,1024]{1,0:T(8,128)(2,1)} %get-tuple-element.28.c0) | copy-start | bytes 786436
  90.1 57.0 %all-to-all-start.1 = ((bf16[32,16,1792]{2,1,0:T(8,128)(2,1)}), bf16[32,16,1792]{2,1,0:T(8,128)(2,1)S(1)}, u32[]{:S(2)}, u32[]{:S(2)}) async-start(bf16[32,16,1792]{2,1,0:T(8,128)(2,1)} %bitcast.26), calls=%async_computation.1 | async-start | bytes 3670016 | tf_op jit(solution)/shard_map/all_to_all | solution.py:462
  96.4 50.7 %copy-start.1 = (s32[1,128]{1,0:T(1,128)S(1)}, s32[1,128]{1,0:T(1,128)}, u32[]{:S(2)}) copy-start(s32[1,128]{1,0:T(1,128)} %place_ref.1) | copy-start | bytes 1540
  96.4 20.8 %collective-permute-start.5 = (bf16[128,1024]{1,0:T(8,128)(2,1)}, bf16[128,1024]{1,0:T(8,128)(2,1)S(1)}, u32[]{:S(2)}, u32[]{:S(2)}) collective-permute-start(bf16[128,1024]{1,0:T(8,128)(2,1)} %get-tuple-element.25), channel_id=1, source_target_pairs={{0,2},{1,3},{2,0},{3,1},{4,6},{5,7},{6,4},{7,5},{8,10},{9,11},{10,... | collective-permute-start | bytes 786440 | tf_op jit(solution)/shard_map/ppermute | solution.py:370
  99.8 22.3 %collective-permute-start.6 = (bf16[128,1024]{1,0:T(8,128)(2,1)S(1)}, bf16[128,1024]{1,0:T(8,128)(2,1)S(1)}, u32[]{:S(2)}, u32[]{:S(2)}) collective-permute-start(bf16[128,1024]{1,0:T(8,128)(2,1)S(1)} %copy-done.6), channel_id=1, source_target_pairs={{0,3},{1,2},{2,1},{3,0},{4,7},{5,6},{6,5},{7,4},{8,11},{9,10},{10,... | collective-permute-start | bytes 786440 | tf_op jit(solution)/shard_map/ppermute | solution.py:370
  99.8 22.9 %collective-permute-start.8 = (bf16[128,1024]{1,0:T(8,128)(2,1)S(1)}, bf16[128,1024]{1,0:T(8,128)(2,1)S(1)}, u32[]{:S(2)}, u32[]{:S(2)}) collective-permute-start(bf16[128,1024]{1,0:T(8,128)(2,1)S(1)} %copy-done.5), channel_id=1, source_target_pairs={{0,1},{1,0},{2,3},{3,2},{4,5},{5,4},{6,7},{7,6},{8,9},{9,8},{10,11... | collective-permute-start | bytes 786440 | tf_op jit(solution)/shard_map/ppermute | solution.py:370
  100.1 3.7 %collective-permute-start.3 = (f32[16,128]{1,0:T(8,128)S(1)}, f32[16,128]{1,0:T(8,128)S(1)}, u32[]{:S(2)}, u32[]{:S(2)}) collective-permute-start(f32[16,128]{1,0:T(8,128)S(1)} %copy-done.4), channel_id=1, source_target_pairs={{0,64},{32,96},{64,0},{96,32},{128,192},{160,224},{192,128},{224,1... | collective-permute-start | bytes 24584 | tf_op jit(solution)/shard_map/ppermute | solution.py:370
  103.8 5.2 %collective-permute-start.4 = (f32[16,128]{1,0:T(8,128)S(1)}, f32[16,128]{1,0:T(8,128)S(1)}, u32[]{:S(2)}, u32[]{:S(2)}) collective-permute-start(f32[16,128]{1,0:T(8,128)S(1)} %add.64), channel_id=1, source_target_pairs={{0,128},{32,160},{64,192},{96,224},{128,0},{160,32},{192,64},{224,... | collective-permute-start | bytes 24584 | tf_op jit(solution)/shard_map/ppermute | solution.py:370
  122.1 4.1 %collective-permute-start.7 = (f32[16,128]{1,0:T(8,128)S(1)}, f32[16,128]{1,0:T(8,128)S(1)}, u32[]{:S(2)}, u32[]{:S(2)}) collective-permute-start(f32[16,128]{1,0:T(8,128)S(1)} %add.65), channel_id=1, source_target_pairs={{0,32},{32,0},{64,96},{96,64},{128,160},{160,128},{192,224},{224,1... | collective-permute-start | bytes 24584 | tf_op jit(solution)/shard_map/ppermute | solution.py:370
  126.2 1.2 collective-permute-start.9
  127.4 5.2 %collective-permute-start.10 = (f32[16,128]{1,0:T(8,128)S(1)}, f32[16,128]{1,0:T(8,128)S(1)}, u32[]{:S(2)}, u32[]{:S(2)}) collective-permute-start(f32[16,128]{1,0:T(8,128)S(1)} %fusion.1), channel_id=1, source_target_pairs={{0,2},{1,3},{2,0},{3,1},{4,6},{5,7},{6,4},{7,5},{8,10},{9,11},{10,... | collective-permute-start | bytes 24584 | tf_op jit(solution)/shard_map/ppermute | solution.py:370
  132.6 9.2 %collective-permute-start.13 = (f32[16,128]{1,0:T(8,128)S(1)}, f32[16,128]{1,0:T(8,128)S(1)}, u32[]{:S(2)}, u32[]{:S(2)}) collective-permute-start(f32[16,128]{1,0:T(8,128)S(1)} %add.68), channel_id=1, source_target_pairs={{0,24},{1,25},{2,26},{3,27},{4,28},{5,29},{6,30},{7,31},{8,16},{9,... | collective-permute-start | bytes 24584 | tf_op jit(solution)/shard_map/ppermute | solution.py:370
  139.4 7.6 %collective-permute-start.12 = (f32[16,128]{1,0:T(8,128)S(1)}, f32[16,128]{1,0:T(8,128)S(1)}, u32[]{:S(2)}, u32[]{:S(2)}) collective-permute-start(f32[16,128]{1,0:T(8,128)S(1)} %add.68), channel_id=1, source_target_pairs={{0,16},{1,17},{2,18},{3,19},{4,20},{5,21},{6,22},{7,23},{8,24},{9,... | collective-permute-start | bytes 24584 | tf_op jit(solution)/shard_map/ppermute | solution.py:370
  140.6 6.4 %collective-permute-start.11 = (f32[16,128]{1,0:T(8,128)S(1)}, f32[16,128]{1,0:T(8,128)S(1)}, u32[]{:S(2)}, u32[]{:S(2)}) collective-permute-start(f32[16,128]{1,0:T(8,128)S(1)} %add.68), channel_id=1, source_target_pairs={{0,8},{1,9},{2,10},{3,11},{4,12},{5,13},{6,14},{7,15},{8,0},{9,1},... | collective-permute-start | bytes 24584 | tf_op jit(solution)/shard_map/ppermute | solution.py:370
  147.0 3.7 %collective-permute-start.14 = (f32[16,128]{1,0:T(8,128)S(1)}, f32[16,128]{1,0:T(8,128)S(1)}, u32[]{:S(2)}, u32[]{:S(2)}) collective-permute-start(f32[16,128]{1,0:T(8,128)S(1)} %add_add_fusion.mine_ref), channel_id=1, source_target_pairs={{0,4},{1,5},{2,6},{3,7},{4,0},{5,1},{6,2},{7,3},{8,12},{9,13},{10,... | collective-permute-start | bytes 24584 | tf_op jit(solution)/shard_map/ppermute | solution.py:370

commit v4 on v3

--- a/solution.py
+++ b/solution.py
@@ -416,7 +416,7 @@
             pltpu.VMEM((SLAB, BACK), BF16),
             pltpu.SemaphoreType.DMA((10,)),
         ],
-        compiler_params=pltpu.CompilerParams(vmem_limit_bytes=60 * MIB),
+        compiler_params=pltpu.CompilerParams(vmem_limit_bytes=50 * MIB),
         cost_estimate=pl.CostEstimate(flops=8 * 10**9, bytes_accessed=8 * MIB, transcendentals=5 * 10**6),
     )(col_arr, recv, *ups, q_bias, k_bias, v_bias, cos_table, sin_table)
 

time: 152 us -> 150 us (0.987)
  local copies, waits for them, and re-layouts: 2.12 us -> 0.13 us
  transfers between devices with their start and end apart: 17 -> 17, of which waited for: 12 -> 12; matrix products, arithmetic and copies ran while one was open for 3% -> 2% of each run, Pallas kernels for 2% -> 2%
where the time goes in v4:
time: 150 us
  waiting for transfers between devices  75.9 us (51%)
  starting transfers between devices  38 us (25%)
  Pallas kernels  32.1 us (21%)
  other arithmetic  2.89 us (2%)
    ppermute x15, waiting for transfers between devices, swap(): return lax.ppermute(values, axis, [(c, c ^ step) for c in range(size)])  55.1 us
    pallas_call x1, Pallas kernels, attend(): pl.pallas_call(attend_kernel, out_shape=[shape((TOK, PART), BF16)] * 4 +...  25.2 us
    all_to_all x1, waiting for transfers between devices, per_device(): lax.all_to_all(packed.reshape(32, 16, SENT), 'col', split_axis=0, concat_...  20.8 us
    ppermute x15, starting transfers between devices, swap(): return lax.ppermute(values, axis, [(c, c ^ step) for c in range(size)])  20.3 us
    all_to_all x1, starting transfers between devices, per_device(): lax.all_to_all(packed.reshape(32, 16, SENT), 'col', split_axis=0, concat_...  11.6 us
    all_to_all x1, starting transfers between devices, per_device(): lax.all_to_all(back.reshape(32, 16, BACK), 'col', split_axis=0, concat_ax...  6.17 us
    pallas_call x1, Pallas kernels, per_device(): pl.pallas_call(pack_kernel, out_shape=shape((8, KV_HEADS, 16, SENT), BF16...  3.01 us
  transfers between devices with their start and end apart: 17, of which 12 were waited for; matrix products, arithmetic and copies ran while one was open for 2% of the time, Pallas kernels for 2%

profile of v4, /device:TPU:16, one launch (start us, length us, event | category | flops | bytes accessed | tf_op | source)
XLA Modules:
  0.0 149.8 jit_solution(1800290129624096540)
XLA Ops:
  0.6 3.0 %shard_map.136 = bf16[8,4,16,1920]{3,2,1,0:T(8,128)(2,1)} custom-call(bf16[128,4096]{1,0:T(8,128)(2,1)} %bitcast.30, bf16[128,512]{1,0:T(8,128)(2,1)} %bitcast.31, bf16[128,512]{1,0:T(8,128)(2,1)} %bitcast.32, s32[1,128]{1,0:T(1,128)} %place_ref.1, s32[1,128]{1,0:T(1,128)} %seg_hbm.1), custom_call_target="tpu_custom_call" | custom-call | flops 167772160 | bytes 5242880 | tf_op jit(solution)/shard_map/pallas_call | solution.py:431
  3.7 11.6 %all-to-all-start = ((bf16[32,16,1920]{2,1,0:T(8,128)(2,1)}), bf16[32,16,1920]{2,1,0:T(8,128)(2,1)}, u32[]{:S(2)}, u32[]{:S(2)}) async-start(bf16[32,16,1920]{2,1,0:T(8,128)(2,1)} %bitcast.27), calls=%async_computation | async-start | bytes 3932160 | tf_op jit(solution)/shard_map/all_to_all | solution.py:448
  15.4 3.1 %collective-permute-start.2 = (bf16[128,1024]{1,0:T(8,128)(2,1)S(1)}, bf16[128,1024]{1,0:T(8,128)(2,1)S(1)}, u32[]{:S(2)}, u32[]{:S(2)}) collective-permute-start(bf16[128,1024]{1,0:T(8,128)(2,1)S(1)} %get-tuple-element.42), channel_id=1, source_target_pairs={{0,3},{1,2},{2,1},{3,0},{4,7},{5,6},{6,5},{7,4},{8,11},{9,10},{10,... | collective-permute-start | bytes 786440 | tf_op jit(solution)/shard_map/ppermute | solution.py:370
  18.5 0.4 collective-permute-start
  19.1 2.4 %fusion = (f32[1280,64]{1,0:T(8,128)S(1)}, f32[1280,64]{1,0:T(8,128)S(1)}, f32[1280,64]{1,0:T(8,128)S(1)}) fusion(f32[64]{0:T(128)S(1)} %negate_power_fusion, f32[1280]{0:T(1024)S(1)} %add_convert_fusion), kind=kLoop, calls=%fused_computation.8 | loop fusion | flops 163840 | bytes 988416 | tf_op jit(solution)/shard_map/neg | solution.py:382
  21.5 0.4 pad_maximum_fusion
  22.0 10.2 %collective-permute-done.2.up3 = bf16[128,1024]{1,0:T(8,128)(2,1)S(1)} collective-permute-done((bf16[128,1024]{1,0:T(8,128)(2,1)S(1)}, bf16[128,1024]{1,0:T(8,128)(2,1)S(1)}, u32[]{:S(2)}, u32[]{:S(2)}) %collective-permute-start.2) | collective-permute-done | bytes 262176 | tf_op jit(solution)/shard_map/ppermute | solution.py:370
  32.1 10.0 %collective-permute-done.1.up2 = bf16[128,1024]{1,0:T(8,128)(2,1)S(1)} collective-permute-done((bf16[128,1024]{1,0:T(8,128)(2,1)S(1)}, bf16[128,1024]{1,0:T(8,128)(2,1)S(1)}, u32[]{:S(2)}, u32[]{:S(2)}) %collective-permute-start.1) | collective-permute-done | bytes 262176 | tf_op jit(solution)/shard_map/ppermute | solution.py:370
  42.1 20.8 %all-to-all-done = bf16[32,16,1920]{2,1,0:T(8,128)(2,1)} async-done(((bf16[32,16,1920]{2,1,0:T(8,128)(2,1)}), bf16[32,16,1920]{2,1,0:T(8,128)(2,1)}, u32[]{:S(2)}, u32[]{:S(2)}) %all-to-all-start) | async-done | bytes 1966112 | tf_op jit(solution)/shard_map/all_to_all | solution.py:448
  62.8 25.2 %shard_map.137 = (bf16[128,1024]{1,0:T(8,128)(2,1)S(1)}, bf16[128,1024]{1,0:T(8,128)(2,1)S(1)}, bf16[128,1024]{1,0:T(8,128)(2,1)}, bf16[128,1024]{1,0:T(8,128)(2...) custom-call(s32[1]{0:T(128)} %bitcast.col_ref, bf16[512,1920]{1,0:T(8,128)(2,1)} %bitcast.5.recv_hbm, ...), custom_call_target="tpu_custom_call" | custom-call | flops 8000000000 | bytes 8388608 | tf_op jit(solution)/shard_map/pallas_call | solution.py:388
  88.1 6.2 %all-to-all-start.1 = ((bf16[32,16,1792]{2,1,0:T(8,128)(2,1)}), bf16[32,16,1792]{2,1,0:T(8,128)(2,1)S(1)}, u32[]{:S(2)}, u32[]{:S(2)}) async-start(bf16[32,16,1792]{2,1,0:T(8,128)(2,1)} %bitcast.28), calls=%async_computation.1 | async-start | bytes 3670016 | tf_op jit(solution)/shard_map/all_to_all | solution.py:462
  94.3 3.4 %collective-permute-start.5 = (bf16[128,1024]{1,0:T(8,128)(2,1)}, bf16[128,1024]{1,0:T(8,128)(2,1)S(1)}, u32[]{:S(2)}, u32[]{:S(2)}) collective-permute-start(bf16[128,1024]{1,0:T(8,128)(2,1)} %get-tuple-element.25), channel_id=1, source_target_pairs={{0,2},{1,3},{2,0},{3,1},{4,6},{5,7},{6,4},{7,5},{8,10},{9,11},{10,... | collective-permute-start | bytes 786440 | tf_op jit(solution)/shard_map/ppermute | solution.py:370
  97.7 0.3 collective-permute-start.8
  98.0 1.3 collective-permute-start.3
  99.3 2.4 %collective-permute-done.3 = f32[16,128]{1,0:T(8,128)S(1)} collective-permute-done((f32[16,128]{1,0:T(8,128)S(1)}, f32[16,128]{1,0:T(8,128)S(1)}, u32[]{:S(2)}, u32[]{:S(2)}) %collective-permute-start.3) | collective-permute-done | bytes 8224 | tf_op jit(solution)/shard_map/ppermute | solution.py:370
  101.7 0.8 collective-permute-start.4
  102.5 4.3 %collective-permute-done.4 = f32[16,128]{1,0:T(8,128)S(1)} collective-permute-done((f32[16,128]{1,0:T(8,128)S(1)}, f32[16,128]{1,0:T(8,128)S(1)}, u32[]{:S(2)}, u32[]{:S(2)}) %collective-permute-start.4) | collective-permute-done | bytes 8224 | tf_op jit(solution)/shard_map/ppermute | solution.py:370
  106.8 8.3 %collective-permute-done.5.c2 = bf16[128,1024]{1,0:T(8,128)(2,1)S(1)} collective-permute-done((bf16[128,1024]{1,0:T(8,128)(2,1)}, bf16[128,1024]{1,0:T(8,128)(2,1)S(1)}, u32[]{:S(2)}, u32[]{:S(2)}) %collective-permute-start.5) | collective-permute-done | bytes 262176 | tf_op jit(solution)/shard_map/ppermute | solution.py:370
  115.1 4.9 %collective-permute-done.6.c3 = bf16[128,1024]{1,0:T(8,128)(2,1)S(1)} collective-permute-done((bf16[128,1024]{1,0:T(8,128)(2,1)S(1)}, bf16[128,1024]{1,0:T(8,128)(2,1)S(1)}, u32[]{:S(2)}, u32[]{:S(2)}) %collective-permute-start.6) | collective-permute-done | bytes 262176 | tf_op jit(solution)/shard_map/ppermute | solution.py:370
  120.0 0.6 collective-permute-start.7
  120.6 1.0 shard_map.138
  121.6 2.5 %collective-permute-done.7 = f32[16,128]{1,0:T(8,128)S(1)} collective-permute-done((f32[16,128]{1,0:T(8,128)S(1)}, f32[16,128]{1,0:T(8,128)S(1)}, u32[]{:S(2)}, u32[]{:S(2)}) %collective-permute-start.7) | collective-permute-done | bytes 8224 | tf_op jit(solution)/shard_map/ppermute | solution.py:370
  124.1 1.2 collective-permute-done.9
  125.3 0.9 collective-permute-start.10
  126.2 4.3 %collective-permute-done.10 = f32[16,128]{1,0:T(8,128)S(1)} collective-permute-done((f32[16,128]{1,0:T(8,128)S(1)}, f32[16,128]{1,0:T(8,128)S(1)}, u32[]{:S(2)}, u32[]{:S(2)}) %collective-permute-start.10) | collective-permute-done | bytes 8224 | tf_op jit(solution)/shard_map/ppermute | solution.py:370
  130.5 6.8 %collective-permute-start.13 = (f32[16,128]{1,0:T(8,128)S(1)}, f32[16,128]{1,0:T(8,128)S(1)}, u32[]{:S(2)}, u32[]{:S(2)}) collective-permute-start(f32[16,128]{1,0:T(8,128)S(1)} %add.68), channel_id=1, source_target_pairs={{0,24},{1,25},{2,26},{3,27},{4,28},{5,29},{6,30},{7,31},{8,16},{9,... | collective-permute-start | bytes 24584 | tf_op jit(solution)/shard_map/ppermute | solution.py:370
  137.3 1.2 collective-permute-start.12
  138.5 1.1 collective-permute-start.11
  139.7 5.2 %collective-permute-done.12 = f32[16,128]{1,0:T(8,128)S(1)} collective-permute-done((f32[16,128]{1,0:T(8,128)S(1)}, f32[16,128]{1,0:T(8,128)S(1)}, u32[]{:S(2)}, u32[]{:S(2)}) %collective-permute-start.12) | collective-permute-done | bytes 8224 | tf_op jit(solution)/shard_map/ppermute | solution.py:370
  145.0 1.6 %shard_map.139 = (bf16[128,4096]{1,0:T(8,128)(2,1)}, bf16[128,512]{1,0:T(8,128)(2,1)}, bf16[128,512]{1,0:T(8,128)(2,1)}) custom-call(bf16[32,16,1792]{2,1,0:T(8,128)(2,1)S(1)} %all-to-all-done.1.back_ref, s32[1,128]{1,0:T(1,128)S(1)} %copy-done), custom_call_target="tpu_custom_call" | custom-call | flops 167772160 | bytes 4194304 | tf_op jit(solution)/shard_map/pallas_call | solution.py:485
  146.6 2.0 %collective-permute-done.14.other_ref = f32[16,128]{1,0:T(8,128)S(1)} collective-permute-done((f32[16,128]{1,0:T(8,128)S(1)}, f32[16,128]{1,0:T(8,128)S(1)}, u32[]{:S(2)}, u32[]{:S(2)}) %collective-permute-start.14) | collective-permute-done | bytes 8224 | tf_op jit(solution)/shard_map/ppermute | solution.py:370
  148.6 1.2 shard_map.140
  (30 shorter events, 0.7 us)
Async XLA Ops:
  3.6 11.6 %copy-start.4 = (bf16[1,128,4096]{2,1,0:T(8,128)(2,1)S(1)}, bf16[1,128,4096]{2,1,0:T(8,128)(2,1)}, u32[]{:S(2)}) copy-start(bf16[1,128,4096]{2,1,0:T(8,128)(2,1)} %param.17) | copy-start | bytes 3145732
  3.7 59.2 %all-to-all-start = ((bf16[32,16,1920]{2,1,0:T(8,128)(2,1)}), bf16[32,16,1920]{2,1,0:T(8,128)(2,1)}, u32[]{:S(2)}, u32[]{:S(2)}) async-start(bf16[32,16,1920]{2,1,0:T(8,128)(2,1)} %bitcast.27), calls=%async_computation | async-start | bytes 3932160 | tf_op jit(solution)/shard_map/all_to_all | solution.py:448
  15.4 16.7 %collective-permute-start.2 = (bf16[128,1024]{1,0:T(8,128)(2,1)S(1)}, bf16[128,1024]{1,0:T(8,128)(2,1)S(1)}, u32[]{:S(2)}, u32[]{:S(2)}) collective-permute-start(bf16[128,1024]{1,0:T(8,128)(2,1)S(1)} %get-tuple-element.42), channel_id=1, source_target_pairs={{0,3},{1,2},{2,1},{3,0},{4,7},{5,6},{6,5},{7,4},{8,11},{9,10},{10,... | collective-permute-start | bytes 786440 | tf_op jit(solution)/shard_map/ppermute | solution.py:370
  18.5 13.7 %collective-permute-start = (bf16[128,1024]{1,0:T(8,128)(2,1)S(1)}, bf16[128,1024]{1,0:T(8,128)(2,1)S(1)}, u32[]{:S(2)}, u32[]{:S(2)}) collective-permute-start(bf16[128,1024]{1,0:T(8,128)(2,1)S(1)} %get-tuple-element.43), channel_id=1, source_target_pairs={{0,1},{1,0},{2,3},{3,2},{4,5},{5,4},{6,7},{7,6},{8,9},{9,8},{10,11... | collective-permute-start | bytes 786440 | tf_op jit(solution)/shard_map/ppermute | solution.py:370
  18.8 23.2 %collective-permute-start.1 = (bf16[128,1024]{1,0:T(8,128)(2,1)S(1)}, bf16[128,1024]{1,0:T(8,128)(2,1)S(1)}, u32[]{:S(2)}, u32[]{:S(2)}) collective-permute-start(bf16[128,1024]{1,0:T(8,128)(2,1)S(1)} %get-tuple-element.45), channel_id=1, source_target_pairs={{0,2},{1,3},{2,0},{3,1},{4,6},{5,7},{6,4},{7,5},{8,10},{9,11},{10,... | collective-permute-start | bytes 786440 | tf_op jit(solution)/shard_map/ppermute | solution.py:370
  21.5 41.3 %copy-start.1 = (f32[4096]{0:T(1024)S(1)}, f32[4096]{0:T(1024)}, u32[]{:S(2)}) copy-start(f32[4096]{0:T(1024)} %param.12) | copy-start | bytes 49156
  21.5 41.3 %copy-start.2 = (f32[512]{0:T(512)S(1)}, f32[512]{0:T(512)}, u32[]{:S(2)}) copy-start(f32[512]{0:T(512)} %param.13) | copy-start | bytes 6148
  21.5 41.3 %copy-start.3 = (f32[512]{0:T(512)S(1)}, f32[512]{0:T(512)}, u32[]{:S(2)}) copy-start(f32[512]{0:T(512)} %param.14) | copy-start | bytes 6148
  88.1 56.9 %all-to-all-start.1 = ((bf16[32,16,1792]{2,1,0:T(8,128)(2,1)}), bf16[32,16,1792]{2,1,0:T(8,128)(2,1)S(1)}, u32[]{:S(2)}, u32[]{:S(2)}) async-start(bf16[32,16,1792]{2,1,0:T(8,128)(2,1)} %bitcast.28), calls=%async_computation.1 | async-start | bytes 3670016 | tf_op jit(solution)/shard_map/all_to_all | solution.py:462
  94.3 50.7 %copy-start = (s32[1,128]{1,0:T(1,128)S(1)}, s32[1,128]{1,0:T(1,128)}, u32[]{:S(2)}) copy-start(s32[1,128]{1,0:T(1,128)} %place_ref.1) | copy-start | bytes 1540
  94.3 20.8 %collective-permute-start.5 = (bf16[128,1024]{1,0:T(8,128)(2,1)}, bf16[128,1024]{1,0:T(8,128)(2,1)S(1)}, u32[]{:S(2)}, u32[]{:S(2)}) collective-permute-start(bf16[128,1024]{1,0:T(8,128)(2,1)} %get-tuple-element.25), channel_id=1, source_target_pairs={{0,2},{1,3},{2,0},{3,1},{4,6},{5,7},{6,4},{7,5},{8,10},{9,11},{10,... | collective-permute-start | bytes 786440 | tf_op jit(solution)/shard_map/ppermute | solution.py:370
  97.7 22.4 %collective-permute-start.6 = (bf16[128,1024]{1,0:T(8,128)(2,1)S(1)}, bf16[128,1024]{1,0:T(8,128)(2,1)S(1)}, u32[]{:S(2)}, u32[]{:S(2)}) collective-permute-start(bf16[128,1024]{1,0:T(8,128)(2,1)S(1)} %get-tuple-element.26), channel_id=1, source_target_pairs={{0,3},{1,2},{2,1},{3,0},{4,7},{5,6},{6,5},{7,4},{8,11},{9,10},{10,... | collective-permute-start | bytes 786440 | tf_op jit(solution)/shard_map/ppermute | solution.py:370
  97.7 22.9 %collective-permute-start.8 = (bf16[128,1024]{1,0:T(8,128)(2,1)S(1)}, bf16[128,1024]{1,0:T(8,128)(2,1)S(1)}, u32[]{:S(2)}, u32[]{:S(2)}) collective-permute-start(bf16[128,1024]{1,0:T(8,128)(2,1)S(1)} %get-tuple-element.29), channel_id=1, source_target_pairs={{0,1},{1,0},{2,3},{3,2},{4,5},{5,4},{6,7},{7,6},{8,9},{9,8},{10,11... | collective-permute-start | bytes 786440 | tf_op jit(solution)/shard_map/ppermute | solution.py:370
  98.0 3.7 %collective-permute-start.3 = (f32[16,128]{1,0:T(8,128)S(1)}, f32[16,128]{1,0:T(8,128)S(1)}, u32[]{:S(2)}, u32[]{:S(2)}) collective-permute-start(f32[16,128]{1,0:T(8,128)S(1)} %get-tuple-element.24), channel_id=1, source_target_pairs={{0,64},{32,96},{64,0},{96,32},{128,192},{160,224},{192,128},{224,1... | collective-permute-start | bytes 24584 | tf_op jit(solution)/shard_map/ppermute | solution.py:370
  101.7 5.2 %collective-permute-start.4 = (f32[16,128]{1,0:T(8,128)S(1)}, f32[16,128]{1,0:T(8,128)S(1)}, u32[]{:S(2)}, u32[]{:S(2)}) collective-permute-start(f32[16,128]{1,0:T(8,128)S(1)} %add.64), channel_id=1, source_target_pairs={{0,128},{32,160},{64,192},{96,224},{128,0},{160,32},{192,64},{224,... | collective-permute-start | bytes 24584 | tf_op jit(solution)/shard_map/ppermute | solution.py:370
  120.0 4.1 %collective-permute-start.7 = (f32[16,128]{1,0:T(8,128)S(1)}, f32[16,128]{1,0:T(8,128)S(1)}, u32[]{:S(2)}, u32[]{:S(2)}) collective-permute-start(f32[16,128]{1,0:T(8,128)S(1)} %add.65), channel_id=1, source_target_pairs={{0,32},{32,0},{64,96},{96,64},{128,160},{160,128},{192,224},{224,1... | collective-permute-start | bytes 24584 | tf_op jit(solution)/shard_map/ppermute | solution.py:370
  124.1 1.2 collective-permute-start.9
  125.3 5.2 %collective-permute-start.10 = (f32[16,128]{1,0:T(8,128)S(1)}, f32[16,128]{1,0:T(8,128)S(1)}, u32[]{:S(2)}, u32[]{:S(2)}) collective-permute-start(f32[16,128]{1,0:T(8,128)S(1)} %fusion.1), channel_id=1, source_target_pairs={{0,2},{1,3},{2,0},{3,1},{4,6},{5,7},{6,4},{7,5},{8,10},{9,11},{10,... | collective-permute-start | bytes 24584 | tf_op jit(solution)/shard_map/ppermute | solution.py:370
  130.5 9.2 %collective-permute-start.13 = (f32[16,128]{1,0:T(8,128)S(1)}, f32[16,128]{1,0:T(8,128)S(1)}, u32[]{:S(2)}, u32[]{:S(2)}) collective-permute-start(f32[16,128]{1,0:T(8,128)S(1)} %add.68), channel_id=1, source_target_pairs={{0,24},{1,25},{2,26},{3,27},{4,28},{5,29},{6,30},{7,31},{8,16},{9,... | collective-permute-start | bytes 24584 | tf_op jit(solution)/shard_map/ppermute | solution.py:370
  137.3 7.6 %collective-permute-start.12 = (f32[16,128]{1,0:T(8,128)S(1)}, f32[16,128]{1,0:T(8,128)S(1)}, u32[]{:S(2)}, u32[]{:S(2)}) collective-permute-start(f32[16,128]{1,0:T(8,128)S(1)} %add.68), channel_id=1, source_target_pairs={{0,16},{1,17},{2,18},{3,19},{4,20},{5,21},{6,22},{7,23},{8,24},{9,... | collective-permute-start | bytes 24584 | tf_op jit(solution)/shard_map/ppermute | solution.py:370
  138.5 6.4 %collective-permute-start.11 = (f32[16,128]{1,0:T(8,128)S(1)}, f32[16,128]{1,0:T(8,128)S(1)}, u32[]{:S(2)}, u32[]{:S(2)}) collective-permute-start(f32[16,128]{1,0:T(8,128)S(1)} %add.68), channel_id=1, source_target_pairs={{0,8},{1,9},{2,10},{3,11},{4,12},{5,13},{6,14},{7,15},{8,0},{9,1},... | collective-permute-start | bytes 24584 | tf_op jit(solution)/shard_map/ppermute | solution.py:370
  144.9 3.7 %collective-permute-start.14 = (f32[16,128]{1,0:T(8,128)S(1)}, f32[16,128]{1,0:T(8,128)S(1)}, u32[]{:S(2)}, u32[]{:S(2)}) collective-permute-start(f32[16,128]{1,0:T(8,128)S(1)} %add_add_fusion.mine_ref), channel_id=1, source_target_pairs={{0,4},{1,5},{2,6},{3,7},{4,0},{5,1},{6,2},{7,3},{8,12},{9,13},{10,... | collective-permute-start | bytes 24584 | tf_op jit(solution)/shard_map/ppermute | solution.py:370

commit v5 on v4

--- a/solution.py
+++ b/solution.py
@@ -128,7 +128,7 @@
     scale = HEAD_DIM ** (-0.5)
 
     copies = [
-        pltpu.make_async_copy(recv_hbm, recv_s, sems.at[0]),
+        pltpu.make_async_copy(recv_hbm.at[:, PART:SENT], recv_s.at[:, PART:SENT], sems.at[0]),
         pltpu.make_async_copy(cos_hbm, cos_t, sems.at[1]),
         pltpu.make_async_copy(sin_hbm, sin_t, sems.at[2]),
         pltpu.make_async_copy(kb_hbm.at[:, pl.ds(pl.multiple_of(HEAD_DIM * j, HEAD_DIM), HEAD_DIM)], kb_s, sems.at[3]),
@@ -141,6 +141,9 @@
                 ref, up_s.at[pl.ds(pl.multiple_of(TOK * (j ^ s), TOK), TOK), :], sems.at[6 + s]
             )
         )
+    copies.append(
+        pltpu.make_async_copy(recv_hbm.at[:, 0:PART], recv_s.at[:, 0:PART], sems.at[10])
+    )
     for copy in copies:
         copy.start()
     dk_s[...] = jnp.zeros_like(dk_s)
@@ -193,6 +196,7 @@
         kt_s[:, rows] = jnp.transpose(keys).astype(BF16)
         vt_s[:, rows] = jnp.transpose(vals).astype(BF16)
         if t == 2:
+            copies[10].wait()
             other = jnp.where((lane >= 8) & (lane < 17), MASKED * (1.0 - name), 0.0).astype(BF16)
             for pair in range(4):
                 lanes = slice(256 * pair, 256 * (pair + 1))
@@ -202,7 +206,7 @@
                     q_s[2 * pair + u, :, 0:HEAD_DIM] = turn(one, cos_s[rows, :], sin_s[rows, :]).astype(BF16)
                     q_s[2 * pair + u, :, HEAD_DIM:] = other
 
-    for copy in copies[6:]:
+    for copy in copies[6:10]:
         copy.wait()
 
     def one_head(h, spans):
@@ -414,7 +418,7 @@
             pltpu.VMEM((SLAB, PART), BF16),
             pltpu.VMEM((SLAB, PART), BF16),
             pltpu.VMEM((SLAB, BACK), BF16),
-            pltpu.SemaphoreType.DMA((10,)),
+            pltpu.SemaphoreType.DMA((11,)),
         ],
         compiler_params=pltpu.CompilerParams(vmem_limit_bytes=50 * MIB),
         cost_estimate=pl.CostEstimate(flops=8 * 10**9, bytes_accessed=8 * MIB, transcendentals=5 * 10**6),

time: 150 us -> 150 us (level)
  no operation moved by 1% of the time
where the time goes in v5:
time: 150 us
  waiting for transfers between devices  76.3 us (51%)
  starting transfers between devices  37.6 us (25%)
  Pallas kernels  32.1 us (21%)
  other arithmetic  2.89 us (2%)
    ppermute x15, waiting for transfers between devices, swap(): return lax.ppermute(values, axis, [(c, c ^ step) for c in range(size)])  55.5 us
    pallas_call x1, Pallas kernels, attend(): pl.pallas_call(attend_kernel, out_shape=[shape((TOK, PART), BF16)] * 4 +...  25.2 us
    all_to_all x1, waiting for transfers between devices, per_device(): lax.all_to_all(packed.reshape(32, 16, SENT), 'col', split_axis=0, concat_...  20.8 us
    ppermute x15, starting transfers between devices, swap(): return lax.ppermute(values, axis, [(c, c ^ step) for c in range(size)])  19.9 us
    all_to_all x1, starting transfers between devices, per_device(): lax.all_to_all(packed.reshape(32, 16, SENT), 'col', split_axis=0, concat_...  11.6 us
    all_to_all x1, starting transfers between devices, per_device(): lax.all_to_all(back.reshape(32, 16, BACK), 'col', split_axis=0, concat_ax...  6.12 us
    pallas_call x1, Pallas kernels, per_device(): pl.pallas_call(pack_kernel, out_shape=shape((8, KV_HEADS, 16, SENT), BF16...  3.01 us
  transfers between devices with their start and end apart: 17, of which 12 were waited for; matrix products, arithmetic and copies ran while one was open for 2% of the time, Pallas kernels for 2%

profile of v5, /device:TPU:16, one launch (start us, length us, event | category | flops | bytes accessed | tf_op | source)
XLA Modules:
  0.0 149.8 jit_solution(1671528825934027850)
XLA Ops:
  0.6 3.0 %shard_map.136 = bf16[8,4,16,1920]{3,2,1,0:T(8,128)(2,1)} custom-call(bf16[128,4096]{1,0:T(8,128)(2,1)} %bitcast.30, bf16[128,512]{1,0:T(8,128)(2,1)} %bitcast.31, bf16[128,512]{1,0:T(8,128)(2,1)} %bitcast.32, s32[1,128]{1,0:T(1,128)} %place_ref.1, s32[1,128]{1,0:T(1,128)} %seg_hbm.1), custom_call_target="tpu_custom_call" | custom-call | flops 167772160 | bytes 5242880 | tf_op jit(solution)/shard_map/pallas_call | solution.py:435
  3.7 11.6 %all-to-all-start = ((bf16[32,16,1920]{2,1,0:T(8,128)(2,1)}), bf16[32,16,1920]{2,1,0:T(8,128)(2,1)}, u32[]{:S(2)}, u32[]{:S(2)}) async-start(bf16[32,16,1920]{2,1,0:T(8,128)(2,1)} %bitcast.27), calls=%async_computation | async-start | bytes 3932160 | tf_op jit(solution)/shard_map/all_to_all | solution.py:452
  15.4 3.1 %collective-permute-start.2 = (bf16[128,1024]{1,0:T(8,128)(2,1)S(1)}, bf16[128,1024]{1,0:T(8,128)(2,1)S(1)}, u32[]{:S(2)}, u32[]{:S(2)}) collective-permute-start(bf16[128,1024]{1,0:T(8,128)(2,1)S(1)} %get-tuple-element.42), channel_id=1, source_target_pairs={{0,3},{1,2},{2,1},{3,0},{4,7},{5,6},{6,5},{7,4},{8,11},{9,10},{10,... | collective-permute-start | bytes 786440 | tf_op jit(solution)/shard_map/ppermute | solution.py:374
  18.5 0.4 collective-permute-start
  19.1 2.4 %fusion = (f32[1280,64]{1,0:T(8,128)S(1)}, f32[1280,64]{1,0:T(8,128)S(1)}, f32[1280,64]{1,0:T(8,128)S(1)}) fusion(f32[64]{0:T(128)S(1)} %negate_power_fusion, f32[1280]{0:T(1024)S(1)} %add_convert_fusion), kind=kLoop, calls=%fused_computation.8 | loop fusion | flops 163840 | bytes 988416 | tf_op jit(solution)/shard_map/neg | solution.py:386
  21.5 0.4 pad_maximum_fusion
  22.0 10.2 %collective-permute-done.2.up3 = bf16[128,1024]{1,0:T(8,128)(2,1)S(1)} collective-permute-done((bf16[128,1024]{1,0:T(8,128)(2,1)S(1)}, bf16[128,1024]{1,0:T(8,128)(2,1)S(1)}, u32[]{:S(2)}, u32[]{:S(2)}) %collective-permute-start.2) | collective-permute-done | bytes 262176 | tf_op jit(solution)/shard_map/ppermute | solution.py:374
  32.1 10.0 %collective-permute-done.1.up2 = bf16[128,1024]{1,0:T(8,128)(2,1)S(1)} collective-permute-done((bf16[128,1024]{1,0:T(8,128)(2,1)S(1)}, bf16[128,1024]{1,0:T(8,128)(2,1)S(1)}, u32[]{:S(2)}, u32[]{:S(2)}) %collective-permute-start.1) | collective-permute-done | bytes 262176 | tf_op jit(solution)/shard_map/ppermute | solution.py:374
  42.1 20.8 %all-to-all-done = bf16[32,16,1920]{2,1,0:T(8,128)(2,1)} async-done(((bf16[32,16,1920]{2,1,0:T(8,128)(2,1)}), bf16[32,16,1920]{2,1,0:T(8,128)(2,1)}, u32[]{:S(2)}, u32[]{:S(2)}) %all-to-all-start) | async-done | bytes 1966112 | tf_op jit(solution)/shard_map/all_to_all | solution.py:452
  62.8 25.2 %shard_map.137 = (bf16[128,1024]{1,0:T(8,128)(2,1)S(1)}, bf16[128,1024]{1,0:T(8,128)(2,1)S(1)}, bf16[128,1024]{1,0:T(8,128)(2,1)}, bf16[128,1024]{1,0:T(8,128)(2...) custom-call(s32[1]{0:T(128)} %bitcast.col_ref, bf16[512,1920]{1,0:T(8,128)(2,1)} %bitcast.5.recv_hbm, ...), custom_call_target="tpu_custom_call" | custom-call | flops 8000000000 | bytes 8388608 | tf_op jit(solution)/shard_map/pallas_call | solution.py:392
  88.1 6.1 %all-to-all-start.1 = ((bf16[32,16,1792]{2,1,0:T(8,128)(2,1)}), bf16[32,16,1792]{2,1,0:T(8,128)(2,1)S(1)}, u32[]{:S(2)}, u32[]{:S(2)}) async-start(bf16[32,16,1792]{2,1,0:T(8,128)(2,1)} %bitcast.28), calls=%async_computation.1 | async-start | bytes 3670016 | tf_op jit(solution)/shard_map/all_to_all | solution.py:466
  94.2 3.4 %collective-permute-start.5 = (bf16[128,1024]{1,0:T(8,128)(2,1)}, bf16[128,1024]{1,0:T(8,128)(2,1)S(1)}, u32[]{:S(2)}, u32[]{:S(2)}) collective-permute-start(bf16[128,1024]{1,0:T(8,128)(2,1)} %get-tuple-element.25), channel_id=1, source_target_pairs={{0,2},{1,3},{2,0},{3,1},{4,6},{5,7},{6,4},{7,5},{8,10},{9,11},{10,... | collective-permute-start | bytes 786440 | tf_op jit(solution)/shard_map/ppermute | solution.py:374
  97.6 0.3 collective-permute-start.8
  97.9 1.3 collective-permute-start.3
  99.2 2.4 %collective-permute-done.3 = f32[16,128]{1,0:T(8,128)S(1)} collective-permute-done((f32[16,128]{1,0:T(8,128)S(1)}, f32[16,128]{1,0:T(8,128)S(1)}, u32[]{:S(2)}, u32[]{:S(2)}) %collective-permute-start.3) | collective-permute-done | bytes 8224 | tf_op jit(solution)/shard_map/ppermute | solution.py:374
  101.6 0.4 collective-permute-start.4
  102.0 4.8 %collective-permute-done.4 = f32[16,128]{1,0:T(8,128)S(1)} collective-permute-done((f32[16,128]{1,0:T(8,128)S(1)}, f32[16,128]{1,0:T(8,128)S(1)}, u32[]{:S(2)}, u32[]{:S(2)}) %collective-permute-start.4) | collective-permute-done | bytes 8224 | tf_op jit(solution)/shard_map/ppermute | solution.py:374
  106.8 8.3 %collective-permute-done.5.c2 = bf16[128,1024]{1,0:T(8,128)(2,1)S(1)} collective-permute-done((bf16[128,1024]{1,0:T(8,128)(2,1)}, bf16[128,1024]{1,0:T(8,128)(2,1)S(1)}, u32[]{:S(2)}, u32[]{:S(2)}) %collective-permute-start.5) | collective-permute-done | bytes 262176 | tf_op jit(solution)/shard_map/ppermute | solution.py:374
  115.0 4.9 %collective-permute-done.6.c3 = bf16[128,1024]{1,0:T(8,128)(2,1)S(1)} collective-permute-done((bf16[128,1024]{1,0:T(8,128)(2,1)S(1)}, bf16[128,1024]{1,0:T(8,128)(2,1)S(1)}, u32[]{:S(2)}, u32[]{:S(2)}) %collective-permute-start.6) | collective-permute-done | bytes 262176 | tf_op jit(solution)/shard_map/ppermute | solution.py:374
  119.9 0.6 collective-permute-start.7
  120.6 1.0 shard_map.138
  121.6 2.5 %collective-permute-done.7 = f32[16,128]{1,0:T(8,128)S(1)} collective-permute-done((f32[16,128]{1,0:T(8,128)S(1)}, f32[16,128]{1,0:T(8,128)S(1)}, u32[]{:S(2)}, u32[]{:S(2)}) %collective-permute-start.7) | collective-permute-done | bytes 8224 | tf_op jit(solution)/shard_map/ppermute | solution.py:374
  124.1 1.2 collective-permute-done.9
  125.3 0.9 collective-permute-start.10
  126.2 4.3 %collective-permute-done.10 = f32[16,128]{1,0:T(8,128)S(1)} collective-permute-done((f32[16,128]{1,0:T(8,128)S(1)}, f32[16,128]{1,0:T(8,128)S(1)}, u32[]{:S(2)}, u32[]{:S(2)}) %collective-permute-start.10) | collective-permute-done | bytes 8224 | tf_op jit(solution)/shard_map/ppermute | solution.py:374
  130.5 6.8 %collective-permute-start.13 = (f32[16,128]{1,0:T(8,128)S(1)}, f32[16,128]{1,0:T(8,128)S(1)}, u32[]{:S(2)}, u32[]{:S(2)}) collective-permute-start(f32[16,128]{1,0:T(8,128)S(1)} %add.68), channel_id=1, source_target_pairs={{0,24},{1,25},{2,26},{3,27},{4,28},{5,29},{6,30},{7,31},{8,16},{9,... | collective-permute-start | bytes 24584 | tf_op jit(solution)/shard_map/ppermute | solution.py:374
  137.2 1.2 collective-permute-start.12
  138.4 1.1 collective-permute-start.11
  139.7 5.2 %collective-permute-done.12 = f32[16,128]{1,0:T(8,128)S(1)} collective-permute-done((f32[16,128]{1,0:T(8,128)S(1)}, f32[16,128]{1,0:T(8,128)S(1)}, u32[]{:S(2)}, u32[]{:S(2)}) %collective-permute-start.12) | collective-permute-done | bytes 8224 | tf_op jit(solution)/shard_map/ppermute | solution.py:374
  144.9 1.6 %shard_map.139 = (bf16[128,4096]{1,0:T(8,128)(2,1)}, bf16[128,512]{1,0:T(8,128)(2,1)}, bf16[128,512]{1,0:T(8,128)(2,1)}) custom-call(bf16[32,16,1792]{2,1,0:T(8,128)(2,1)S(1)} %all-to-all-done.1.back_ref, s32[1,128]{1,0:T(1,128)S(1)} %copy-done), custom_call_target="tpu_custom_call" | custom-call | flops 167772160 | bytes 4194304 | tf_op jit(solution)/shard_map/pallas_call | solution.py:489
  146.6 2.0 %collective-permute-done.14.other_ref = f32[16,128]{1,0:T(8,128)S(1)} collective-permute-done((f32[16,128]{1,0:T(8,128)S(1)}, f32[16,128]{1,0:T(8,128)S(1)}, u32[]{:S(2)}, u32[]{:S(2)}) %collective-permute-start.14) | collective-permute-done | bytes 8224 | tf_op jit(solution)/shard_map/ppermute | solution.py:374
  148.6 1.2 shard_map.140
  (30 shorter events, 0.7 us)
Async XLA Ops:
  3.6 11.6 %copy-start.4 = (bf16[1,128,4096]{2,1,0:T(8,128)(2,1)S(1)}, bf16[1,128,4096]{2,1,0:T(8,128)(2,1)}, u32[]{:S(2)}) copy-start(bf16[1,128,4096]{2,1,0:T(8,128)(2,1)} %param.17) | copy-start | bytes 3145732
  3.7 59.2 %all-to-all-start = ((bf16[32,16,1920]{2,1,0:T(8,128)(2,1)}), bf16[32,16,1920]{2,1,0:T(8,128)(2,1)}, u32[]{:S(2)}, u32[]{:S(2)}) async-start(bf16[32,16,1920]{2,1,0:T(8,128)(2,1)} %bitcast.27), calls=%async_computation | async-start | bytes 3932160 | tf_op jit(solution)/shard_map/all_to_all | solution.py:452
  15.4 16.7 %collective-permute-start.2 = (bf16[128,1024]{1,0:T(8,128)(2,1)S(1)}, bf16[128,1024]{1,0:T(8,128)(2,1)S(1)}, u32[]{:S(2)}, u32[]{:S(2)}) collective-permute-start(bf16[128,1024]{1,0:T(8,128)(2,1)S(1)} %get-tuple-element.42), channel_id=1, source_target_pairs={{0,3},{1,2},{2,1},{3,0},{4,7},{5,6},{6,5},{7,4},{8,11},{9,10},{10,... | collective-permute-start | bytes 786440 | tf_op jit(solution)/shard_map/ppermute | solution.py:374
  18.5 13.7 %collective-permute-start = (bf16[128,1024]{1,0:T(8,128)(2,1)S(1)}, bf16[128,1024]{1,0:T(8,128)(2,1)S(1)}, u32[]{:S(2)}, u32[]{:S(2)}) collective-permute-start(bf16[128,1024]{1,0:T(8,128)(2,1)S(1)} %get-tuple-element.43), channel_id=1, source_target_pairs={{0,1},{1,0},{2,3},{3,2},{4,5},{5,4},{6,7},{7,6},{8,9},{9,8},{10,11... | collective-permute-start | bytes 786440 | tf_op jit(solution)/shard_map/ppermute | solution.py:374
  18.8 23.2 %collective-permute-start.1 = (bf16[128,1024]{1,0:T(8,128)(2,1)S(1)}, bf16[128,1024]{1,0:T(8,128)(2,1)S(1)}, u32[]{:S(2)}, u32[]{:S(2)}) collective-permute-start(bf16[128,1024]{1,0:T(8,128)(2,1)S(1)} %get-tuple-element.45), channel_id=1, source_target_pairs={{0,2},{1,3},{2,0},{3,1},{4,6},{5,7},{6,4},{7,5},{8,10},{9,11},{10,... | collective-permute-start | bytes 786440 | tf_op jit(solution)/shard_map/ppermute | solution.py:374
  21.5 41.3 %copy-start.1 = (f32[4096]{0:T(1024)S(1)}, f32[4096]{0:T(1024)}, u32[]{:S(2)}) copy-start(f32[4096]{0:T(1024)} %param.12) | copy-start | bytes 49156
  21.5 41.3 %copy-start.2 = (f32[512]{0:T(512)S(1)}, f32[512]{0:T(512)}, u32[]{:S(2)}) copy-start(f32[512]{0:T(512)} %param.13) | copy-start | bytes 6148
  21.5 41.3 %copy-start.3 = (f32[512]{0:T(512)S(1)}, f32[512]{0:T(512)}, u32[]{:S(2)}) copy-start(f32[512]{0:T(512)} %param.14) | copy-start | bytes 6148
  88.1 56.9 %all-to-all-start.1 = ((bf16[32,16,1792]{2,1,0:T(8,128)(2,1)}), bf16[32,16,1792]{2,1,0:T(8,128)(2,1)S(1)}, u32[]{:S(2)}, u32[]{:S(2)}) async-start(bf16[32,16,1792]{2,1,0:T(8,128)(2,1)} %bitcast.28), calls=%async_computation.1 | async-start | bytes 3670016 | tf_op jit(solution)/shard_map/all_to_all | solution.py:466
  94.2 50.7 %copy-start = (s32[1,128]{1,0:T(1,128)S(1)}, s32[1,128]{1,0:T(1,128)}, u32[]{:S(2)}) copy-start(s32[1,128]{1,0:T(1,128)} %place_ref.1) | copy-start | bytes 1540
  94.2 20.8 %collective-permute-start.5 = (bf16[128,1024]{1,0:T(8,128)(2,1)}, bf16[128,1024]{1,0:T(8,128)(2,1)S(1)}, u32[]{:S(2)}, u32[]{:S(2)}) collective-permute-start(bf16[128,1024]{1,0:T(8,128)(2,1)} %get-tuple-element.25), channel_id=1, source_target_pairs={{0,2},{1,3},{2,0},{3,1},{4,6},{5,7},{6,4},{7,5},{8,10},{9,11},{10,... | collective-permute-start | bytes 786440 | tf_op jit(solution)/shard_map/ppermute | solution.py:374
  97.6 22.4 %collective-permute-start.6 = (bf16[128,1024]{1,0:T(8,128)(2,1)S(1)}, bf16[128,1024]{1,0:T(8,128)(2,1)S(1)}, u32[]{:S(2)}, u32[]{:S(2)}) collective-permute-start(bf16[128,1024]{1,0:T(8,128)(2,1)S(1)} %get-tuple-element.26), channel_id=1, source_target_pairs={{0,3},{1,2},{2,1},{3,0},{4,7},{5,6},{6,5},{7,4},{8,11},{9,10},{10,... | collective-permute-start | bytes 786440 | tf_op jit(solution)/shard_map/ppermute | solution.py:374
  97.6 23.0 %collective-permute-start.8 = (bf16[128,1024]{1,0:T(8,128)(2,1)S(1)}, bf16[128,1024]{1,0:T(8,128)(2,1)S(1)}, u32[]{:S(2)}, u32[]{:S(2)}) collective-permute-start(bf16[128,1024]{1,0:T(8,128)(2,1)S(1)} %get-tuple-element.29), channel_id=1, source_target_pairs={{0,1},{1,0},{2,3},{3,2},{4,5},{5,4},{6,7},{7,6},{8,9},{9,8},{10,11... | collective-permute-start | bytes 786440 | tf_op jit(solution)/shard_map/ppermute | solution.py:374
  97.9 3.7 %collective-permute-start.3 = (f32[16,128]{1,0:T(8,128)S(1)}, f32[16,128]{1,0:T(8,128)S(1)}, u32[]{:S(2)}, u32[]{:S(2)}) collective-permute-start(f32[16,128]{1,0:T(8,128)S(1)} %get-tuple-element.24), channel_id=1, source_target_pairs={{0,64},{32,96},{64,0},{96,32},{128,192},{160,224},{192,128},{224,1... | collective-permute-start | bytes 24584 | tf_op jit(solution)/shard_map/ppermute | solution.py:374
  101.6 5.2 %collective-permute-start.4 = (f32[16,128]{1,0:T(8,128)S(1)}, f32[16,128]{1,0:T(8,128)S(1)}, u32[]{:S(2)}, u32[]{:S(2)}) collective-permute-start(f32[16,128]{1,0:T(8,128)S(1)} %add.64), channel_id=1, source_target_pairs={{0,128},{32,160},{64,192},{96,224},{128,0},{160,32},{192,64},{224,... | collective-permute-start | bytes 24584 | tf_op jit(solution)/shard_map/ppermute | solution.py:374
  119.9 4.1 %collective-permute-start.7 = (f32[16,128]{1,0:T(8,128)S(1)}, f32[16,128]{1,0:T(8,128)S(1)}, u32[]{:S(2)}, u32[]{:S(2)}) collective-permute-start(f32[16,128]{1,0:T(8,128)S(1)} %add.65), channel_id=1, source_target_pairs={{0,32},{32,0},{64,96},{96,64},{128,160},{160,128},{192,224},{224,1... | collective-permute-start | bytes 24584 | tf_op jit(solution)/shard_map/ppermute | solution.py:374
  124.1 1.2 collective-permute-start.9
  125.3 5.2 %collective-permute-start.10 = (f32[16,128]{1,0:T(8,128)S(1)}, f32[16,128]{1,0:T(8,128)S(1)}, u32[]{:S(2)}, u32[]{:S(2)}) collective-permute-start(f32[16,128]{1,0:T(8,128)S(1)} %fusion.1), channel_id=1, source_target_pairs={{0,2},{1,3},{2,0},{3,1},{4,6},{5,7},{6,4},{7,5},{8,10},{9,11},{10,... | collective-permute-start | bytes 24584 | tf_op jit(solution)/shard_map/ppermute | solution.py:374
  130.5 9.2 %collective-permute-start.13 = (f32[16,128]{1,0:T(8,128)S(1)}, f32[16,128]{1,0:T(8,128)S(1)}, u32[]{:S(2)}, u32[]{:S(2)}) collective-permute-start(f32[16,128]{1,0:T(8,128)S(1)} %add.68), channel_id=1, source_target_pairs={{0,24},{1,25},{2,26},{3,27},{4,28},{5,29},{6,30},{7,31},{8,16},{9,... | collective-permute-start | bytes 24584 | tf_op jit(solution)/shard_map/ppermute | solution.py:374
  137.2 7.6 %collective-permute-start.12 = (f32[16,128]{1,0:T(8,128)S(1)}, f32[16,128]{1,0:T(8,128)S(1)}, u32[]{:S(2)}, u32[]{:S(2)}) collective-permute-start(f32[16,128]{1,0:T(8,128)S(1)} %add.68), channel_id=1, source_target_pairs={{0,16},{1,17},{2,18},{3,19},{4,20},{5,21},{6,22},{7,23},{8,24},{9,... | collective-permute-start | bytes 24584 | tf_op jit(solution)/shard_map/ppermute | solution.py:374
  138.4 6.4 %collective-permute-start.11 = (f32[16,128]{1,0:T(8,128)S(1)}, f32[16,128]{1,0:T(8,128)S(1)}, u32[]{:S(2)}, u32[]{:S(2)}) collective-permute-start(f32[16,128]{1,0:T(8,128)S(1)} %add.68), channel_id=1, source_target_pairs={{0,8},{1,9},{2,10},{3,11},{4,12},{5,13},{6,14},{7,15},{8,0},{9,1},... | collective-permute-start | bytes 24584 | tf_op jit(solution)/shard_map/ppermute | solution.py:374
  144.8 3.7 %collective-permute-start.14 = (f32[16,128]{1,0:T(8,128)S(1)}, f32[16,128]{1,0:T(8,128)S(1)}, u32[]{:S(2)}, u32[]{:S(2)}) collective-permute-start(f32[16,128]{1,0:T(8,128)S(1)} %add_add_fusion.mine_ref), channel_id=1, source_target_pairs={{0,4},{1,5},{2,6},{3,7},{4,0},{5,1},{6,2},{7,3},{8,12},{9,13},{10,... | collective-permute-start | bytes 24584 | tf_op jit(solution)/shard_map/ppermute | solution.py:374
